TPU v7x, 256 devices: a whole 4x4x8 slice. The times are simulated.
256 devices in a mesh: day: 32 (over y, x, core), cls: 8 (over z).
Axes of the slice: x: 4, y: 4, z: 8, core: 2. Of those that a mesh axis runs over, the one named last changes fastest.
Arguments:
- cost: float32 [256, 8, 65536], P('day', None, 'cls'), may hold values from -6 to 6
- x_start: float32 [256, 8, 65536], P('day', None, 'cls'), may hold values from 0 to 1
- ybal_start: float32 [256, 65536], P('day', 'cls'), may hold values from -3 to 3
- inflow: float32 [256, 65536], P('day', 'cls'), may hold values from 0.5 to 3
- ycap_start: float32 [256, 256], P('day', 'cls'), may hold values from -1 to 0
- capacity: float32 [256, 256], P('day', 'cls'), may hold values from 2 to 60
- upper: float32 [8, 65536], P(None, 'cls'), may hold values from 0.3 to 3
- facility: int32 [65536], P('cls'), may hold values from 0 to 255
- option_count: int32 [65536], P('cls'), may hold values from 1 to 8
- decay_index: int32 [65536], P('cls'), may hold values from 0 to 15
- decay_table: float32 [16], replicated, may hold values from 0.3 to 0.99
- usage: float32 [8], replicated, may hold values from 0.02 to 0.2
Outputs:
- x_final: float32 [256, 8, 65536], P('day', None, 'cls')
- ybal_final: float32 [256, 65536], P('day', 'cls')
- ycap_final: float32 [256, 256], P('day', 'cls')
All inputs are finite; a program needn't handle non-finite values.
Results may differ from a plain program's by a relative error of at most 0.0003.
Values sent between devices are 32-bit elements; how exact they have to be, the bound alone decides.
No kernel may reach another device: no remote copies, remote signals or barrier semaphores. Data moves between devices by JAX's collectives and lax.ppermute only.
A program may use at most 64 MiB of HBM per device.

v0:
```python
import jax
import jax.numpy as jnp
from jax import lax
from jax.sharding import PartitionSpec as P

ITERS = 2


ETA = 0.3
HIGH = lax.Precision.HIGHEST


def passed_along(block, axis, distance):
    devices = range(lax.axis_size(axis))
    route = [(i - distance, i) for i in devices if i - distance in devices]
    return lax.ppermute(block, axis, route)


def movement_sums(primal_part_sum, dual_part_sum):
    return lax.psum((primal_part_sum, dual_part_sum), ("day", "cls"))


def local(
    cost,
    x_start,
    ybal_start,
    inflow,
    ycap_start,
    capacity,
    upper,
    facility,
    option_count,
    decay_index,
    decay_table,
    usage,
):
    fac_dev = ycap_start.shape[1]
    fac_all = fac_dev * lax.axis_size("cls")
    opts = cost.shape[1]
    member = (facility[:, None] == jnp.arange(fac_all, dtype=jnp.int32)[None, :]).astype(
        jnp.float32
    )
    levels = decay_table.shape[0]
    picked = (decay_index[:, None] == jnp.arange(levels, dtype=jnp.int32)[None, :]).astype(
        jnp.float32
    )
    gamma = jnp.sum(picked * decay_table[None, :], axis=1)
    live = jnp.arange(opts, dtype=jnp.int32)[:, None] < option_count[None, :]
    bound = jnp.where(live, upper, jnp.float32(0.0))
    weights = usage[None, :, None]
    field, duals = (x_start, ybal_start)
    omega = jnp.float32(1.0)
    caps = ycap_start
    for step in range(ITERS):
        tau = ETA / omega
        sigma = ETA * omega
        pulled = jnp.dot(
            lax.all_gather(caps, "cls", axis=1, tiled=True),
            member.T,
            precision=HIGH,
            preferred_element_type=jnp.float32,
        )
        after = passed_along(duals[0:1], "day", -1)
        grad = (
            cost
            - (duals - gamma[None, :] * jnp.concatenate([duals[1:], after], axis=0))[:, None, :]
            - weights * pulled[:, None, :]
        )
        field_new = jnp.minimum(jnp.maximum(field - tau * grad, 0.0), bound[None])
        field_new, extra = (field_new, 2.0 * field_new - field)
        sums = jnp.sum(extra, axis=1)
        prior = passed_along(sums[-1:], "day", 1)
        duals_new = duals - sigma * (
            sums - gamma[None, :] * jnp.concatenate([prior, sums[:-1]], axis=0) - inflow
        )
        weighted = jnp.sum(weights * extra, axis=1)
        owned = lax.psum_scatter(
            jnp.dot(weighted, member, precision=HIGH, preferred_element_type=jnp.float32),
            "cls",
            scatter_dimension=1,
            tiled=True,
        )
        caps_new = jnp.minimum(caps - sigma * (owned - capacity), 0.0)
        if step == 0:
            moved, dual_moved = movement_sums(
                jnp.sum((field_new - field) ** 2),
                jnp.sum((duals_new - duals) ** 2) + jnp.sum((caps_new - caps) ** 2),
            )
            omega = jnp.sqrt(omega * jnp.sqrt((dual_moved + 1e-06) / (moved + 1e-06)))
        field, duals, caps = (field_new, duals_new, caps_new)
    return (field, duals, caps)


def solution(mesh):
    in_specs = (
        P("day", None, "cls"),
        P("day", None, "cls"),
        P("day", "cls"),
        P("day", "cls"),
        P("day", "cls"),
        P("day", "cls"),
        P(None, "cls"),
        P("cls"),
        P("cls"),
        P("cls"),
        P(),
        P(),
    )
    out_specs = (P("day", None, "cls"), P("day", "cls"), P("day", "cls"))
    return jax.shard_map(local, mesh=mesh, in_specs=in_specs, out_specs=out_specs, check_vma=False)
```

profile of v0, /device:TPU:2, one launch (start us, length us, event | category | flops | bytes accessed | tf_op | source)
XLA Modules:
  0.0 261.4 jit_solution(13296102688556336643)
XLA Ops:
  7.2 0.0 copy-start.1
  7.2 0.0 copy-start.6
  7.2 0.0 copy-start.4
  7.2 0.0 copy-start.10
  7.2 0.0 copy-start.7
  7.2 0.0 reduce-scatter.7.cloned.1.call-start
  7.3 1.0 slice.25
  8.3 1.9 collective-permute-start
  10.2 28.2 %all-gather = f32[8,32,8]{1,2,0:T(8,128)S(1)} all-gather(f32[1,32,8]{1,2,0:T(8,128)} %bitcast.27), channel_id=1, replica_groups=mesh['day'=32,'cls'=8] {'cls'}, dimensions={0}, use_global_device_ids=true | all-gather | bytes 9216 | tf_op jit(solution)/shard_map/all_gather | solution.py:58
  38.5 0.1 reshape.18
  38.5 0.0 copy-start
  38.5 0.0 copy-start.2
  38.5 0.0 copy-start.9
  38.6 6.0 %convolution_bitcast_fusion = f32[8,8192]{1,0:T(8,128)S(1)} fusion(f32[256,8]{0,1:T(8,128)S(1)} %reshape.18, s32[8192]{0:T(1024)} %param.19), kind=kOutput, calls=%fused_computation | convolution fusion | flops 203423744 | bytes 303104 | tf_op jit(solution)/shard_map/dot_general | solution.py:57
  44.6 0.0 copy-done.6
  44.6 0.0 copy-done.4
  44.6 0.0 copy-done.10
  44.6 0.0 copy-done.7
  44.6 0.2 select_reduce_fusion
  44.8 0.0 copy-done.1
  44.9 0.0 collective-permute-done
  44.9 0.1 fusion.11
  45.0 0.0 copy-done
  45.0 0.0 copy-done.2
  45.0 0.0 copy-done.9
  45.0 0.0 copy-start.11
  45.0 3.0 %multiply_reduce_fusion.1 = (f32[]{:T(128)}, f32[8,8192]{1,0:T(8,128)S(1)}, f32[8,8192]{1,0:T(8,128)S(1)}, f32[8,8,8192]{2,1,0:T(8,128)}) fusion(f32[8,8,8192]{2,1,0:T(8,128)S(1)} %copy-done.2, f32[8]{0:T(128)S(1)} %copy-done.9, f32[8,8192]{1,0:T(8,128)S(1)} %fusion.21, f32[8,8192]{1,0:T(8,128)S(1)} %convolution_bitcast_fusion, ...), kind=kLoop, calls=%fused_computation.12 | loop fusion | flops 7733247 | bytes 7602212 | tf_op jit(solution)/shard_map/reduce_sum | solution.py:86
  48.0 0.0 copy-done.11
  48.0 0.0 copy-start.5
  48.0 0.0 copy-start.8
  48.0 0.0 copy-start.3
  48.0 8.4 %fusion.7 = f32[256,8]{1,0:T(8,128)} fusion(f32[8,8192]{1,0:T(8,128)S(1)} %get-tuple-element.6, s32[8192]{0:T(1024)S(1)} %copy-done.11), kind=kOutput, calls=%fused_computation.16 | convolution fusion | flops 203423744 | bytes 303104
  56.4 0.0 reduce-scatter.7.cloned.1.call-update
  56.4 0.0 reduce-scatter.9.cloned.1.call-start
  56.5 1.9 collective-permute-start.1
  58.4 34.0 %reduce-scatter.7.cloned.1.call-done = f32[32,8]{1,0:T(8,128)} async-done(((f32[256,8]{1,0:T(8,128)}), f32[32,8]{1,0:T(8,128)}) %reduce-scatter.7.cloned.1.call-update) | async-done | bytes 1040
  92.4 0.8 copy.22
  93.2 0.0 copy-done.5
  93.2 0.0 copy-done.8
  93.2 0.6 multiply_reduce_fusion.4
  93.8 24.5 %all-gather.1 = f32[8,32,8]{1,2,0:T(8,128)S(1)} all-gather(f32[1,32,8]{1,2,0:T(8,128)S(1)} %get-tuple-element.15), channel_id=1, replica_groups=mesh['day'=32,'cls'=8] {'cls'}, dimensions={0}, use_global_device_ids=true | all-gather | bytes 9216 | tf_op jit(solution)/shard_map/all_gather | solution.py:58
  118.3 0.1 reshape.20
  118.4 0.0 collective-permute-done.1
  118.4 0.0 copy-done.3
  118.4 0.8 multiply_reduce_fusion.3
  119.2 1.9 collective-permute-start.2
  121.1 5.9 %fusion.1 = f32[8,8192]{1,0:T(8,128)S(1)} fusion(f32[256,8]{0,1:T(8,128)S(1)} %reshape.20, s32[8192]{0:T(1024)} %param.19), kind=kOutput, calls=%fused_computation.3 | convolution fusion | flops 203423744 | bytes 303104 | tf_op jit(solution)/shard_map/dot_general | solution.py:57
  128.4 75.5 %all-reduce = (f32[]{:T(128)}, f32[]{:T(128)}) all-reduce(f32[]{:T(128)S(6)} %add.17, f32[]{:T(128)} %get-tuple-element.5), channel_id=1, replica_groups=mesh['day'=32,'cls'=8] {'day','cls'}, use_global_device_ids=true, to_apply=%region_6.7 | all-reduce | flops 2 | bytes 16 | tf_op jit(solution)/shard_map/psum | solution.py:20
  205.3 0.0 collective-permute-done.2
  205.3 0.1 fusion.16
  205.4 0.0 copy-start.12
  205.4 4.3 %multiply_reduce_fusion = (f32[8,8192]{1,0:T(8,128)S(1)}, f32[8,8192]{1,0:T(8,128)S(1)}, f32[8,8,8192]{2,1,0:T(8,128)}) fusion(f32[8]{0:T(128)S(1)} %copy-done.9, f32[8,8,8192]{2,1,0:T(8,128)} %get-tuple-element.13, f32[8,8192]{1,0:T(8,128)S(1)} %fusion.21, f32[8,8192]{1,0:T(8,128)S(1)} %fusion.1, f32[8,8,8192]{2,1,0:T(8,128)S(1)} %copy-done, ...), kind=kLoop, calls=%fused_computation.9 | loop fusion | flops 6160384 | bytes 7602212 | tf_op jit(solution)/shard_map/reduce_sum | solution.py:76
  209.8 0.0 copy-done.12
  209.8 8.4 %fusion.8 = f32[256,8]{1,0:T(8,128)} fusion(f32[8,8192]{1,0:T(8,128)S(1)} %get-tuple-element.3, s32[8192]{0:T(1024)S(1)} %copy-done.12), kind=kOutput, calls=%fused_computation.17 | convolution fusion | flops 203423744 | bytes 303104
  218.2 0.0 reduce-scatter.9.cloned.1.call-update
  218.2 1.9 collective-permute-start.3
  220.2 32.2 %reduce-scatter.9.cloned.1.call-done = f32[32,8]{1,0:T(8,128)} async-done(((f32[256,8]{1,0:T(8,128)}), f32[32,8]{1,0:T(8,128)}) %reduce-scatter.9.cloned.1.call-update) | async-done | bytes 1040
  252.4 0.8 copy.24
  253.1 0.6 subtract_minimum_fusion
  253.7 0.0 collective-permute-done.3
  253.8 0.8 fusion.20
  (8 shorter events, 0.2 us)
Async XLA Ops:
  7.2 37.7 %copy-start.1 = (f32[8,8192]{1,0:T(8,128)S(1)}, f32[8,8192]{1,0:T(8,128)}, u32[]{:S(2)}) copy-start(f32[8,8192]{1,0:T(8,128)} %param.14) | copy-start | bytes 786436
  7.2 37.4 %copy-start.6 = (s32[8192]{0:T(1024)S(1)}, s32[8192]{0:T(1024)}, u32[]{:S(2)}) copy-start(s32[8192]{0:T(1024)} %param.20) | copy-start | bytes 98308
  7.2 37.4 %copy-start.4 = (f32[8,8192]{1,0:T(8,128)S(1)}, f32[8,8192]{1,0:T(8,128)}, u32[]{:S(2)}) copy-start(f32[8,8192]{1,0:T(8,128)} %param.18) | copy-start | bytes 786436
  7.2 37.4 %copy-start.10 = (f32[16]{0:T(128)S(1)}, f32[16]{0:T(128)}, u32[]{:S(2)}) copy-start(f32[16]{0:T(128)} %param.22) | copy-start | bytes 196
  7.2 37.4 %copy-start.7 = (s32[8192]{0:T(1024)S(1)}, s32[8192]{0:T(1024)}, u32[]{:S(2)}) copy-start(s32[8192]{0:T(1024)} %param.21) | copy-start | bytes 98308
  7.2 85.2 %reduce-scatter.7.cloned.1.call-start = ((), (), s32[]{:S(2)}) async-start(), calls=%async_computation.2 | async-start | bytes 147456
  8.3 36.6 %collective-permute-start = (f32[1,8192]{1,0:T(1,128)S(1)}, f32[1,8192]{1,0:T(1,128)S(1)}, u32[]{:S(2)}, u32[]{:S(2)}) collective-permute-start(f32[1,8192]{1,0:T(1,128)S(1)} %slice.25), channel_id=1, source_target_pairs={{8,0},{16,8},{24,16},{32,24},{40,32},{48,40},{56,48},{64,56},{72,6... | collective-permute-start | bytes 98312 | tf_op jit(solution)/shard_map/ppermute | solution.py:16
  38.5 6.4 %copy-start = (f32[8,8,8192]{2,1,0:T(8,128)S(1)}, f32[8,8,8192]{2,1,0:T(8,128)}, u32[]{:S(2)}) copy-start(f32[8,8,8192]{2,1,0:T(8,128)} %param.12) | copy-start | bytes 6291460
  38.5 6.4 %copy-start.2 = (f32[8,8,8192]{2,1,0:T(8,128)S(1)}, f32[8,8,8192]{2,1,0:T(8,128)}, u32[]{:S(2)}) copy-start(f32[8,8,8192]{2,1,0:T(8,128)} %param.13) | copy-start | bytes 6291460
  38.5 6.4 %copy-start.9 = (f32[8]{0:T(128)S(1)}, f32[8]{0:T(128)}, u32[]{:S(2)}) copy-start(f32[8]{0:T(128)} %param.23) | copy-start | bytes 100
  45.0 3.0 %copy-start.11 = (s32[8192]{0:T(1024)S(1)}, s32[8192]{0:T(1024)}, u32[]{:S(2)}) copy-start(s32[8192]{0:T(1024)} %param.19) | copy-start | bytes 98308
  48.0 45.2 %copy-start.5 = (f32[8,32]{1,0:T(8,128)S(1)}, f32[8,32]{1,0:T(8,128)}, u32[]{:S(2)}) copy-start(f32[8,32]{1,0:T(8,128)} %param.16) | copy-start | bytes 3076
  48.0 45.2 %copy-start.8 = (f32[8,32]{1,0:T(8,128)S(1)}, f32[8,32]{1,0:T(8,128)}, u32[]{:S(2)}) copy-start(f32[8,32]{1,0:T(8,128)} %param.17) | copy-start | bytes 3076
  48.0 70.4 %copy-start.3 = (f32[8,8192]{1,0:T(8,128)S(1)}, f32[8,8192]{1,0:T(8,128)}, u32[]{:S(2)}) copy-start(f32[8,8192]{1,0:T(8,128)} %param.15) | copy-start | bytes 786436
  56.4 195.9 %reduce-scatter.9.cloned.1.call-start = ((), (), s32[]{:S(2)}) async-start(), calls=%async_computation.3 | async-start | bytes 147456
  56.5 61.9 %collective-permute-start.1 = (f32[1,8192]{1,0:T(1,128)S(1)}, f32[1,8192]{1,0:T(1,128)S(1)}, u32[]{:S(2)}, u32[]{:S(2)}) collective-permute-start(f32[1,8192]{1,0:T(1,128)S(1)} %slice.32), channel_id=1, source_target_pairs={{0,8},{8,16},{16,24},{24,32},{32,40},{40,48},{48,56},{56,64},{64,7... | collective-permute-start | bytes 98312 | tf_op jit(solution)/shard_map/ppermute | solution.py:16
  119.2 86.1 %collective-permute-start.2 = (f32[1,8192]{1,0:T(1,128)S(1)}, f32[1,8192]{1,0:T(1,128)S(1)}, u32[]{:S(2)}, u32[]{:S(2)}) collective-permute-start(f32[1,8192]{1,0:T(1,128)S(1)} %slice.35), channel_id=1, source_target_pairs={{8,0},{16,8},{24,16},{32,24},{40,32},{48,40},{56,48},{64,56},{72,6... | collective-permute-start | bytes 98312 | tf_op jit(solution)/shard_map/ppermute | solution.py:16
  205.4 4.3 %copy-start.12 = (s32[8192]{0:T(1024)S(1)}, s32[8192]{0:T(1024)}, u32[]{:S(2)}) copy-start(s32[8192]{0:T(1024)} %param.19) | copy-start | bytes 98308
  218.2 35.5 %collective-permute-start.3 = (f32[1,8192]{1,0:T(1,128)S(1)}, f32[1,8192]{1,0:T(1,128)S(1)}, u32[]{:S(2)}, u32[]{:S(2)}) collective-permute-start(f32[1,8192]{1,0:T(1,128)S(1)} %slice.36), channel_id=1, source_target_pairs={{0,8},{8,16},{16,24},{24,32},{32,40},{40,48},{48,56},{56,64},{64,7... | collective-permute-start | bytes 98312 | tf_op jit(solution)/shard_map/ppermute | solution.py:16
Sparse Core Ops, SparseCore 0:
  56.5 35.8 reduce-scatter.6
  218.3 34.0 reduce-scatter.8
where the time goes:
time: 262 us; the launch traced here: 261 us
  blocking collectives  128 us (49%)
  waiting for transfers between devices  66.2 us (25%)
  matrix products  28.7 us (11%)
  between operations  17.1 us (7%)
  other arithmetic  10.5 us (4%)
  starting transfers between devices  7.76 us (3%)
  local copies, waits for them, and re-layouts  2.96 us (1%)
    psum x1, blocking collectives, movement_sums(): return lax.psum((primal_part_sum, dual_part_sum), ('day', 'cls'))  75.5 us
    unnamed x4, waiting for transfers between devices  66.2 us
    all_gather x2, blocking collectives, local(): lax.all_gather(caps, 'cls', axis=1, tiled=True)  52.7 us
    unnamed x2, matrix products  16.8 us
    dot_general x2, matrix products, local(): jnp.dot(lax.all_gather(caps, 'cls', axis=1, tiled=True), member.T, precis...  11.9 us
    ppermute x4, starting transfers between devices, passed_along(): return lax.ppermute(block, axis, route)  7.68 us
  transfers between devices with their start and end apart: 6, of which 2 were waited for; matrix products, arithmetic and copies ran while one was open for 6% of the time, Pallas kernels for 0%

commit v1 on v0

v1 whole, which is shorter than its diff:
```python
import jax
import jax.numpy as jnp
from jax import lax
from jax.experimental import pallas as pl
from jax.experimental.pallas import tpu as pltpu
from jax.sharding import PartitionSpec as P

ETA = 0.3
EPS = 1e-6
LANES = 128
STEP = 256
PART = 1024
WIDE = 64

VM = pl.BlockSpec(memory_space=pltpu.VMEM)
SM = pl.BlockSpec(memory_space=pltpu.SMEM)
F32 = jnp.float32


def struct(*shape):
    return jax.ShapeDtypeStruct(shape, F32)


def call(body, name, outs, ins, scratch=(), cost=None):
    return pl.pallas_call(
        body,
        name=name,
        out_shape=outs,
        in_specs=ins,
        out_specs=[VM] * len(outs),
        scratch_shapes=list(scratch),
        compiler_params=pltpu.CompilerParams(vmem_limit_bytes=40 << 20),
        cost_estimate=cost,
    )


def rows_iota(shape):
    return lax.broadcasted_iota(jnp.int32, shape, 0)


def lanes_iota(shape):
    return lax.broadcasted_iota(jnp.int32, shape, 1)


def tile_of(ref, count, index):
    out = jnp.zeros(index.shape, F32)
    for k in range(count):
        out = jnp.where(index == k, ref[k], out)
    return out


def lookup(table, index):
    return jnp.take_along_axis(table, index, axis=1, mode="promise_in_bounds")


def folded(wide):
    out = wide[:, :LANES]
    for k in range(1, wide.shape[1] // LANES):
        out = out + wide[:, k * LANES : (k + 1) * LANES]
    return out


def pulled_of(caps, facility):
    days = caps.shape[0]
    parts = []
    for k in range(facility.shape[1] // LANES):
        own = jnp.broadcast_to(facility[:, k * LANES : (k + 1) * LANES], (days, LANES))
        low = jnp.bitwise_and(own, LANES - 1)
        got = lookup(caps[:, :LANES], low)
        for g in range(1, caps.shape[1] // LANES):
            got = jnp.where(own >= g * LANES, lookup(caps[:, g * LANES : (g + 1) * LANES], low), got)
        parts.append(got)
    return jnp.concatenate(parts, axis=1)


def gamma_of(table, index):
    parts = []
    for k in range(index.shape[1] // LANES):
        own = jnp.broadcast_to(index[:, k * LANES : (k + 1) * LANES], (8, LANES))
        parts.append(lookup(table, own))
    return jnp.concatenate(parts, axis=1)


def facility_sums(weighted_ref, facility_ref, facilities):
    days, classes = weighted_ref.shape
    groups = facilities // WIDE
    total = jnp.zeros((groups * 3 * days, WIDE), F32)
    for k in range(classes // PART):
        at = pl.ds(k * PART, PART)
        w = weighted_ref[:, at]
        fac = facility_ref[:, at]
        top = w.astype(jnp.bfloat16).astype(F32)
        rest = w - top
        mid = rest.astype(jnp.bfloat16).astype(F32)
        low = rest - mid
        group = jnp.broadcast_to(fac // WIDE, (days, PART))
        rows = []
        for g in range(groups):
            mine = group == g
            rows += [jnp.where(mine, top, 0.0), jnp.where(mine, mid, 0.0), jnp.where(mine, low, 0.0)]
        left = jnp.concatenate(rows, axis=0).astype(jnp.bfloat16)
        within = jnp.broadcast_to(jnp.bitwise_and(fac, WIDE - 1), (WIDE, PART))
        member = jnp.where(within == rows_iota((WIDE, PART)), 1.0, 0.0).astype(jnp.bfloat16)
        total = total + lax.dot_general(
            left, member, (((1,), (1,)), ((), ())), preferred_element_type=F32
        )
    out = []
    for g in range(groups):
        base = g * 3 * days
        out.append(
            total[base : base + days]
            + total[base + days : base + 2 * days]
            + total[base + 2 * days : base + 3 * days]
        )
    return out


def primal_rows(at, kt, pulled, tau, weights, bound, cost_ref, x_ref, x1_ref, sum_ref, weighted_ref, moved):
    for t in range(cost_ref.shape[0]):
        grad = cost_ref[t, :, at] - kt[t : t + 1] - weights * pulled[t : t + 1]
        old = x_ref[t, :, at]
        new = jnp.minimum(jnp.maximum(old - tau * grad, 0.0), bound)
        x1_ref[t, :, at] = new
        gone = new - old
        extra = new + gone
        sum_ref[t : t + 1, at] = jnp.sum(extra, axis=0, keepdims=True)
        weighted_ref[t : t + 1, at] = jnp.sum(weights * extra, axis=0, keepdims=True)
        if moved is not None:
            moved = moved + gone * gone
    return moved


def first_primal(
    usage_ref, table_ref, ends_ref, after_ref, cost_ref, x_ref, w_ref, inflow_ref, upper_ref,
    fac_ref, count_ref, index_ref,
    x1_ref, sum_ref, weighted_ref, last_ref, lead_ref, gamma_ref, moved_ref, caps_ref, room_ref,
):
    days, classes = w_ref.shape
    own = ends_ref.shape[2]
    for k in range(ends_ref.shape[0]):
        caps_ref[:, k * own : (k + 1) * own] = ends_ref[k, :days, :]
        room_ref[:, k * own : (k + 1) * own] = ends_ref[k, days:, :]
    caps = caps_ref[...]
    weights = tile_of(usage_ref, 8, rows_iota((8, STEP)))
    table = tile_of(table_ref, 16, lanes_iota((8, LANES)))
    rows = rows_iota((days, STEP))

    def step(j, moved):
        at = pl.ds(pl.multiple_of(j * STEP, STEP), STEP)
        gamma = gamma_of(table, index_ref[:, at])
        gamma_ref[:, at] = gamma[:1]
        bound = jnp.where(rows < count_ref[:, at], upper_ref[:, at], 0.0)
        w = w_ref[:, at]
        after = jnp.where(rows == days - 1, after_ref[:, at], pltpu.roll(w, days - 1, 0))
        moved = primal_rows(
            at, w - gamma * after, pulled_of(caps, fac_ref[:, at]), F32(ETA), weights, bound,
            cost_ref, x_ref, x1_ref, sum_ref, weighted_ref, moved,
        )
        last_ref[:, at] = sum_ref[days - 1 :, at]
        lead_ref[:, at] = w[:1] - ETA * (sum_ref[:1, at] - inflow_ref[:1, at])
        return moved

    moved = lax.fori_loop(0, classes // STEP, step, jnp.zeros((8, STEP), F32))
    moved_ref[...] = folded(moved)
    lead_ref[:, classes:] = jnp.ones((1, LANES), F32)


def first_use(weighted_ref, sum_ref, inflow_ref, gamma_ref, fac_ref, use_ref, moved_ref):
    days, classes = sum_ref.shape
    parts = facility_sums(weighted_ref, fac_ref, use_ref.shape[1])
    for g, part in enumerate(parts):
        use_ref[:, g * WIDE : (g + 1) * WIDE] = part
    total = jnp.zeros((days, PART), F32)
    for k in range(classes // PART):
        at = pl.ds(k * PART, PART)
        sums = sum_ref[:, at]
        gap = sums - gamma_ref[:, at] * pltpu.roll(sums, 1, 0) - inflow_ref[:, at]
        total = total + gap * gap
    moved_ref[...] = jnp.where(
        rows_iota((days, LANES)) > 0, (ETA * ETA) * folded(total), 0.0
    )


def first_send(use_ref, moved_ref, dual_ref, prior_ref, sum_ref, inflow_ref, gamma_ref, out_ref):
    days, classes = sum_ref.shape
    total = jnp.zeros((1, PART), F32)
    for k in range(classes // PART):
        at = pl.ds(k * PART, PART)
        gap = sum_ref[:1, at] - gamma_ref[:, at] * prior_ref[:, at] - inflow_ref[:1, at]
        total = total + gap * gap
    edge = (ETA * ETA) * folded(total)
    dual = dual_ref[...] + jnp.where(rows_iota((days, LANES)) == 0, edge, 0.0)
    use = use_ref[...]
    moved = moved_ref[...]
    for k in range(out_ref.shape[0]):
        out_ref[k, :days, :] = use
        out_ref[k, days:, :LANES] = moved
        out_ref[k, days:, LANES:] = dual


def caps_step(in_ref, caps_ref, room_ref, caps1_ref, out_ref):
    days = caps_ref.shape[0]
    total = in_ref[0]
    for k in range(1, in_ref.shape[0]):
        total = total + in_ref[k]
    caps = caps_ref[...]
    new = jnp.minimum(caps - ETA * (total[:days] - room_ref[...]), 0.0)
    caps1_ref[...] = new
    gone = new - caps
    primal = jnp.sum(total[days:, :LANES], axis=0, keepdims=True)
    dual = jnp.sum(total[days:, LANES:] + folded(gone * gone), axis=0, keepdims=True)
    rows = rows_iota((days, LANES))
    both = jnp.where(rows == 0, primal, jnp.where(rows == 1, dual, 0.0))
    for k in range(out_ref.shape[0]):
        out_ref[k] = both


def second_primal(
    usage_ref, moved_ref, caps_ref, cost_ref, x_ref, w_ref, inflow_ref, upper_ref, fac_ref, count_ref,
    gamma_ref, sums_ref, prior_ref, lead_ref,
    x2_ref, w1_ref, sum_ref, weighted_ref, last_ref, omega_ref,
):
    days, classes = w_ref.shape
    total = moved_ref[0]
    for k in range(1, moved_ref.shape[0]):
        total = total + moved_ref[k]
    primal = jnp.sum(total[0:1], axis=1, keepdims=True)
    dual = jnp.sum(total[1:2], axis=1, keepdims=True)
    omega = jnp.sqrt(jnp.sqrt((dual + EPS) / (primal + EPS)))
    omega_ref[...] = jnp.broadcast_to(omega, omega_ref.shape)
    tau = jnp.broadcast_to(ETA / omega, (8, STEP))
    caps = caps_ref[...]
    weights = tile_of(usage_ref, 8, rows_iota((8, STEP)))
    rows = rows_iota((days, STEP))
    more = ETA * jnp.max(lead_ref[:, classes:], axis=1, keepdims=True)

    def step(j, _):
        at = pl.ds(pl.multiple_of(j * STEP, STEP), STEP)
        gamma = gamma_ref[:, at]
        bound = jnp.where(rows < count_ref[:, at], upper_ref[:, at], 0.0)
        sums = sums_ref[:, at]
        prior = jnp.where(rows == 0, prior_ref[:, at], pltpu.roll(sums, 1, 0))
        w = w_ref[:, at] - ETA * (sums - gamma * prior - inflow_ref[:, at])
        w1_ref[:, at] = w
        edge = lead_ref[:, at] + more * gamma * sums[days - 1 :]
        after = jnp.where(rows == days - 1, edge, pltpu.roll(w, days - 1, 0))
        primal_rows(
            at, w - gamma * after, pulled_of(caps, fac_ref[:, at]), tau, weights, bound,
            cost_ref, x_ref, x2_ref, sum_ref, weighted_ref, None,
        )
        last_ref[:, at] = sum_ref[days - 1 :, at]
        return 0

    lax.fori_loop(0, classes // STEP, step, 0)


def second_use(weighted_ref, fac_ref, caps_ref, out_ref):
    days = weighted_ref.shape[0]
    parts = facility_sums(weighted_ref, fac_ref, caps_ref.shape[1])
    own = out_ref.shape[2]
    for k in range(out_ref.shape[0]):
        g, place = divmod(k * own, WIDE)
        out_ref[k, :days, :] = parts[g][:, place : place + own]
        out_ref[k, days:, :] = caps_ref[:, k * own : (k + 1) * own]


def last_duals(in_ref, room_ref, omega_ref, w_ref, sum_ref, prior_ref, inflow_ref, gamma_ref, w2_ref, caps2_ref):
    days, classes = w_ref.shape
    sigma = ETA * omega_ref[...]
    use = in_ref[0, :days]
    for k in range(1, in_ref.shape[0]):
        use = use + in_ref[k, :days]
    caps2_ref[...] = jnp.minimum(in_ref[0, days:] - sigma[:1, :1] * (use - room_ref[...]), 0.0)
    rows = rows_iota((days, LANES))
    for k in range(classes // LANES):
        at = pl.ds(k * LANES, LANES)
        sums = sum_ref[:, at]
        prior = jnp.where(rows == 0, prior_ref[:, at], pltpu.roll(sums, 1, 0))
        w2_ref[:, at] = w_ref[:, at] - sigma * (sums - gamma_ref[:, at] * prior - inflow_ref[:, at])


def to_next(row):
    n = lax.axis_size("day")
    return lax.ppermute(row, "day", [(i, i + 1) for i in range(n - 1)])


def to_previous(row):
    n = lax.axis_size("day")
    return lax.ppermute(row, "day", [(i + 1, i) for i in range(n - 1)])


def local(
    cost, x_start, ybal_start, inflow, ycap_start, capacity, upper, facility, option_count,
    decay_index, decay_table, usage,
):
    days, opts, classes = cost.shape
    own = ycap_start.shape[1]
    blocks = lax.axis_size("cls")
    facilities = own * blocks
    fac = facility.reshape(1, classes)
    count = option_count.reshape(1, classes)
    index = decay_index.reshape(1, classes)

    ends = jnp.broadcast_to(
        jnp.concatenate([ycap_start, capacity], axis=0)[None], (blocks, 2 * days, own)
    )
    after = to_previous(ybal_start[:1])
    ends = lax.all_to_all(ends, "cls", 0, 0)
    x1, sums, weighted, last, lead, gamma, moved, caps, room = call(
        first_primal, "first_primal",
        [struct(days, opts, classes), struct(days, classes), struct(days, classes), struct(1, classes),
         struct(1, classes + LANES), struct(1, classes), struct(8, LANES), struct(days, facilities),
         struct(days, facilities)],
        [SM, SM] + [VM] * 10,
    )(usage, decay_table, ends, after, cost, x_start, ybal_start, inflow, upper, fac, count, index)
    prior = to_next(last)
    lead = to_previous(lead)
    use, dual = call(
        first_use, "first_use", [struct(days, facilities), struct(days, LANES)], [VM] * 5,
        cost=pl.CostEstimate(flops=10_000_000, bytes_accessed=8_000_000, transcendentals=0),
    )(weighted, sums, inflow, gamma, fac)
    (sent,) = call(first_send, "first_send", [struct(blocks, 2 * days, facilities)], [VM] * 7)(
        use, moved, dual, prior, sums, inflow, gamma
    )
    got = lax.all_to_all(sent, "cls", 0, 0)
    caps1, sent = call(
        caps_step, "caps_step", [struct(days, facilities), struct(lax.axis_size("day"), days, LANES)],
        [VM] * 3,
    )(got, caps, room)
    got = lax.all_to_all(sent, "day", 0, 0)
    x2, w1, sums2, weighted2, last2, omega = call(
        second_primal, "second_primal",
        [struct(days, opts, classes), struct(days, classes), struct(days, classes), struct(days, classes),
         struct(1, classes), struct(8, LANES)],
        [SM] + [VM] * 13,
    )(usage, got, caps1, cost, x1, ybal_start, inflow, upper, fac, count, gamma, sums, prior, lead)
    prior2 = to_next(last2)
    (sent,) = call(
        second_use, "second_use", [struct(blocks, 2 * days, own)], [VM] * 3,
        cost=pl.CostEstimate(flops=10_000_000, bytes_accessed=8_000_000, transcendentals=0),
    )(weighted2, fac, caps1)
    got = lax.all_to_all(sent, "cls", 0, 0)
    w2, caps2 = call(last_duals, "last_duals", [struct(days, classes), struct(days, own)], [VM] * 8)(
        got, capacity, omega, w1, sums2, prior2, inflow, gamma
    )
    return x2, w2, caps2


def solution(mesh):
    in_specs = (
        P("day", None, "cls"), P("day", None, "cls"), P("day", "cls"), P("day", "cls"),
        P("day", "cls"), P("day", "cls"), P(None, "cls"), P("cls"), P("cls"), P("cls"), P(), P(),
    )
    out_specs = (P("day", None, "cls"), P("day", "cls"), P("day", "cls"))
    return jax.shard_map(local, mesh=mesh, in_specs=in_specs, out_specs=out_specs, check_vma=False)
```

time: 262 us -> 99.8 us (0.38)
  the two profiles are of different devices: /device:TPU:2 before, /device:TPU:1 now
where the time goes in v1:
time: 99.8 us; the launch traced here: 98.9 us
  blocking collectives  32.2 us (32%)
  starting transfers between devices  25.7 us (26%)
  local copies, waits for them, and re-layouts  17.7 us (18%)
  Pallas kernels  14.6 us (15%)
  waiting for transfers between devices  5.84 us (6%)
  other arithmetic  2.08 us (2%)
    all_to_all x2, blocking collectives, local(): got = lax.all_to_all(sent, 'cls', 0, 0)  19.3 us
    unnamed x52, local copies, waits for them, and re-layouts  16.2 us
    all_to_all x1, blocking collectives, local(): ends = lax.all_to_all(ends, 'cls', 0, 0)  12.9 us
    all_to_all x1, starting transfers between devices, local(): got = lax.all_to_all(sent, 'day', 0, 0)  11.3 us
    ppermute x2, starting transfers between devices, to_previous(): return lax.ppermute(row, 'day', [(i + 1, i) for i in range(n - 1)])  7.29 us
    ppermute x2, starting transfers between devices, to_next(): return lax.ppermute(row, 'day', [(i, i + 1) for i in range(n - 1)])  7.1 us
    pallas_call x1, Pallas kernels, local(): call(second_primal, 'second_primal', [struct(days, opts, classes), struct...  6.5 us
    pallas_call x1, Pallas kernels, local(): call(first_primal, 'first_primal', [struct(days, opts, classes), struct(d...  5.34 us
  transfers between devices with their start and end apart: 5, of which 3 were waited for; matrix products, arithmetic and copies ran while one was open for 3% of the time, Pallas kernels for 1%

profile of v1, /device:TPU:1, one launch (start us, length us, event | category | flops | bytes accessed | tf_op | source)
XLA Modules:
  0.0 98.9 jit_solution(6201806893663514843)
XLA Ops:
  0.6 1.0 slice.3
  1.6 5.1 %collective-permute-start = (f32[1,8192]{1,0:T(1,128)S(1)}, f32[1,8192]{1,0:T(1,128)S(1)}, u32[]{:S(2)}, u32[]{:S(2)}) collective-permute-start(f32[1,8192]{1,0:T(1,128)S(1)} %slice.3), channel_id=1, source_target_pairs={{8,0},{16,8},{24,16},{32,24},{40,32},{48,40},{56,48},{64,56},{72,6... | collective-permute-start | bytes 98312 | tf_op jit(solution)/shard_map/ppermute | solution.py:289
  6.8 0.7 pad_maximum_fusion
  7.5 0.1 reshape.19
  7.6 12.9 %all_to_all.20 = f32[8,1,512]{2,1,0:T(1,128)S(1)} all-to-all(f32[8,1,512]{2,1,0:T(1,128)S(1)} %reshape.19), channel_id=1, replica_groups=mesh['day'=32,'cls'=8] {'cls'}, dimensions={0} | all-to-all | bytes 32768 | tf_op jit(solution)/shard_map/all_to_all | solution.py:308
  20.5 0.5 broadcast.1
  21.0 0.7 reduce
  21.7 0.1 reshape.20.ends_ref
  21.7 0.0 collective-permute-done.after_ref
  21.7 0.0 copy-start
  21.8 1.6 %copy-done = f32[8,8,8192]{2,1,0:T(8,128)S(1)} copy-done((f32[8,8,8192]{2,1,0:T(8,128)S(1)}, f32[8,8,8192]{2,1,0:T(8,128)}, u32[]{:S(2)}) %copy-start) | copy-done | bytes 2097176
  23.3 0.0 copy-start.2
  23.3 0.9 copy-done.2
  24.3 0.0 copy-start.4
  24.3 1.6 %copy-done.4 = f32[8,8,8192]{2,1,0:T(8,128)S(1)} copy-done((f32[8,8,8192]{2,1,0:T(8,128)S(1)}, f32[8,8,8192]{2,1,0:T(8,128)}, u32[]{:S(2)}) %copy-start.4) | copy-done | bytes 2097176
  25.9 0.0 copy-start.7
  25.9 0.9 copy-done.7
  26.8 0.0 copy-start.9
  26.8 0.9 copy-done.9
  27.8 0.0 copy-start.11
  27.8 0.8 copy-done.11
  28.5 0.0 copy-start.17
  28.5 0.8 copy-done.17
  29.3 0.0 copy-start.19
  29.3 0.8 copy-done.19
  30.1 0.0 copy-start.21
  30.1 0.7 copy-done.21
  30.7 0.7 copy-done.23
  31.4 5.3 %first_primal.1 = (f32[8,8,8192]{2,1,0:T(8,128)S(1)}, f32[8,8192]{1,0:T(8,128)S(1)}, f32[8,8192]{1,0:T(8,128)S(1)}, f32[1,8192]{1,0:T(1,128)S(1)}, f32[1,8320]{1...) custom-call(f32[8]{0:T(128)S(1)} %copy-done.21, ...), custom_call_target="tpu_custom_call" | custom-call | tf_op jit(solution)/shard_map/first_primal/pallas_call | solution.py:309
  36.7 0.0 copy-start.5
  36.7 1.3 %copy-done.5 = f32[8,8,8192]{2,1,0:T(8,128)} copy-done((f32[8,8,8192]{2,1,0:T(8,128)}, f32[8,8,8192]{2,1,0:T(8,128)S(1)}, u32[]{:S(2)}) %copy-start.5) | copy-done | bytes 2097176
  38.1 4.6 %collective-permute-start.1 = (f32[1,8192]{1,0:T(1,128)S(1)}, f32[1,8192]{1,0:T(1,128)S(1)}, u32[]{:S(2)}, u32[]{:S(2)}) collective-permute-start(f32[1,8192]{1,0:T(1,128)S(1)} %get-tuple-element.30), channel_id=1, source_target_pairs={{0,8},{8,16},{16,24},{24,32},{32,40},{40,48},{48,56},{56,64},{64,7... | collective-permute-start | bytes 98312 | tf_op jit(solution)/shard_map/ppermute | solution.py:284
  42.6 0.6 first_use.1
  43.3 0.4 collective-permute-done.1.prior_ref
  43.7 10.3 %all_to_all.21.in_ref = f32[8,16,256]{2,1,0:T(8,128)S(1)} all-to-all(f32[8,16,256]{2,1,0:T(8,128)S(1)} %first_send.1), channel_id=1, replica_groups=mesh['day'=32,'cls'=8] {'cls'}, dimensions={0} | all-to-all | bytes 262144 | tf_op jit(solution)/shard_map/all_to_all | solution.py:325
  54.0 0.7 caps_step.1
  54.7 11.3 %all-to-all-start.2 = ((f32[32,8,128]{2,1,0:T(8,128)}), f32[32,8,128]{2,1,0:T(8,128)S(1)}, u32[]{:S(2)}, u32[]{:S(2)}) async-start(f32[32,8,128]{2,1,0:T(8,128)} %get-tuple-element.33), calls=%async_computation.2 | async-start | bytes 262144 | tf_op jit(solution)/shard_map/all_to_all | solution.py:330
  66.0 2.1 %collective-permute-start.2 = (f32[1,8320]{1,0:T(1,128)S(1)}, f32[1,8320]{1,0:T(1,128)S(1)}, u32[]{:S(2)}, u32[]{:S(2)}) collective-permute-start(f32[1,8320]{1,0:T(1,128)S(1)} %get-tuple-element.36), channel_id=1, source_target_pairs={{8,0},{16,8},{24,16},{32,24},{40,32},{48,40},{56,48},{64,56},{72,6... | collective-permute-start | bytes 99848 | tf_op jit(solution)/shard_map/ppermute | solution.py:289
  68.1 3.4 %collective-permute-done.2.lead_ref = f32[1,8320]{1,0:T(1,128)S(1)} collective-permute-done((f32[1,8320]{1,0:T(1,128)S(1)}, f32[1,8320]{1,0:T(1,128)S(1)}, u32[]{:S(2)}, u32[]{:S(2)}) %collective-permute-start.2) | collective-permute-done | bytes 33312 | tf_op jit(solution)/shard_map/ppermute | solution.py:289
  71.5 2.1 %all-to-all-done.2.moved_ref = f32[32,8,128]{2,1,0:T(8,128)S(1)} async-done(((f32[32,8,128]{2,1,0:T(8,128)}), f32[32,8,128]{2,1,0:T(8,128)S(1)}, u32[]{:S(2)}, u32[]{:S(2)}) %all-to-all-start.2) | async-done | bytes 131104 | tf_op jit(solution)/shard_map/all_to_all | solution.py:330
  73.6 0.0 copy-done.3
  73.6 0.0 copy-done.8
  73.6 0.0 copy-done.10
  73.6 0.0 copy-done.1
  73.6 0.0 copy-done.12
  73.6 0.0 copy-done.18
  73.6 0.0 copy-done.22
  73.7 0.0 copy-start.6
  73.7 1.6 %copy-done.6 = f32[8,8,8192]{2,1,0:T(8,128)S(1)} copy-done((f32[8,8,8192]{2,1,0:T(8,128)S(1)}, f32[8,8,8192]{2,1,0:T(8,128)}, u32[]{:S(2)}) %copy-start.6) | copy-done | bytes 2097176
  75.3 6.5 %second_primal.1 = (f32[8,8,8192]{2,1,0:T(8,128)}, f32[8,8192]{1,0:T(8,128)S(1)}, f32[8,8192]{1,0:T(8,128)S(1)}, f32[8,8192]{1,0:T(8,128)S(1)}, f32[1,8192]{1,0:T(1,128)S(1)}, /*index=5*/f32[8,128]{1,0:T(8,128)S(1)}) custom-call(f32[8]{0:T(128)S(1)} %copy-done.22, f32[32,8,128]{2,1,0:T(8,128)S(1)} %all-to-all-done.2.moved_ref, ...), custom_call_target="tpu_custom_call" | custom-call | tf_op jit(solution)/shard_map/second_primal/pallas_call | solution.py:331
  81.8 0.7 copy-done.13
  82.5 0.7 copy-done.15
  83.2 2.5 %collective-permute-start.3 = (f32[1,8192]{1,0:T(1,128)S(1)}, f32[1,8192]{1,0:T(1,128)S(1)}, u32[]{:S(2)}, u32[]{:S(2)}) collective-permute-start(f32[1,8192]{1,0:T(1,128)S(1)} %get-tuple-element.42), channel_id=1, source_target_pairs={{0,8},{8,16},{16,24},{24,32},{32,40},{40,48},{48,56},{56,64},{64,7... | collective-permute-start | bytes 98312 | tf_op jit(solution)/shard_map/ppermute | solution.py:284
  85.7 0.6 second_use.1
  86.3 0.1 reshape.21
  86.4 9.0 %all_to_all.22 = f32[8,1,512]{2,1,0:T(1,128)S(1)} all-to-all(f32[8,1,512]{2,1,0:T(1,128)S(1)} %reshape.21), channel_id=1, replica_groups=mesh['day'=32,'cls'=8] {'cls'}, dimensions={0} | all-to-all | bytes 32768 | tf_op jit(solution)/shard_map/all_to_all | solution.py:342
  95.4 0.7 reduce.1
  96.1 0.1 reshape.22.in_ref
  96.2 0.0 collective-permute-done.3.prior_ref
  96.2 0.0 copy-done.20
  96.2 0.0 copy-start.14
  96.2 0.9 copy-done.14
  97.2 0.9 copy-done.16
  98.1 0.8 last_duals.1
  (14 shorter events, 0.1 us)
Async XLA Ops:
  1.6 20.1 %collective-permute-start = (f32[1,8192]{1,0:T(1,128)S(1)}, f32[1,8192]{1,0:T(1,128)S(1)}, u32[]{:S(2)}, u32[]{:S(2)}) collective-permute-start(f32[1,8192]{1,0:T(1,128)S(1)} %slice.3), channel_id=1, source_target_pairs={{8,0},{16,8},{24,16},{32,24},{40,32},{48,40},{56,48},{64,56},{72,6... | collective-permute-start | bytes 98312 | tf_op jit(solution)/shard_map/ppermute | solution.py:289
  21.7 1.6 %copy-start = (f32[8,8,8192]{2,1,0:T(8,128)S(1)}, f32[8,8,8192]{2,1,0:T(8,128)}, u32[]{:S(2)}) copy-start(f32[8,8,8192]{2,1,0:T(8,128)} %cost_ref.3) | copy-start | bytes 6291460
  23.3 0.9 copy-start.2
  24.3 1.6 %copy-start.4 = (f32[8,8,8192]{2,1,0:T(8,128)S(1)}, f32[8,8,8192]{2,1,0:T(8,128)}, u32[]{:S(2)}) copy-start(f32[8,8,8192]{2,1,0:T(8,128)} %x_ref.1) | copy-start | bytes 6291460
  25.9 0.9 copy-start.7
  26.8 0.9 copy-start.9
  27.8 0.8 copy-start.11
  28.5 0.8 copy-start.17
  29.3 0.8 copy-start.19
  30.1 0.7 copy-start.21
  30.7 0.7 copy-start.23
  31.4 42.2 %copy-start.3 = (f32[8,8192]{1,0:T(8,128)S(1)}, f32[8,8192]{1,0:T(8,128)}, u32[]{:S(2)}) copy-start(f32[8,8192]{1,0:T(8,128)} %inflow_ref.9) | copy-start | bytes 786436
  31.4 42.2 %copy-start.8 = (f32[8,8192]{1,0:T(8,128)S(1)}, f32[8,8192]{1,0:T(8,128)}, u32[]{:S(2)}) copy-start(f32[8,8192]{1,0:T(8,128)} %w_ref.3) | copy-start | bytes 786436
  31.4 42.2 %copy-start.10 = (f32[8,8192]{1,0:T(8,128)S(1)}, f32[8,8192]{1,0:T(8,128)}, u32[]{:S(2)}) copy-start(f32[8,8192]{1,0:T(8,128)} %upper_ref.3) | copy-start | bytes 786436
  36.7 1.3 %copy-start.5 = (f32[8,8,8192]{2,1,0:T(8,128)}, f32[8,8,8192]{2,1,0:T(8,128)S(1)}, u32[]{:S(2)}) copy-start(f32[8,8,8192]{2,1,0:T(8,128)S(1)} %get-tuple-element.35.x_ref) | copy-start | bytes 6291460
  38.0 35.6 %copy-start.1 = (f32[8,8,8192]{2,1,0:T(8,128)S(1)}, f32[8,8,8192]{2,1,0:T(8,128)}, u32[]{:S(2)}) copy-start(f32[8,8,8192]{2,1,0:T(8,128)} %cost_ref.3) | copy-start | bytes 6291460
  38.0 35.6 %copy-start.12 = (s32[8192]{0:T(1024)S(1)}, s32[8192]{0:T(1024)}, u32[]{:S(2)}) copy-start(s32[8192]{0:T(1024)} %param.19) | copy-start | bytes 98308
  38.0 35.6 %copy-start.18 = (s32[8192]{0:T(1024)S(1)}, s32[8192]{0:T(1024)}, u32[]{:S(2)}) copy-start(s32[8192]{0:T(1024)} %param.20) | copy-start | bytes 98308
  38.0 35.6 %copy-start.22 = (f32[8]{0:T(128)S(1)}, f32[8]{0:T(128)}, u32[]{:S(2)}) copy-start(f32[8]{0:T(128)} %usage_ref.3) | copy-start | bytes 100
  38.1 5.6 %collective-permute-start.1 = (f32[1,8192]{1,0:T(1,128)S(1)}, f32[1,8192]{1,0:T(1,128)S(1)}, u32[]{:S(2)}, u32[]{:S(2)}) collective-permute-start(f32[1,8192]{1,0:T(1,128)S(1)} %get-tuple-element.30), channel_id=1, source_target_pairs={{0,8},{8,16},{16,24},{24,32},{32,40},{40,48},{48,56},{56,64},{64,7... | collective-permute-start | bytes 98312 | tf_op jit(solution)/shard_map/ppermute | solution.py:284
  54.7 18.9 %all-to-all-start.2 = ((f32[32,8,128]{2,1,0:T(8,128)}), f32[32,8,128]{2,1,0:T(8,128)S(1)}, u32[]{:S(2)}, u32[]{:S(2)}) async-start(f32[32,8,128]{2,1,0:T(8,128)} %get-tuple-element.33), calls=%async_computation.2 | async-start | bytes 262144 | tf_op jit(solution)/shard_map/all_to_all | solution.py:330
  66.0 5.5 %collective-permute-start.2 = (f32[1,8320]{1,0:T(1,128)S(1)}, f32[1,8320]{1,0:T(1,128)S(1)}, u32[]{:S(2)}, u32[]{:S(2)}) collective-permute-start(f32[1,8320]{1,0:T(1,128)S(1)} %get-tuple-element.36), channel_id=1, source_target_pairs={{8,0},{16,8},{24,16},{32,24},{40,32},{48,40},{56,48},{64,56},{72,6... | collective-permute-start | bytes 99848 | tf_op jit(solution)/shard_map/ppermute | solution.py:289
  73.7 1.6 %copy-start.6 = (f32[8,8,8192]{2,1,0:T(8,128)S(1)}, f32[8,8,8192]{2,1,0:T(8,128)}, u32[]{:S(2)}) copy-start(f32[8,8,8192]{2,1,0:T(8,128)} %copy-done.5) | copy-start | bytes 6291460
  75.2 20.9 %copy-start.20 = (f32[8,32]{1,0:T(8,128)S(1)}, f32[8,32]{1,0:T(8,128)}, u32[]{:S(2)}) copy-start(f32[8,32]{1,0:T(8,128)} %room_ref.1) | copy-start | bytes 3076
  81.8 0.7 copy-start.13
  82.5 0.7 copy-start.15
  83.2 13.0 %collective-permute-start.3 = (f32[1,8192]{1,0:T(1,128)S(1)}, f32[1,8192]{1,0:T(1,128)S(1)}, u32[]{:S(2)}, u32[]{:S(2)}) collective-permute-start(f32[1,8192]{1,0:T(1,128)S(1)} %get-tuple-element.42), channel_id=1, source_target_pairs={{0,8},{8,16},{16,24},{24,32},{32,40},{40,48},{48,56},{56,64},{64,7... | collective-permute-start | bytes 98312 | tf_op jit(solution)/shard_map/ppermute | solution.py:284
  96.2 1.0 copy-start.14
  97.2 0.9 copy-start.16

commit v2 on v1

--- a/solution.py
+++ b/solution.py
@@ -8,12 +8,13 @@
 ETA = 0.3
 EPS = 1e-6
 LANES = 128
+BLOCK = 1024
 STEP = 256
 PART = 1024
 WIDE = 64
 
 VM = pl.BlockSpec(memory_space=pltpu.VMEM)
-SM = pl.BlockSpec(memory_space=pltpu.SMEM)
+ANY = pl.BlockSpec(memory_space=pl.ANY)
 F32 = jnp.float32
 
 
@@ -21,17 +22,21 @@
     return jax.ShapeDtypeStruct(shape, F32)
 
 
-def call(body, name, outs, ins, scratch=(), cost=None):
+def call(body, name, outs, ins, scratch=(), cost=None, limit=4, out_specs=None):
     return pl.pallas_call(
         body,
         name=name,
         out_shape=outs,
         in_specs=ins,
-        out_specs=[VM] * len(outs),
+        out_specs=out_specs or [VM] * len(outs),
         scratch_shapes=list(scratch),
-        compiler_params=pltpu.CompilerParams(vmem_limit_bytes=40 << 20),
+        compiler_params=pltpu.CompilerParams(vmem_limit_bytes=limit << 20),
         cost_estimate=cost,
     )
+
+
+def in_hbm(*arrays):
+    return [pltpu.with_memory_space_constraint(a, pltpu.HBM) for a in arrays]
 
 
 def rows_iota(shape):
@@ -130,18 +135,60 @@
     return moved
 
 
+def start(caps_ref, room_ref, w_ref, out_ref, row_ref, caps, room, sems):
+    copies = [
+        pltpu.make_async_copy(caps_ref, caps, sems.at[0]),
+        pltpu.make_async_copy(room_ref, room, sems.at[1]),
+        pltpu.make_async_copy(w_ref.at[pl.ds(0, 1)], row_ref, sems.at[2]),
+    ]
+    for copy in copies:
+        copy.start()
+    out_ref[...] = jnp.zeros(out_ref.shape, F32)
+    copies[0].wait()
+    copies[1].wait()
+    own = caps.shape[1]
+    for k in range(out_ref.shape[0]):
+        out_ref[k, :, :own] = caps[...]
+        out_ref[k, :, own : 2 * own] = room[...]
+    copies[2].wait()
+
+
 def first_primal(
-    usage_ref, table_ref, ends_ref, after_ref, cost_ref, x_ref, w_ref, inflow_ref, upper_ref,
-    fac_ref, count_ref, index_ref,
-    x1_ref, sum_ref, weighted_ref, last_ref, lead_ref, gamma_ref, moved_ref, caps_ref, room_ref,
+    usage_hbm, table_hbm, cost_hbm, x_hbm, w_hbm, inflow_hbm, upper_hbm, fac_hbm, count_hbm, index_hbm,
+    ends_ref, after_ref,
+    cost_ref, x1_ref, w_ref, inflow_ref, bound_ref, fac_ref,
+    sum_ref, weighted_ref, last_ref, lead_ref, gamma_ref, moved_ref, caps_ref, room_ref, weights_ref,
+    usage_ref, table_ref, count_ref, index_ref, sems,
 ):
     days, classes = w_ref.shape
-    own = ends_ref.shape[2]
+    small = [
+        (usage_hbm, usage_ref), (table_hbm, table_ref), (fac_hbm, fac_ref), (count_hbm, count_ref),
+        (index_hbm, index_ref), (w_hbm, w_ref), (inflow_hbm, inflow_ref), (upper_hbm, bound_ref),
+    ]
+    small = [pltpu.make_async_copy(a, b, sems.at[k]) for k, (a, b) in enumerate(small)]
+    large = []
+    for k in range(classes // BLOCK):
+        at = pl.ds(k * BLOCK, BLOCK)
+        place = len(small) + 2 * k
+        large.append((
+            pltpu.make_async_copy(cost_hbm.at[:, :, at], cost_ref.at[:, :, at], sems.at[place]),
+            pltpu.make_async_copy(x_hbm.at[:, :, at], x1_ref.at[:, :, at], sems.at[place + 1]),
+        ))
+    for copy in small:
+        copy.start()
+    for pair in large:
+        for copy in pair:
+            copy.start()
+    own = caps_ref.shape[1] // ends_ref.shape[0]
     for k in range(ends_ref.shape[0]):
-        caps_ref[:, k * own : (k + 1) * own] = ends_ref[k, :days, :]
-        room_ref[:, k * own : (k + 1) * own] = ends_ref[k, days:, :]
+        caps_ref[:, k * own : (k + 1) * own] = ends_ref[k, :, :own]
+        room_ref[:, k * own : (k + 1) * own] = ends_ref[k, :, own : 2 * own]
     caps = caps_ref[...]
-    weights = tile_of(usage_ref, 8, rows_iota((8, STEP)))
+    for copy in small:
+        copy.wait()
+    weights = tile_of(usage_ref, 8, rows_iota((8, LANES)))
+    weights_ref[...] = weights
+    weights = jnp.concatenate([weights] * (STEP // LANES), axis=1)
     table = tile_of(table_ref, 16, lanes_iota((8, LANES)))
     rows = rows_iota((days, STEP))
 
@@ -149,18 +196,24 @@
         at = pl.ds(pl.multiple_of(j * STEP, STEP), STEP)
         gamma = gamma_of(table, index_ref[:, at])
         gamma_ref[:, at] = gamma[:1]
-        bound = jnp.where(rows < count_ref[:, at], upper_ref[:, at], 0.0)
+        bound = jnp.where(rows < count_ref[:, at], bound_ref[:, at], 0.0)
+        bound_ref[:, at] = bound
         w = w_ref[:, at]
         after = jnp.where(rows == days - 1, after_ref[:, at], pltpu.roll(w, days - 1, 0))
         moved = primal_rows(
             at, w - gamma * after, pulled_of(caps, fac_ref[:, at]), F32(ETA), weights, bound,
-            cost_ref, x_ref, x1_ref, sum_ref, weighted_ref, moved,
+            cost_ref, x1_ref, x1_ref, sum_ref, weighted_ref, moved,
         )
         last_ref[:, at] = sum_ref[days - 1 :, at]
         lead_ref[:, at] = w[:1] - ETA * (sum_ref[:1, at] - inflow_ref[:1, at])
         return moved
 
-    moved = lax.fori_loop(0, classes // STEP, step, jnp.zeros((8, STEP), F32))
+    moved = jnp.zeros((8, STEP), F32)
+    each = BLOCK // STEP
+    for k, pair in enumerate(large):
+        for copy in pair:
+            copy.wait()
+        moved = lax.fori_loop(k * each, (k + 1) * each, step, moved)
     moved_ref[...] = folded(moved)
     lead_ref[:, classes:] = jnp.ones((1, LANES), F32)
 
@@ -181,11 +234,13 @@
     )
 
 
-def first_send(use_ref, moved_ref, dual_ref, prior_ref, sum_ref, inflow_ref, gamma_ref, out_ref):
+def first_send(use_ref, moved_ref, dual_ref, prior_ref, lead_ref, sum_ref, inflow_ref, gamma_ref, out_ref, edge_ref):
     days, classes = sum_ref.shape
     total = jnp.zeros((1, PART), F32)
+    more = ETA * jnp.max(lead_ref[:, classes:], axis=1, keepdims=True)
     for k in range(classes // PART):
         at = pl.ds(k * PART, PART)
+        edge_ref[:, at] = lead_ref[:, at] + more * (gamma_ref[:, at] * sum_ref[days - 1 :, at])
         gap = sum_ref[:1, at] - gamma_ref[:, at] * prior_ref[:, at] - inflow_ref[:1, at]
         total = total + gap * gap
     edge = (ETA * ETA) * folded(total)
@@ -216,9 +271,10 @@
 
 
 def second_primal(
-    usage_ref, moved_ref, caps_ref, cost_ref, x_ref, w_ref, inflow_ref, upper_ref, fac_ref, count_ref,
-    gamma_ref, sums_ref, prior_ref, lead_ref,
-    x2_ref, w1_ref, sum_ref, weighted_ref, last_ref, omega_ref,
+    moved_ref, weights_ref, caps_ref, cost_ref, x_ref, w_ref, inflow_ref, bound_ref, fac_ref,
+    gamma_ref, sums_ref, prior_ref, edge_ref,
+    out_hbm, w1_ref, sum_ref, weighted_ref, last_ref, omega_ref,
+    x2_ref, sems,
 ):
     days, classes = w_ref.shape
     total = moved_ref[0]
@@ -230,47 +286,56 @@
     omega_ref[...] = jnp.broadcast_to(omega, omega_ref.shape)
     tau = jnp.broadcast_to(ETA / omega, (8, STEP))
     caps = caps_ref[...]
-    weights = tile_of(usage_ref, 8, rows_iota((8, STEP)))
+    weights = jnp.concatenate([weights_ref[...]] * (STEP // LANES), axis=1)
     rows = rows_iota((days, STEP))
-    more = ETA * jnp.max(lead_ref[:, classes:], axis=1, keepdims=True)
 
     def step(j, _):
         at = pl.ds(pl.multiple_of(j * STEP, STEP), STEP)
         gamma = gamma_ref[:, at]
-        bound = jnp.where(rows < count_ref[:, at], upper_ref[:, at], 0.0)
         sums = sums_ref[:, at]
         prior = jnp.where(rows == 0, prior_ref[:, at], pltpu.roll(sums, 1, 0))
         w = w_ref[:, at] - ETA * (sums - gamma * prior - inflow_ref[:, at])
         w1_ref[:, at] = w
-        edge = lead_ref[:, at] + more * gamma * sums[days - 1 :]
-        after = jnp.where(rows == days - 1, edge, pltpu.roll(w, days - 1, 0))
+        after = jnp.where(rows == days - 1, edge_ref[:, at], pltpu.roll(w, days - 1, 0))
         primal_rows(
-            at, w - gamma * after, pulled_of(caps, fac_ref[:, at]), tau, weights, bound,
+            at, w - gamma * after, pulled_of(caps, fac_ref[:, at]), tau, weights, bound_ref[:, at],
             cost_ref, x_ref, x2_ref, sum_ref, weighted_ref, None,
         )
         last_ref[:, at] = sum_ref[days - 1 :, at]
         return 0
 
-    lax.fori_loop(0, classes // STEP, step, 0)
+    copies = []
+    each = BLOCK // STEP
+    for k in range(classes // BLOCK):
+        lax.fori_loop(k * each, (k + 1) * each, step, 0)
+        at = pl.ds(k * BLOCK, BLOCK)
+        copies.append(pltpu.make_async_copy(x2_ref.at[:, :, at], out_hbm.at[:, :, at], sems.at[k]))
+        copies[-1].start()
+    for copy in copies:
+        copy.wait()
 
 
 def second_use(weighted_ref, fac_ref, caps_ref, out_ref):
     days = weighted_ref.shape[0]
     parts = facility_sums(weighted_ref, fac_ref, caps_ref.shape[1])
-    own = out_ref.shape[2]
+    own = caps_ref.shape[1] // out_ref.shape[0]
+    out_ref[...] = jnp.zeros(out_ref.shape, F32)
     for k in range(out_ref.shape[0]):
         g, place = divmod(k * own, WIDE)
-        out_ref[k, :days, :] = parts[g][:, place : place + own]
-        out_ref[k, days:, :] = caps_ref[:, k * own : (k + 1) * own]
+        out_ref[k, :, :own] = parts[g][:, place : place + own]
+        out_ref[k, :, own : 2 * own] = caps_ref[:, k * own : (k + 1) * own]
 
 
 def last_duals(in_ref, room_ref, omega_ref, w_ref, sum_ref, prior_ref, inflow_ref, gamma_ref, w2_ref, caps2_ref):
     days, classes = w_ref.shape
     sigma = ETA * omega_ref[...]
-    use = in_ref[0, :days]
+    own = room_ref.shape[1]
+    use = in_ref[0, :, :own]
     for k in range(1, in_ref.shape[0]):
-        use = use + in_ref[k, :days]
-    caps2_ref[...] = jnp.minimum(in_ref[0, days:] - sigma[:1, :1] * (use - room_ref[...]), 0.0)
+        use = use + in_ref[k, :, :own]
+    caps2_ref[...] = jnp.minimum(
+        in_ref[0, :, own : 2 * own] - sigma[:1, :1] * (use - room_ref[...]), 0.0
+    )
     rows = rows_iota((days, LANES))
     for k in range(classes // LANES):
         at = pl.ds(k * LANES, LANES)
@@ -301,27 +366,35 @@
     count = option_count.reshape(1, classes)
     index = decay_index.reshape(1, classes)
 
-    ends = jnp.broadcast_to(
-        jnp.concatenate([ycap_start, capacity], axis=0)[None], (blocks, 2 * days, own)
-    )
-    after = to_previous(ybal_start[:1])
+    ends, row = call(
+        start, "start", [struct(blocks, days, LANES), struct(1, classes)], [ANY] * 3,
+        [pltpu.VMEM((days, own), F32), pltpu.VMEM((days, own), F32), pltpu.SemaphoreType.DMA((3,))],
+    )(*in_hbm(ycap_start, capacity, ybal_start))
+    after = to_previous(row)
     ends = lax.all_to_all(ends, "cls", 0, 0)
-    x1, sums, weighted, last, lead, gamma, moved, caps, room = call(
+    (cost, x1, ybal_start, inflow, bound, fac, sums, weighted, last, lead, gamma, moved, caps, room,
+     weights) = call(
         first_primal, "first_primal",
-        [struct(days, opts, classes), struct(days, classes), struct(days, classes), struct(1, classes),
+        [struct(days, opts, classes), struct(days, opts, classes), struct(days, classes),
+         struct(days, classes), struct(opts, classes), jax.ShapeDtypeStruct((1, classes), jnp.int32),
+         struct(days, classes), struct(days, classes), struct(1, classes),
          struct(1, classes + LANES), struct(1, classes), struct(8, LANES), struct(days, facilities),
-         struct(days, facilities)],
-        [SM, SM] + [VM] * 10,
-    )(usage, decay_table, ends, after, cost, x_start, ybal_start, inflow, upper, fac, count, index)
+         struct(days, facilities), struct(8, LANES)],
+        [ANY] * 10 + [VM] * 2,
+        [pltpu.SMEM((opts,), F32), pltpu.SMEM(decay_table.shape, F32), pltpu.VMEM((1, classes), jnp.int32),
+         pltpu.VMEM((1, classes), jnp.int32), pltpu.SemaphoreType.DMA((8 + 2 * (classes // BLOCK),))],
+    )(
+        *in_hbm(usage, decay_table, cost, x_start, ybal_start, inflow, upper, fac, count, index), ends, after
+    )
     prior = to_next(last)
     lead = to_previous(lead)
     use, dual = call(
         first_use, "first_use", [struct(days, facilities), struct(days, LANES)], [VM] * 5,
         cost=pl.CostEstimate(flops=10_000_000, bytes_accessed=8_000_000, transcendentals=0),
     )(weighted, sums, inflow, gamma, fac)
-    (sent,) = call(first_send, "first_send", [struct(blocks, 2 * days, facilities)], [VM] * 7)(
-        use, moved, dual, prior, sums, inflow, gamma
-    )
+    sent, edge = call(
+        first_send, "first_send", [struct(blocks, 2 * days, facilities), struct(1, classes)], [VM] * 8
+    )(use, moved, dual, prior, lead, sums, inflow, gamma)
     got = lax.all_to_all(sent, "cls", 0, 0)
     caps1, sent = call(
         caps_step, "caps_step", [struct(days, facilities), struct(lax.axis_size("day"), days, LANES)],
@@ -332,11 +405,13 @@
         second_primal, "second_primal",
         [struct(days, opts, classes), struct(days, classes), struct(days, classes), struct(days, classes),
          struct(1, classes), struct(8, LANES)],
-        [SM] + [VM] * 13,
-    )(usage, got, caps1, cost, x1, ybal_start, inflow, upper, fac, count, gamma, sums, prior, lead)
+        [VM] * 13,
+        [pltpu.VMEM((days, opts, classes), F32), pltpu.SemaphoreType.DMA((classes // BLOCK,))],
+        out_specs=[ANY] + [VM] * 5,
+    )(got, weights, caps1, cost, x1, ybal_start, inflow, bound, fac, gamma, sums, prior, edge)
     prior2 = to_next(last2)
     (sent,) = call(
-        second_use, "second_use", [struct(blocks, 2 * days, own)], [VM] * 3,
+        second_use, "second_use", [struct(blocks, days, LANES)], [VM] * 3,
         cost=pl.CostEstimate(flops=10_000_000, bytes_accessed=8_000_000, transcendentals=0),
     )(weighted2, fac, caps1)
     got = lax.all_to_all(sent, "cls", 0, 0)

time: 99.8 us -> 83 us (0.83)
  local copies, waits for them, and re-layouts: 17.7 us -> 0.01 us
  waiting for transfers between devices: 5.84 us -> 8.63 us
  other arithmetic: 2.08 us -> 0 us
  Pallas kernels: 14.6 us -> 16 us
    unnamed x52 -> x2, local copies, waits for them, and re-layouts: 16.2 us -> 0.01 us
    all_to_all x1, blocking collectives: 12.9 us -> 19.8 us  [local(): got = lax.all_to_all(sent, 'day', 0, 0)]
    all_to_all x2 -> x1, blocking collectives: 19.3 us -> 12.6 us  [local(): got = lax.all_to_all(sent, 'cls', 0, 0)]
    all_to_all x1 -> x2, waiting for transfers between devices: 2.09 us -> 4.29 us  [the longest x1 3.25 us: local(): got = lax.all_to_all(sent, 'cls', 0, 0)]
    pallas_call x2 -> x3, Pallas kernels: 0.68 us -> 2.8 us  [the longest x1 1.43 us: local(): call(start, 'start', [struct(blocks, days, LANES), struct(1, classes)], [...]
    ppermute x2, starting transfers between devices: 7.1 us -> 5.55 us  [to_next(): return lax.ppermute(row, 'day', [(i, i + 1) for i in range(n - 1)])]
    all_to_all x2 -> x0, other arithmetic: 1.37 us -> none  [the longest x1 0.68 us: local(): got = lax.all_to_all(sent, 'cls', 0, 0)]
    pallas_call x1, Pallas kernels: 6.5 us -> 5.38 us  [local(): call(second_primal, 'second_primal', [struct(days, opts, classes), struct...]
  transfers between devices with their start and end apart: 5 -> 6, of which waited for: 3 -> 5; matrix products, arithmetic and copies ran while one was open for 3% -> 0% of each run, Pallas kernels for 1% -> 1%
where the time goes in v2:
time: 83 us; the launch traced here: 82.5 us
  blocking collectives  32.4 us (39%)
  starting transfers between devices  24.8 us (30%)
  Pallas kernels  16 us (19%)
  waiting for transfers between devices  8.63 us (10%)
    all_to_all x1, blocking collectives, local(): got = lax.all_to_all(sent, 'day', 0, 0)  19.8 us
    all_to_all x1, blocking collectives, local(): got = lax.all_to_all(sent, 'cls', 0, 0)  12.6 us
    all_to_all x1, starting transfers between devices, local(): ends = lax.all_to_all(ends, 'cls', 0, 0)  9.03 us
    ppermute x2, starting transfers between devices, to_previous(): return lax.ppermute(row, 'day', [(i + 1, i) for i in range(n - 1)])  6.86 us
    pallas_call x1, Pallas kernels, local(): call(first_primal, 'first_primal', [struct(days, opts, classes), struct(d...  6.28 us
    ppermute x2, starting transfers between devices, to_next(): return lax.ppermute(row, 'day', [(i, i + 1) for i in range(n - 1)])  5.55 us
    pallas_call x1, Pallas kernels, local(): call(second_primal, 'second_primal', [struct(days, opts, classes), struct...  5.38 us
    all_to_all x1, starting transfers between devices, local(): got = lax.all_to_all(sent, 'cls', 0, 0)  3.34 us
  transfers between devices with their start and end apart: 6, of which 5 were waited for; matrix products, arithmetic and copies ran while one was open for 0% of the time, Pallas kernels for 1%

profile of v2, /device:TPU:1, one launch (start us, length us, event | category | flops | bytes accessed | tf_op | source)
XLA Modules:
  0.0 82.5 jit_solution(10202237692741058035)
XLA Ops:
  0.6 1.4 %start.1 = (f32[8,8,128]{2,1,0:T(8,128)}, f32[1,8192]{1,0:T(1,128)S(1)}) custom-call(f32[8,32]{1,0:T(8,128)} %caps_ref.1, f32[8,32]{1,0:T(8,128)} %room_ref.3, f32[8,8192]{1,0:T(8,128)} %w_hbm.1), custom_call_target="tpu_custom_call" | custom-call | tf_op jit(solution)/shard_map/start/pallas_call | solution.py:369
  2.1 9.0 %all-to-all-start = ((f32[8,8,128]{2,1,0:T(8,128)}), f32[8,8,128]{2,1,0:T(8,128)S(1)}, u32[]{:S(2)}, u32[]{:S(2)}) async-start(f32[8,8,128]{2,1,0:T(8,128)} %get-tuple-element.34), calls=%async_computation | async-start | bytes 65536 | tf_op jit(solution)/shard_map/all_to_all | solution.py:374
  11.1 2.9 %collective-permute-start = (f32[1,8192]{1,0:T(1,128)S(1)}, f32[1,8192]{1,0:T(1,128)S(1)}, u32[]{:S(2)}, u32[]{:S(2)}) collective-permute-start(f32[1,8192]{1,0:T(1,128)S(1)} %get-tuple-element.35), channel_id=1, source_target_pairs={{8,0},{16,8},{24,16},{32,24},{40,32},{48,40},{56,48},{64,56},{72,6... | collective-permute-start | bytes 98312 | tf_op jit(solution)/shard_map/ppermute | solution.py:354
  14.0 3.0 %collective-permute-done.after_ref = f32[1,8192]{1,0:T(1,128)S(1)} collective-permute-done((f32[1,8192]{1,0:T(1,128)S(1)}, f32[1,8192]{1,0:T(1,128)S(1)}, u32[]{:S(2)}, u32[]{:S(2)}) %collective-permute-start) | collective-permute-done | bytes 32800 | tf_op jit(solution)/shard_map/ppermute | solution.py:354
  16.9 1.0 %all-to-all-done.ends_ref = f32[8,8,128]{2,1,0:T(8,128)S(1)} async-done(((f32[8,8,128]{2,1,0:T(8,128)}), f32[8,8,128]{2,1,0:T(8,128)S(1)}, u32[]{:S(2)}, u32[]{:S(2)}) %all-to-all-start) | async-done | bytes 32800 | tf_op jit(solution)/shard_map/all_to_all | solution.py:374
  18.0 6.3 %first_primal.1 = (f32[8,8,8192]{2,1,0:T(8,128)S(1)}, f32[8,8,8192]{2,1,0:T(8,128)S(1)}, f32[8,8192]{1,0:T(8,128)S(1)}, f32[8,8192]{1,0:T(8,128)S(1)}, f32[8,819...) custom-call(f32[8]{0:T(128)} %usage_hbm.1, ...), custom_call_target="tpu_custom_call" | custom-call | tf_op jit(solution)/shard_map/first_primal/pallas_call | solution.py:376
  24.3 4.0 %collective-permute-start.2 = (f32[1,8320]{1,0:T(1,128)S(1)}, f32[1,8320]{1,0:T(1,128)S(1)}, u32[]{:S(2)}, u32[]{:S(2)}) collective-permute-start(f32[1,8320]{1,0:T(1,128)S(1)} %get-tuple-element.45), channel_id=1, source_target_pairs={{8,0},{16,8},{24,16},{32,24},{40,32},{48,40},{56,48},{64,56},{72,6... | collective-permute-start | bytes 99848 | tf_op jit(solution)/shard_map/ppermute | solution.py:354
  28.3 3.0 %collective-permute-start.1 = (f32[1,8192]{1,0:T(1,128)S(1)}, f32[1,8192]{1,0:T(1,128)S(1)}, u32[]{:S(2)}, u32[]{:S(2)}) collective-permute-start(f32[1,8192]{1,0:T(1,128)S(1)} %get-tuple-element.44), channel_id=1, source_target_pairs={{0,8},{8,16},{16,24},{24,32},{32,40},{40,48},{48,56},{56,64},{64,7... | collective-permute-start | bytes 98312 | tf_op jit(solution)/shard_map/ppermute | solution.py:349
  31.3 0.6 first_use.1
  32.0 0.4 collective-permute-done.1.prior_ref
  32.3 0.0 collective-permute-done.2.lead_ref
  32.3 0.1 first_send.1
  32.4 12.6 %all_to_all.20.in_ref = f32[8,16,256]{2,1,0:T(8,128)S(1)} all-to-all(f32[8,16,256]{2,1,0:T(8,128)S(1)} %get-tuple-element.46), channel_id=1, replica_groups=mesh['day'=32,'cls'=8] {'cls'}, dimensions={0} | all-to-all | bytes 262144 | tf_op jit(solution)/shard_map/all_to_all | solution.py:398
  45.1 19.8 %all_to_all.21.moved_ref = f32[32,8,128]{2,1,0:T(8,128)S(1)} all-to-all(f32[32,8,128]{2,1,0:T(8,128)S(1)} %get-tuple-element.49), channel_id=1, replica_groups=mesh['day'=32,'cls'=8] {'day'}, dimensions={0} | all-to-all | bytes 262144 | tf_op jit(solution)/shard_map/all_to_all | solution.py:403
  64.9 0.0 copy-start
  64.9 5.4 %second_primal.1 = (f32[8,8,8192]{2,1,0:T(8,128)}, f32[8,8192]{1,0:T(8,128)S(1)}, f32[8,8192]{1,0:T(8,128)S(1)}, f32[8,8192]{1,0:T(8,128)S(1)}, f32[1,8192]{1,0:T(1,128)S(1)}, /*index=5*/f32[8,128]{1,0:T(8,128)S(1)}) custom-call(f32[32,8,128]{2,1,0:T(8,128)S(1)} %all_to_all.21.moved_ref, f32[8,128]{1,0:T(8,128)S(1)} %get-tuple-element.50.weights_ref, ...), custom_call_target="tpu_custom_call" | custom-call | tf_op jit(solution)/shard_map/second_primal/pallas_call | solution.py:404
  70.3 1.3 %second_use.1 = f32[8,8,128]{2,1,0:T(8,128)} custom-call(f32[8,8192]{1,0:T(8,128)S(1)} %get-tuple-element.58.weighted_ref, s32[1,8192]{1,0:T(1,128)S(1)} %get-tuple-element.40.fac_ref, f32[8,256]{1,0:T(8,128)S(1)} %get-tuple-element.51.caps_ref), custom_call_target="tpu_custom_call" | custom-call | flops 10000000 | bytes 8000000 | tf_op jit(solution)/shard_map/second_use/pallas_call | solution.py:413
  71.5 3.3 %all-to-all-start.3 = ((f32[8,8,128]{2,1,0:T(8,128)}), f32[8,8,128]{2,1,0:T(8,128)S(1)}, u32[]{:S(2)}, u32[]{:S(2)}) async-start(f32[8,8,128]{2,1,0:T(8,128)} %second_use.1), calls=%async_computation.3 | async-start | bytes 65536 | tf_op jit(solution)/shard_map/all_to_all | solution.py:417
  74.9 2.5 %collective-permute-start.3 = (f32[1,8192]{1,0:T(1,128)S(1)}, f32[1,8192]{1,0:T(1,128)S(1)}, u32[]{:S(2)}, u32[]{:S(2)}) collective-permute-start(f32[1,8192]{1,0:T(1,128)S(1)} %get-tuple-element.62), channel_id=1, source_target_pairs={{0,8},{8,16},{16,24},{24,32},{32,40},{40,48},{48,56},{56,64},{64,7... | collective-permute-start | bytes 98312 | tf_op jit(solution)/shard_map/ppermute | solution.py:349
  77.4 1.0 %collective-permute-done.3.prior_ref = f32[1,8192]{1,0:T(1,128)S(1)} collective-permute-done((f32[1,8192]{1,0:T(1,128)S(1)}, f32[1,8192]{1,0:T(1,128)S(1)}, u32[]{:S(2)}, u32[]{:S(2)}) %collective-permute-start.3) | collective-permute-done | bytes 32800 | tf_op jit(solution)/shard_map/ppermute | solution.py:349
  78.4 3.3 %all-to-all-done.3.in_ref = f32[8,8,128]{2,1,0:T(8,128)S(1)} async-done(((f32[8,8,128]{2,1,0:T(8,128)}), f32[8,8,128]{2,1,0:T(8,128)S(1)}, u32[]{:S(2)}, u32[]{:S(2)}) %all-to-all-start.3) | async-done | bytes 32800 | tf_op jit(solution)/shard_map/all_to_all | solution.py:417
  81.7 0.0 copy-done
  81.7 0.9 %last_duals.1 = (f32[8,8192]{1,0:T(8,128)}, f32[8,32]{1,0:T(8,128)}) custom-call(f32[8,8,128]{2,1,0:T(8,128)S(1)} %all-to-all-done.3.in_ref, f32[8,32]{1,0:T(8,128)S(1)} %copy-done, f32[8,128]{1,0:T(8,128)S(1)} %get-tuple-element.59.omega_ref, f32[8,8192]{1,0:T(8,128)S(1)} %get-tuple-element.60.w_ref, f32[8,8192]{1,0:T(8,128)S(1)} %get-tuple-element.61.sum_ref, ...), custom_call_target="tpu_custom_call" | custom-call | tf_op jit(solution)/shard_map/last_duals/pallas_call | solution.py:418
  (1 shorter events, 0.0 us)
Async XLA Ops:
  2.1 15.9 %all-to-all-start = ((f32[8,8,128]{2,1,0:T(8,128)}), f32[8,8,128]{2,1,0:T(8,128)S(1)}, u32[]{:S(2)}, u32[]{:S(2)}) async-start(f32[8,8,128]{2,1,0:T(8,128)} %get-tuple-element.34), calls=%async_computation | async-start | bytes 65536 | tf_op jit(solution)/shard_map/all_to_all | solution.py:374
  11.1 5.8 %collective-permute-start = (f32[1,8192]{1,0:T(1,128)S(1)}, f32[1,8192]{1,0:T(1,128)S(1)}, u32[]{:S(2)}, u32[]{:S(2)}) collective-permute-start(f32[1,8192]{1,0:T(1,128)S(1)} %get-tuple-element.35), channel_id=1, source_target_pairs={{8,0},{16,8},{24,16},{32,24},{40,32},{48,40},{56,48},{64,56},{72,6... | collective-permute-start | bytes 98312 | tf_op jit(solution)/shard_map/ppermute | solution.py:354
  24.3 8.1 %collective-permute-start.2 = (f32[1,8320]{1,0:T(1,128)S(1)}, f32[1,8320]{1,0:T(1,128)S(1)}, u32[]{:S(2)}, u32[]{:S(2)}) collective-permute-start(f32[1,8320]{1,0:T(1,128)S(1)} %get-tuple-element.45), channel_id=1, source_target_pairs={{8,0},{16,8},{24,16},{32,24},{40,32},{48,40},{56,48},{64,56},{72,6... | collective-permute-start | bytes 99848 | tf_op jit(solution)/shard_map/ppermute | solution.py:354
  28.3 4.0 %collective-permute-start.1 = (f32[1,8192]{1,0:T(1,128)S(1)}, f32[1,8192]{1,0:T(1,128)S(1)}, u32[]{:S(2)}, u32[]{:S(2)}) collective-permute-start(f32[1,8192]{1,0:T(1,128)S(1)} %get-tuple-element.44), channel_id=1, source_target_pairs={{0,8},{8,16},{16,24},{24,32},{32,40},{40,48},{48,56},{56,64},{64,7... | collective-permute-start | bytes 98312 | tf_op jit(solution)/shard_map/ppermute | solution.py:349
  64.9 16.8 %copy-start = (f32[8,32]{1,0:T(8,128)S(1)}, f32[8,32]{1,0:T(8,128)}, u32[]{:S(2)}) copy-start(f32[8,32]{1,0:T(8,128)} %room_ref.3) | copy-start | bytes 3076
  71.5 10.1 %all-to-all-start.3 = ((f32[8,8,128]{2,1,0:T(8,128)}), f32[8,8,128]{2,1,0:T(8,128)S(1)}, u32[]{:S(2)}, u32[]{:S(2)}) async-start(f32[8,8,128]{2,1,0:T(8,128)} %second_use.1), calls=%async_computation.3 | async-start | bytes 65536 | tf_op jit(solution)/shard_map/all_to_all | solution.py:417
  74.9 3.5 %collective-permute-start.3 = (f32[1,8192]{1,0:T(1,128)S(1)}, f32[1,8192]{1,0:T(1,128)S(1)}, u32[]{:S(2)}, u32[]{:S(2)}) collective-permute-start(f32[1,8192]{1,0:T(1,128)S(1)} %get-tuple-element.62), channel_id=1, source_target_pairs={{0,8},{8,16},{16,24},{24,32},{32,40},{40,48},{48,56},{56,64},{64,7... | collective-permute-start | bytes 98312 | tf_op jit(solution)/shard_map/ppermute | solution.py:349

commit v3 on v2

--- a/solution.py
+++ b/solution.py
@@ -8,12 +8,13 @@
 ETA = 0.3
 EPS = 1e-6
 LANES = 128
+STEP = 512
+PART = 1024
 BLOCK = 1024
-STEP = 256
-PART = 1024
 WIDE = 64
 
 VM = pl.BlockSpec(memory_space=pltpu.VMEM)
+PASS = pl.CostEstimate(flops=10_000_000, bytes_accessed=8_000_000, transcendentals=0)
 ANY = pl.BlockSpec(memory_space=pl.ANY)
 F32 = jnp.float32
 
@@ -120,19 +121,20 @@
     return out
 
 
-def primal_rows(at, kt, pulled, tau, weights, bound, cost_ref, x_ref, x1_ref, sum_ref, weighted_ref, moved):
-    for t in range(cost_ref.shape[0]):
-        grad = cost_ref[t, :, at] - kt[t : t + 1] - weights * pulled[t : t + 1]
-        old = x_ref[t, :, at]
-        new = jnp.minimum(jnp.maximum(old - tau * grad, 0.0), bound)
-        x1_ref[t, :, at] = new
-        gone = new - old
-        extra = new + gone
-        sum_ref[t : t + 1, at] = jnp.sum(extra, axis=0, keepdims=True)
-        weighted_ref[t : t + 1, at] = jnp.sum(weights * extra, axis=0, keepdims=True)
-        if moved is not None:
-            moved = moved + gone * gone
-    return moved
+def combined(a, b, mask, distance):
+    return jnp.where(mask, a, b) + pltpu.roll(jnp.where(mask, b, a), distance, 0)
+
+
+def row_sums(tiles):
+    rows = rows_iota(tiles[0].shape)
+    for distance in (1, 2, 4):
+        mask = jnp.bitwise_and(rows, distance) == 0
+        tiles = [combined(tiles[k], tiles[k + 1], mask, distance) for k in range(0, len(tiles), 2)]
+    return tiles[0]
+
+
+def spread(tile, row):
+    return jnp.broadcast_to(tile[row : row + 1], tile.shape)
 
 
 def start(caps_ref, room_ref, w_ref, out_ref, row_ref, caps, room, sems):
@@ -153,11 +155,37 @@
     copies[2].wait()
 
 
-def first_primal(
-    usage_hbm, table_hbm, cost_hbm, x_hbm, w_hbm, inflow_hbm, upper_hbm, fac_hbm, count_hbm, index_hbm,
-    ends_ref, after_ref,
-    cost_ref, x1_ref, w_ref, inflow_ref, bound_ref, fac_ref,
-    sum_ref, weighted_ref, last_ref, lead_ref, gamma_ref, moved_ref, caps_ref, room_ref, weights_ref,
+def lanes_of(j, u):
+    return pl.ds(pl.multiple_of(j * STEP, STEP) + u * LANES, LANES)
+
+
+def block_copies(pairs, sems):
+    classes = pairs[0][0].shape[2]
+    return [
+        [
+            pltpu.make_async_copy(
+                a.at[:, :, pl.ds(k * BLOCK, BLOCK)], b.at[:, :, pl.ds(k * BLOCK, BLOCK)], sems.at[n, k]
+            )
+            for n, (a, b) in enumerate(pairs)
+        ]
+        for k in range(classes // BLOCK)
+    ]
+
+
+def start_all(blocks):
+    for block in blocks:
+        for copy in block:
+            copy.start()
+
+
+def wait_all(block):
+    for copy in block:
+        copy.wait()
+
+
+def load(
+    usage_hbm, table_hbm, w_hbm, inflow_hbm, upper_hbm, fac_hbm, count_hbm, index_hbm,
+    kt_ref, w_ref, inflow_ref, bound_ref, fac_ref, gamma_ref, weights_ref,
     usage_ref, table_ref, count_ref, index_ref, sems,
 ):
     days, classes = w_ref.shape
@@ -166,56 +194,84 @@
         (index_hbm, index_ref), (w_hbm, w_ref), (inflow_hbm, inflow_ref), (upper_hbm, bound_ref),
     ]
     small = [pltpu.make_async_copy(a, b, sems.at[k]) for k, (a, b) in enumerate(small)]
-    large = []
-    for k in range(classes // BLOCK):
-        at = pl.ds(k * BLOCK, BLOCK)
-        place = len(small) + 2 * k
-        large.append((
-            pltpu.make_async_copy(cost_hbm.at[:, :, at], cost_ref.at[:, :, at], sems.at[place]),
-            pltpu.make_async_copy(x_hbm.at[:, :, at], x1_ref.at[:, :, at], sems.at[place + 1]),
-        ))
     for copy in small:
         copy.start()
-    for pair in large:
-        for copy in pair:
-            copy.start()
+    for copy in small:
+        copy.wait()
+    weights_ref[...] = tile_of(usage_ref, 8, rows_iota((8, LANES)))
+    table = tile_of(table_ref, 16, lanes_iota((8, LANES)))
+    rows = rows_iota((days, LANES))
+
+    def step(j, _):
+        for u in range(STEP // LANES):
+            at = lanes_of(j, u)
+            gamma = gamma_of(table, index_ref[:, at])
+            gamma_ref[:, at] = gamma[:1]
+            bound_ref[:, at] = jnp.where(rows < count_ref[:, at], bound_ref[:, at], 0.0)
+            w = w_ref[:, at]
+            kt_ref[:, at] = w - gamma * jnp.where(rows == days - 1, 0.0, pltpu.roll(w, days - 1, 0))
+        return 0
+
+    lax.fori_loop(0, classes // STEP, step, 0)
+
+
+def first_primal(
+    cost_hbm, x_hbm, weights_ref, ends_ref, after_ref, kt_ref, w_ref, inflow_ref, bound_ref, fac_ref, gamma_ref,
+    x1_hbm, sum_ref, weighted_ref, last_ref, lead_ref, moved_ref, caps_ref, room_ref,
+    cost_ref, x_ref, sems,
+):
+    days, classes = w_ref.shape
+    arrive = block_copies([(cost_hbm, cost_ref), (x_hbm, x_ref)], sems)
+    leave = block_copies([(x_ref, x1_hbm)], sems.at[2:])
+    start_all(arrive)
     own = caps_ref.shape[1] // ends_ref.shape[0]
     for k in range(ends_ref.shape[0]):
         caps_ref[:, k * own : (k + 1) * own] = ends_ref[k, :, :own]
         room_ref[:, k * own : (k + 1) * own] = ends_ref[k, :, own : 2 * own]
     caps = caps_ref[...]
-    for copy in small:
-        copy.wait()
-    weights = tile_of(usage_ref, 8, rows_iota((8, LANES)))
-    weights_ref[...] = weights
-    weights = jnp.concatenate([weights] * (STEP // LANES), axis=1)
-    table = tile_of(table_ref, 16, lanes_iota((8, LANES)))
-    rows = rows_iota((days, STEP))
+    weights = weights_ref[...]
+    rows = rows_iota((days, LANES))
 
     def step(j, moved):
-        at = pl.ds(pl.multiple_of(j * STEP, STEP), STEP)
-        gamma = gamma_of(table, index_ref[:, at])
-        gamma_ref[:, at] = gamma[:1]
-        bound = jnp.where(rows < count_ref[:, at], bound_ref[:, at], 0.0)
-        bound_ref[:, at] = bound
-        w = w_ref[:, at]
-        after = jnp.where(rows == days - 1, after_ref[:, at], pltpu.roll(w, days - 1, 0))
-        moved = primal_rows(
-            at, w - gamma * after, pulled_of(caps, fac_ref[:, at]), F32(ETA), weights, bound,
-            cost_ref, x1_ref, x1_ref, sum_ref, weighted_ref, moved,
-        )
-        last_ref[:, at] = sum_ref[days - 1 :, at]
-        lead_ref[:, at] = w[:1] - ETA * (sum_ref[:1, at] - inflow_ref[:1, at])
-        return moved
-
-    moved = jnp.zeros((8, STEP), F32)
+        moved = list(moved)
+        for u in range(STEP // LANES):
+            at = lanes_of(j, u)
+            bound = bound_ref[:, at]
+            pulled = pulled_of(caps, fac_ref[:, at])
+            kt = kt_ref[:, at]
+            kt = jnp.where(rows == days - 1, kt - gamma_ref[:, at] * after_ref[:, at], kt)
+            sums, weighted = [], []
+            for t in range(days):
+                old = x_ref[t, :, at]
+                grad = cost_ref[t, :, at] - spread(kt, t) - weights * spread(pulled, t)
+                new = jnp.minimum(jnp.maximum(old - ETA * grad, 0.0), bound)
+                x_ref[t, :, at] = new
+                gone = new - old
+                moved[u] = moved[u] + gone * gone
+                extra = new + gone
+                sums.append(extra)
+                weighted.append(weights * extra)
+            sums = row_sums(sums)
+            sum_ref[:, at] = sums
+            weighted_ref[:, at] = row_sums(weighted)
+            last_ref[:, at] = sums[days - 1 :]
+            lead_ref[:, at] = w_ref[:1, at] - ETA * (sums[:1] - inflow_ref[:1, at])
+        return tuple(moved)
+
+    zero = jnp.zeros((8, LANES), F32)
+    moved = (zero,) * (STEP // LANES)
     each = BLOCK // STEP
-    for k, pair in enumerate(large):
-        for copy in pair:
-            copy.wait()
+    for k, block in enumerate(arrive):
+        wait_all(block)
         moved = lax.fori_loop(k * each, (k + 1) * each, step, moved)
-    moved_ref[...] = folded(moved)
+        start_all(leave[k : k + 1])
+    total = moved[0]
+    for part in moved[1:]:
+        total = total + part
+    moved_ref[...] = total
     lead_ref[:, classes:] = jnp.ones((1, LANES), F32)
+    for block in leave:
+        wait_all(block)
 
 
 def first_use(weighted_ref, sum_ref, inflow_ref, gamma_ref, fac_ref, use_ref, moved_ref):
@@ -234,13 +290,11 @@
     )
 
 
-def first_send(use_ref, moved_ref, dual_ref, prior_ref, lead_ref, sum_ref, inflow_ref, gamma_ref, out_ref, edge_ref):
+def first_send(use_ref, moved_ref, dual_ref, prior_ref, sum_ref, inflow_ref, gamma_ref, out_ref):
     days, classes = sum_ref.shape
     total = jnp.zeros((1, PART), F32)
-    more = ETA * jnp.max(lead_ref[:, classes:], axis=1, keepdims=True)
     for k in range(classes // PART):
         at = pl.ds(k * PART, PART)
-        edge_ref[:, at] = lead_ref[:, at] + more * (gamma_ref[:, at] * sum_ref[days - 1 :, at])
         gap = sum_ref[:1, at] - gamma_ref[:, at] * prior_ref[:, at] - inflow_ref[:1, at]
         total = total + gap * gap
     edge = (ETA * ETA) * folded(total)
@@ -270,13 +324,55 @@
         out_ref[k] = both
 
 
-def second_primal(
-    moved_ref, weights_ref, caps_ref, cost_ref, x_ref, w_ref, inflow_ref, bound_ref, fac_ref,
-    gamma_ref, sums_ref, prior_ref, edge_ref,
-    out_hbm, w1_ref, sum_ref, weighted_ref, last_ref, omega_ref,
-    x2_ref, sems,
+def next_duals(
+    w_ref, sum_ref, inflow_ref, gamma_ref, prior_ref, lead_ref, caps_ref, w1_ref, kt_ref, caps_out_ref
 ):
     days, classes = w_ref.shape
+    rows = rows_iota((days, LANES))
+    more = ETA * lead_ref[:, classes:]
+    caps_out_ref[...] = caps_ref[...]
+    for k in range(classes // LANES):
+        at = pl.ds(k * LANES, LANES)
+        gamma = gamma_ref[:, at]
+        sums = sum_ref[:, at]
+        prior = jnp.where(rows == 0, prior_ref[:, at], pltpu.roll(sums, 1, 0))
+        w = w_ref[:, at] - ETA * (sums - gamma * prior - inflow_ref[:, at])
+        w1_ref[:, at] = w
+        edge = lead_ref[:, at] + more * (gamma * sums[days - 1 :])
+        kt_ref[:, at] = w - gamma * jnp.where(rows == days - 1, edge, pltpu.roll(w, days - 1, 0))
+
+
+def next_grad(cost_hbm, weights_ref, caps_ref, kt_ref, fac_ref, grad_ref, sems):
+    days, classes = kt_ref.shape
+    arrive = block_copies([(cost_hbm, grad_ref)], sems)
+    start_all(arrive)
+    caps = caps_ref[...]
+    weights = weights_ref[...]
+
+    def step(j, _):
+        for u in range(STEP // LANES):
+            at = lanes_of(j, u)
+            pulled = pulled_of(caps, fac_ref[:, at])
+            kt = kt_ref[:, at]
+            for t in range(days):
+                grad_ref[t, :, at] = grad_ref[t, :, at] - spread(kt, t) - weights * spread(pulled, t)
+        return 0
+
+    each = BLOCK // STEP
+    for k, block in enumerate(arrive):
+        wait_all(block)
+        lax.fori_loop(k * each, (k + 1) * each, step, 0)
+
+
+def second_primal(
+    x_hbm, moved_ref, weights_ref, grad_ref, bound_ref,
+    x2_hbm, sum_ref, weighted_ref, last_ref, omega_ref,
+    x_ref, sems,
+):
+    days, classes = sum_ref.shape
+    arrive = block_copies([(x_hbm, x_ref)], sems)
+    leave = block_copies([(x_ref, x2_hbm)], sems.at[1:])
+    start_all(arrive)
     total = moved_ref[0]
     for k in range(1, moved_ref.shape[0]):
         total = total + moved_ref[k]
@@ -284,35 +380,34 @@
     dual = jnp.sum(total[1:2], axis=1, keepdims=True)
     omega = jnp.sqrt(jnp.sqrt((dual + EPS) / (primal + EPS)))
     omega_ref[...] = jnp.broadcast_to(omega, omega_ref.shape)
-    tau = jnp.broadcast_to(ETA / omega, (8, STEP))
-    caps = caps_ref[...]
-    weights = jnp.concatenate([weights_ref[...]] * (STEP // LANES), axis=1)
-    rows = rows_iota((days, STEP))
+    tau = jnp.broadcast_to(ETA / omega, (8, LANES))
+    weights = weights_ref[...]
 
     def step(j, _):
-        at = pl.ds(pl.multiple_of(j * STEP, STEP), STEP)
-        gamma = gamma_ref[:, at]
-        sums = sums_ref[:, at]
-        prior = jnp.where(rows == 0, prior_ref[:, at], pltpu.roll(sums, 1, 0))
-        w = w_ref[:, at] - ETA * (sums - gamma * prior - inflow_ref[:, at])
-        w1_ref[:, at] = w
-        after = jnp.where(rows == days - 1, edge_ref[:, at], pltpu.roll(w, days - 1, 0))
-        primal_rows(
-            at, w - gamma * after, pulled_of(caps, fac_ref[:, at]), tau, weights, bound_ref[:, at],
-            cost_ref, x_ref, x2_ref, sum_ref, weighted_ref, None,
-        )
-        last_ref[:, at] = sum_ref[days - 1 :, at]
+        for u in range(STEP // LANES):
+            at = lanes_of(j, u)
+            bound = bound_ref[:, at]
+            sums, weighted = [], []
+            for t in range(days):
+                old = x_ref[t, :, at]
+                new = jnp.minimum(jnp.maximum(old - tau * grad_ref[t, :, at], 0.0), bound)
+                x_ref[t, :, at] = new
+                extra = new + (new - old)
+                sums.append(extra)
+                weighted.append(weights * extra)
+            sums = row_sums(sums)
+            sum_ref[:, at] = sums
+            weighted_ref[:, at] = row_sums(weighted)
+            last_ref[:, at] = sums[days - 1 :]
         return 0
 
-    copies = []
     each = BLOCK // STEP
-    for k in range(classes // BLOCK):
+    for k, block in enumerate(arrive):
+        wait_all(block)
         lax.fori_loop(k * each, (k + 1) * each, step, 0)
-        at = pl.ds(k * BLOCK, BLOCK)
-        copies.append(pltpu.make_async_copy(x2_ref.at[:, :, at], out_hbm.at[:, :, at], sems.at[k]))
-        copies[-1].start()
-    for copy in copies:
-        copy.wait()
+        start_all(leave[k : k + 1])
+    for block in leave:
+        wait_all(block)
 
 
 def second_use(weighted_ref, fac_ref, caps_ref, out_ref):
@@ -372,47 +467,56 @@
     )(*in_hbm(ycap_start, capacity, ybal_start))
     after = to_previous(row)
     ends = lax.all_to_all(ends, "cls", 0, 0)
-    (cost, x1, ybal_start, inflow, bound, fac, sums, weighted, last, lead, gamma, moved, caps, room,
-     weights) = call(
+    field, rows, row, tile = (
+        struct(days, opts, classes), struct(days, classes), struct(1, classes), struct(8, LANES)
+    )
+    table = struct(days, facilities)
+    kt, w, inflow, bound, fac, gamma, weights = call(
+        load, "load",
+        [rows, rows, rows, struct(opts, classes),
+         jax.ShapeDtypeStruct((1, classes), jnp.int32), row, tile],
+        [ANY] * 8,
+        [pltpu.SMEM((opts,), F32), pltpu.SMEM(decay_table.shape, F32), pltpu.VMEM((1, classes), jnp.int32),
+         pltpu.VMEM((1, classes), jnp.int32), pltpu.SemaphoreType.DMA((8,))],
+        cost=PASS,
+    )(*in_hbm(usage, decay_table, ybal_start, inflow, upper, fac, count, index))
+    streams = classes // BLOCK
+    x1, sums, weighted, last, lead, moved, caps, room = call(
         first_primal, "first_primal",
-        [struct(days, opts, classes), struct(days, opts, classes), struct(days, classes),
-         struct(days, classes), struct(opts, classes), jax.ShapeDtypeStruct((1, classes), jnp.int32),
-         struct(days, classes), struct(days, classes), struct(1, classes),
-         struct(1, classes + LANES), struct(1, classes), struct(8, LANES), struct(days, facilities),
-         struct(days, facilities), struct(8, LANES)],
-        [ANY] * 10 + [VM] * 2,
-        [pltpu.SMEM((opts,), F32), pltpu.SMEM(decay_table.shape, F32), pltpu.VMEM((1, classes), jnp.int32),
-         pltpu.VMEM((1, classes), jnp.int32), pltpu.SemaphoreType.DMA((8 + 2 * (classes // BLOCK),))],
-    )(
-        *in_hbm(usage, decay_table, cost, x_start, ybal_start, inflow, upper, fac, count, index), ends, after
-    )
+        [pltpu.HBM(field.shape, F32), rows, rows, row, struct(1, classes + LANES), tile, table, table],
+        [ANY] * 2 + [VM] * 9,
+        [pltpu.VMEM(field.shape, F32), pltpu.VMEM(field.shape, F32), pltpu.SemaphoreType.DMA((3, streams))],
+        limit=8, out_specs=[ANY] + [VM] * 7,
+    )(*in_hbm(cost, x_start), weights, ends, after, kt, w, inflow, bound, fac, gamma)
     prior = to_next(last)
     lead = to_previous(lead)
     use, dual = call(
         first_use, "first_use", [struct(days, facilities), struct(days, LANES)], [VM] * 5,
-        cost=pl.CostEstimate(flops=10_000_000, bytes_accessed=8_000_000, transcendentals=0),
+        cost=PASS,
     )(weighted, sums, inflow, gamma, fac)
-    sent, edge = call(
-        first_send, "first_send", [struct(blocks, 2 * days, facilities), struct(1, classes)], [VM] * 8
-    )(use, moved, dual, prior, lead, sums, inflow, gamma)
+    (sent,) = call(first_send, "first_send", [struct(blocks, 2 * days, facilities)], [VM] * 7)(
+        use, moved, dual, prior, sums, inflow, gamma
+    )
     got = lax.all_to_all(sent, "cls", 0, 0)
+    w1, kt, caps = call(next_duals, "next_duals", [rows, rows, table], [VM] * 7, cost=PASS)(
+        w, sums, inflow, gamma, prior, lead, caps
+    )
     caps1, sent = call(
-        caps_step, "caps_step", [struct(days, facilities), struct(lax.axis_size("day"), days, LANES)],
-        [VM] * 3,
+        caps_step, "caps_step", [table, struct(lax.axis_size("day"), days, LANES)], [VM] * 3
     )(got, caps, room)
     got = lax.all_to_all(sent, "day", 0, 0)
-    x2, w1, sums2, weighted2, last2, omega = call(
-        second_primal, "second_primal",
-        [struct(days, opts, classes), struct(days, classes), struct(days, classes), struct(days, classes),
-         struct(1, classes), struct(8, LANES)],
-        [VM] * 13,
-        [pltpu.VMEM((days, opts, classes), F32), pltpu.SemaphoreType.DMA((classes // BLOCK,))],
-        out_specs=[ANY] + [VM] * 5,
-    )(got, weights, caps1, cost, x1, ybal_start, inflow, bound, fac, gamma, sums, prior, edge)
+    (grad,) = call(
+        next_grad, "next_grad", [field], [ANY] + [VM] * 4, [pltpu.SemaphoreType.DMA((1, streams))], cost=PASS
+    )(*in_hbm(cost), weights, caps1, kt, fac)
+    x2, sums2, weighted2, last2, omega = call(
+        second_primal, "second_primal", [pltpu.HBM(field.shape, F32), rows, rows, row, tile],
+        [ANY] + [VM] * 4, [pltpu.VMEM(field.shape, F32), pltpu.SemaphoreType.DMA((2, streams))],
+        limit=8, out_specs=[ANY] + [VM] * 4,
+    )(*in_hbm(x1), got, weights, grad, bound)
     prior2 = to_next(last2)
     (sent,) = call(
         second_use, "second_use", [struct(blocks, days, LANES)], [VM] * 3,
-        cost=pl.CostEstimate(flops=10_000_000, bytes_accessed=8_000_000, transcendentals=0),
+        cost=PASS,
     )(weighted2, fac, caps1)
     got = lax.all_to_all(sent, "cls", 0, 0)
     w2, caps2 = call(last_duals, "last_duals", [struct(days, classes), struct(days, own)], [VM] * 8)(

time: 83 us -> 77.7 us (0.936)
  blocking collectives: 32.4 us -> 0 us
  starting transfers between devices: 24.8 us -> 39.2 us
  waiting for transfers between devices: 8.63 us -> 18.4 us
  Pallas kernels: 16 us -> 18.7 us
    all_to_all x2 -> x0, blocking collectives: 32.4 us -> none  [the longest x1 19.8 us: local(): got = lax.all_to_all(sent, 'day', 0, 0)]
    all_to_all x0 -> x1, starting transfers between devices: none -> 9.31 us  [local(): got = lax.all_to_all(sent, 'day', 0, 0)]
    all_to_all x0 -> x1, waiting for transfers between devices: none -> 4.91 us  [local(): got = lax.all_to_all(sent, 'day', 0, 0)]
    all_to_all x1 -> x2, starting transfers between devices: 3.34 us -> 8.22 us  [local(): got = lax.all_to_all(sent, 'cls', 0, 0)]
    all_to_all x1 -> x2, waiting for transfers between devices: 3.25 us -> 6.26 us  [local(): got = lax.all_to_all(sent, 'cls', 0, 0)]
    pallas_call x4 -> x7, Pallas kernels: 11.8 us -> 14.6 us  [the longest x1 4.72 us: local(): call(first_primal, 'first_primal', [pltpu.HBM(field.shape, F32), rows, ro...]
    ppermute x2, starting transfers between devices: 5.55 us -> 7.91 us  [to_next(): return lax.ppermute(row, 'day', [(i, i + 1) for i in range(n - 1)])]
    ppermute x2, starting transfers between devices: 6.86 us -> 4.76 us  [to_previous(): return lax.ppermute(row, 'day', [(i + 1, i) for i in range(n - 1)])]
  transfers between devices with their start and end apart: 6 -> 8, of which waited for: 5 -> 8; matrix products, arithmetic and copies ran while one was open for 0% -> 0% of each run, Pallas kernels for 1% -> 8%
where the time goes in v3:
time: 77.7 us; the launch traced here: 77.1 us
  starting transfers between devices  39.2 us (50%)
  Pallas kernels  18.7 us (24%)
  waiting for transfers between devices  18.4 us (24%)
    all_to_all x1, starting transfers between devices, local(): got = lax.all_to_all(sent, 'day', 0, 0)  9.31 us
    all_to_all x1, starting transfers between devices, local(): ends = lax.all_to_all(ends, 'cls', 0, 0)  9.03 us
    all_to_all x2, starting transfers between devices, local(): got = lax.all_to_all(sent, 'cls', 0, 0)  8.22 us
    ppermute x2, starting transfers between devices, to_next(): return lax.ppermute(row, 'day', [(i, i + 1) for i in range(n - 1)])  7.91 us
    all_to_all x2, waiting for transfers between devices, local(): got = lax.all_to_all(sent, 'cls', 0, 0)  6.26 us
    all_to_all x1, waiting for transfers between devices, local(): got = lax.all_to_all(sent, 'day', 0, 0)  4.91 us
    ppermute x2, waiting for transfers between devices, to_previous(): return lax.ppermute(row, 'day', [(i + 1, i) for i in range(n - 1)])  4.87 us
    ppermute x2, starting transfers between devices, to_previous(): return lax.ppermute(row, 'day', [(i + 1, i) for i in range(n - 1)])  4.76 us
  transfers between devices with their start and end apart: 8, of which 8 were waited for; matrix products, arithmetic and copies ran while one was open for 0% of the time, Pallas kernels for 8%

profile of v3, /device:TPU:1, one launch (start us, length us, event | category | flops | bytes accessed | tf_op | source)
XLA Modules:
  0.0 77.1 jit_solution(17555997991706711448)
XLA Ops:
  0.6 1.4 %start.1 = (f32[8,8,128]{2,1,0:T(8,128)}, f32[1,8192]{1,0:T(1,128)S(1)}) custom-call(f32[8,32]{1,0:T(8,128)} %caps_ref.1, f32[8,32]{1,0:T(8,128)} %room_ref.3, f32[8,8192]{1,0:T(8,128)} %w_ref.1), custom_call_target="tpu_custom_call" | custom-call | tf_op jit(solution)/shard_map/start/pallas_call | solution.py:464
  2.1 9.0 %all-to-all-start = ((f32[8,8,128]{2,1,0:T(8,128)}), f32[8,8,128]{2,1,0:T(8,128)S(1)}, u32[]{:S(2)}, u32[]{:S(2)}) async-start(f32[8,8,128]{2,1,0:T(8,128)} %get-tuple-element.35), calls=%async_computation | async-start | bytes 65536 | tf_op jit(solution)/shard_map/all_to_all | solution.py:469
  11.1 2.9 %collective-permute-start = (f32[1,8192]{1,0:T(1,128)S(1)}, f32[1,8192]{1,0:T(1,128)S(1)}, u32[]{:S(2)}, u32[]{:S(2)}) collective-permute-start(f32[1,8192]{1,0:T(1,128)S(1)} %get-tuple-element.36), channel_id=1, source_target_pairs={{8,0},{16,8},{24,16},{32,24},{40,32},{48,40},{56,48},{64,56},{72,6... | collective-permute-start | bytes 98312 | tf_op jit(solution)/shard_map/ppermute | solution.py:449
  14.0 2.5 %load.1 = (f32[8,8192]{1,0:T(8,128)S(1)}, f32[8,8192]{1,0:T(8,128)S(1)}, f32[8,8192]{1,0:T(8,128)S(1)}, f32[8,8192]{1,0:T(8,128)S(1)}, s32[1,8192]{1,0:T(1,128)S...) custom-call(f32[8]{0:T(128)} %usage_hbm.1, f32[16]{0:T(128)} %table_hbm.1, f32[8,8192]{1,0:T(8,128)} %w_ref.1, ...), custom_call_target="tpu_custom_call" | custom-call | flops 10000000 | bytes 8000000 | tf_op jit(solution)/shard_map/load/pallas_call | solution.py:474
  16.5 0.4 collective-permute-done.after_ref
  16.9 1.0 %all-to-all-done.ends_ref = f32[8,8,128]{2,1,0:T(8,128)S(1)} async-done(((f32[8,8,128]{2,1,0:T(8,128)}), f32[8,8,128]{2,1,0:T(8,128)S(1)}, u32[]{:S(2)}, u32[]{:S(2)}) %all-to-all-start) | async-done | bytes 32800 | tf_op jit(solution)/shard_map/all_to_all | solution.py:469
  18.0 4.7 %first_primal.1 = (f32[8,8,8192]{2,1,0:T(8,128)}, f32[8,8192]{1,0:T(8,128)S(1)}, f32[8,8192]{1,0:T(8,128)S(1)}, f32[1,8192]{1,0:T(1,128)S(1)}, f32[1,8320]{1,0:T...) custom-call(f32[8,8,8192]{2,1,0:T(8,128)} %cost_hbm.3, f32[8,8,8192]{2,1,0:T(8,128)} %x_hbm.1, ...), custom_call_target="tpu_custom_call" | custom-call | tf_op jit(solution)/shard_map/first_primal/pallas_call | solution.py:484
  22.7 5.1 %collective-permute-start.1 = (f32[1,8192]{1,0:T(1,128)S(1)}, f32[1,8192]{1,0:T(1,128)S(1)}, u32[]{:S(2)}, u32[]{:S(2)}) collective-permute-start(f32[1,8192]{1,0:T(1,128)S(1)} %get-tuple-element.49), channel_id=1, source_target_pairs={{0,8},{8,16},{16,24},{24,32},{32,40},{40,48},{48,56},{56,64},{64,7... | collective-permute-start | bytes 98312 | tf_op jit(solution)/shard_map/ppermute | solution.py:444
  27.8 0.6 first_use.1
  28.5 0.4 collective-permute-done.1.prior_ref
  28.8 0.7 first_send.1
  29.5 3.4 %all-to-all-start.1 = ((f32[8,16,256]{2,1,0:T(8,128)}), f32[8,16,256]{2,1,0:T(8,128)S(1)}, u32[]{:S(2)}, u32[]{:S(2)}) async-start(f32[8,16,256]{2,1,0:T(8,128)} %first_send.1), calls=%async_computation.1 | async-start | bytes 262144 | tf_op jit(solution)/shard_map/all_to_all | solution.py:500
  32.9 1.9 %collective-permute-start.2 = (f32[1,8320]{1,0:T(1,128)S(1)}, f32[1,8320]{1,0:T(1,128)S(1)}, u32[]{:S(2)}, u32[]{:S(2)}) collective-permute-start(f32[1,8320]{1,0:T(1,128)S(1)} %get-tuple-element.50), channel_id=1, source_target_pairs={{8,0},{16,8},{24,16},{32,24},{40,32},{48,40},{56,48},{64,56},{72,6... | collective-permute-start | bytes 99848 | tf_op jit(solution)/shard_map/ppermute | solution.py:449
  34.8 4.4 %collective-permute-done.2.lead_ref = f32[1,8320]{1,0:T(1,128)S(1)} collective-permute-done((f32[1,8320]{1,0:T(1,128)S(1)}, f32[1,8320]{1,0:T(1,128)S(1)}, u32[]{:S(2)}, u32[]{:S(2)}) %collective-permute-start.2) | collective-permute-done | bytes 33312 | tf_op jit(solution)/shard_map/ppermute | solution.py:449
  39.3 0.2 next_duals.1
  39.4 3.1 %all-to-all-done.1.in_ref = f32[8,16,256]{2,1,0:T(8,128)S(1)} async-done(((f32[8,16,256]{2,1,0:T(8,128)}), f32[8,16,256]{2,1,0:T(8,128)S(1)}, u32[]{:S(2)}, u32[]{:S(2)}) %all-to-all-start.1) | async-done | bytes 131104 | tf_op jit(solution)/shard_map/all_to_all | solution.py:500
  42.5 0.7 caps_step.1
  43.2 9.3 %all-to-all-start.2 = ((f32[32,8,128]{2,1,0:T(8,128)}), f32[32,8,128]{2,1,0:T(8,128)S(1)}, u32[]{:S(2)}, u32[]{:S(2)}) async-start(f32[32,8,128]{2,1,0:T(8,128)} %get-tuple-element.54), calls=%async_computation.2 | async-start | bytes 262144 | tf_op jit(solution)/shard_map/all_to_all | solution.py:507
  52.5 2.7 %next_grad.1.grad_ref = f32[8,8,8192]{2,1,0:T(8,128)S(1)} custom-call(f32[8,8,8192]{2,1,0:T(8,128)} %cost_hbm.3, f32[8,128]{1,0:T(8,128)S(1)} %get-tuple-element.34.weights_ref, f32[8,256]{1,0:T(8,128)S(1)} %get-tuple-element.55.caps_ref, f32[8,8192]{1,0:T(8,128)S(1)} %get-tuple-element.56.kt_ref, s32[1,8192]{1,0:T(1,128)S(1)} %get-tuple-element.41.fac_ref), custom_call_target="tpu_custom_call" | custom-call | flops 10000000 | bytes 8000000 | tf_op jit(solution)/shard_map/next_grad/pallas_call | solution.py:508
  55.3 4.9 %all-to-all-done.2.moved_ref = f32[32,8,128]{2,1,0:T(8,128)S(1)} async-done(((f32[32,8,128]{2,1,0:T(8,128)}), f32[32,8,128]{2,1,0:T(8,128)S(1)}, u32[]{:S(2)}, u32[]{:S(2)}) %all-to-all-start.2) | async-done | bytes 131104 | tf_op jit(solution)/shard_map/all_to_all | solution.py:507
  60.2 0.0 copy-start
  60.2 3.0 %second_primal.1 = (f32[8,8,8192]{2,1,0:T(8,128)}, f32[8,8192]{1,0:T(8,128)S(1)}, f32[8,8192]{1,0:T(8,128)S(1)}, f32[1,8192]{1,0:T(1,128)S(1)}, f32[8,128]{1,0:T(8,128)S(1)}) custom-call(f32[8,8,8192]{2,1,0:T(8,128)} %get-tuple-element.43.x_hbm, f32[32,8,128]{2,1,0:T(8,128)S(1)} %all-to-all-done.2.moved_ref, f32[8,128]{1,0:T(8,128)S(1)} %get-tuple-element.34.weights_ref, ...), custom_call_target="tpu_custom_call" | custom-call | tf_op jit(solution)/shard_map/second_primal/pallas_call | solution.py:511
  63.2 1.3 %second_use.1 = f32[8,8,128]{2,1,0:T(8,128)} custom-call(f32[8,8192]{1,0:T(8,128)S(1)} %get-tuple-element.58.weighted_ref, s32[1,8192]{1,0:T(1,128)S(1)} %get-tuple-element.41.fac_ref, f32[8,256]{1,0:T(8,128)S(1)} %get-tuple-element.55.caps_ref), custom_call_target="tpu_custom_call" | custom-call | flops 10000000 | bytes 8000000 | tf_op jit(solution)/shard_map/second_use/pallas_call | solution.py:517
  64.5 4.8 %all-to-all-start.3 = ((f32[8,8,128]{2,1,0:T(8,128)}), f32[8,8,128]{2,1,0:T(8,128)S(1)}, u32[]{:S(2)}, u32[]{:S(2)}) async-start(f32[8,8,128]{2,1,0:T(8,128)} %second_use.1), calls=%async_computation.3 | async-start | bytes 65536 | tf_op jit(solution)/shard_map/all_to_all | solution.py:521
  69.3 2.8 %collective-permute-start.3 = (f32[1,8192]{1,0:T(1,128)S(1)}, f32[1,8192]{1,0:T(1,128)S(1)}, u32[]{:S(2)}, u32[]{:S(2)}) collective-permute-start(f32[1,8192]{1,0:T(1,128)S(1)} %get-tuple-element.62), channel_id=1, source_target_pairs={{0,8},{8,16},{16,24},{24,32},{32,40},{40,48},{48,56},{56,64},{64,7... | collective-permute-start | bytes 98312 | tf_op jit(solution)/shard_map/ppermute | solution.py:444
  72.1 1.0 %collective-permute-done.3.prior_ref = f32[1,8192]{1,0:T(1,128)S(1)} collective-permute-done((f32[1,8192]{1,0:T(1,128)S(1)}, f32[1,8192]{1,0:T(1,128)S(1)}, u32[]{:S(2)}, u32[]{:S(2)}) %collective-permute-start.3) | collective-permute-done | bytes 32800 | tf_op jit(solution)/shard_map/ppermute | solution.py:444
  73.1 3.2 %all-to-all-done.3.in_ref = f32[8,8,128]{2,1,0:T(8,128)S(1)} async-done(((f32[8,8,128]{2,1,0:T(8,128)}), f32[8,8,128]{2,1,0:T(8,128)S(1)}, u32[]{:S(2)}, u32[]{:S(2)}) %all-to-all-start.3) | async-done | bytes 32800 | tf_op jit(solution)/shard_map/all_to_all | solution.py:521
  76.3 0.0 copy-done
  76.3 0.9 %last_duals.1 = (f32[8,8192]{1,0:T(8,128)}, f32[8,32]{1,0:T(8,128)}) custom-call(f32[8,8,128]{2,1,0:T(8,128)S(1)} %all-to-all-done.3.in_ref, f32[8,32]{1,0:T(8,128)S(1)} %copy-done, f32[8,128]{1,0:T(8,128)S(1)} %get-tuple-element.59.omega_ref, f32[8,8192]{1,0:T(8,128)S(1)} %get-tuple-element.60.w_ref, f32[8,8192]{1,0:T(8,128)S(1)} %get-tuple-element.61.sum_ref, ...), custom_call_target="tpu_custom_call" | custom-call | tf_op jit(solution)/shard_map/last_duals/pallas_call | solution.py:522
Async XLA Ops:
  2.1 15.9 %all-to-all-start = ((f32[8,8,128]{2,1,0:T(8,128)}), f32[8,8,128]{2,1,0:T(8,128)S(1)}, u32[]{:S(2)}, u32[]{:S(2)}) async-start(f32[8,8,128]{2,1,0:T(8,128)} %get-tuple-element.35), calls=%async_computation | async-start | bytes 65536 | tf_op jit(solution)/shard_map/all_to_all | solution.py:469
  11.1 5.8 %collective-permute-start = (f32[1,8192]{1,0:T(1,128)S(1)}, f32[1,8192]{1,0:T(1,128)S(1)}, u32[]{:S(2)}, u32[]{:S(2)}) collective-permute-start(f32[1,8192]{1,0:T(1,128)S(1)} %get-tuple-element.36), channel_id=1, source_target_pairs={{8,0},{16,8},{24,16},{32,24},{40,32},{48,40},{56,48},{64,56},{72,6... | collective-permute-start | bytes 98312 | tf_op jit(solution)/shard_map/ppermute | solution.py:449
  22.7 6.1 %collective-permute-start.1 = (f32[1,8192]{1,0:T(1,128)S(1)}, f32[1,8192]{1,0:T(1,128)S(1)}, u32[]{:S(2)}, u32[]{:S(2)}) collective-permute-start(f32[1,8192]{1,0:T(1,128)S(1)} %get-tuple-element.49), channel_id=1, source_target_pairs={{0,8},{8,16},{16,24},{24,32},{32,40},{40,48},{48,56},{56,64},{64,7... | collective-permute-start | bytes 98312 | tf_op jit(solution)/shard_map/ppermute | solution.py:444
  29.5 13.0 %all-to-all-start.1 = ((f32[8,16,256]{2,1,0:T(8,128)}), f32[8,16,256]{2,1,0:T(8,128)S(1)}, u32[]{:S(2)}, u32[]{:S(2)}) async-start(f32[8,16,256]{2,1,0:T(8,128)} %first_send.1), calls=%async_computation.1 | async-start | bytes 262144 | tf_op jit(solution)/shard_map/all_to_all | solution.py:500
  32.9 6.4 %collective-permute-start.2 = (f32[1,8320]{1,0:T(1,128)S(1)}, f32[1,8320]{1,0:T(1,128)S(1)}, u32[]{:S(2)}, u32[]{:S(2)}) collective-permute-start(f32[1,8320]{1,0:T(1,128)S(1)} %get-tuple-element.50), channel_id=1, source_target_pairs={{8,0},{16,8},{24,16},{32,24},{40,32},{48,40},{56,48},{64,56},{72,6... | collective-permute-start | bytes 99848 | tf_op jit(solution)/shard_map/ppermute | solution.py:449
  43.2 16.9 %all-to-all-start.2 = ((f32[32,8,128]{2,1,0:T(8,128)}), f32[32,8,128]{2,1,0:T(8,128)S(1)}, u32[]{:S(2)}, u32[]{:S(2)}) async-start(f32[32,8,128]{2,1,0:T(8,128)} %get-tuple-element.54), calls=%async_computation.2 | async-start | bytes 262144 | tf_op jit(solution)/shard_map/all_to_all | solution.py:507
  60.2 16.1 %copy-start = (f32[8,32]{1,0:T(8,128)S(1)}, f32[8,32]{1,0:T(8,128)}, u32[]{:S(2)}) copy-start(f32[8,32]{1,0:T(8,128)} %room_ref.3) | copy-start | bytes 3076
  64.5 11.8 %all-to-all-start.3 = ((f32[8,8,128]{2,1,0:T(8,128)}), f32[8,8,128]{2,1,0:T(8,128)S(1)}, u32[]{:S(2)}, u32[]{:S(2)}) async-start(f32[8,8,128]{2,1,0:T(8,128)} %second_use.1), calls=%async_computation.3 | async-start | bytes 65536 | tf_op jit(solution)/shard_map/all_to_all | solution.py:521
  69.3 3.8 %collective-permute-start.3 = (f32[1,8192]{1,0:T(1,128)S(1)}, f32[1,8192]{1,0:T(1,128)S(1)}, u32[]{:S(2)}, u32[]{:S(2)}) collective-permute-start(f32[1,8192]{1,0:T(1,128)S(1)} %get-tuple-element.62), channel_id=1, source_target_pairs={{0,8},{8,16},{16,24},{24,32},{32,40},{40,48},{48,56},{56,64},{64,7... | collective-permute-start | bytes 98312 | tf_op jit(solution)/shard_map/ppermute | solution.py:444

commit v4 on v3

--- a/solution.py
+++ b/solution.py
@@ -87,38 +87,26 @@
     return jnp.concatenate(parts, axis=1)
 
 
-def facility_sums(weighted_ref, facility_ref, facilities):
-    days, classes = weighted_ref.shape
-    groups = facilities // WIDE
-    total = jnp.zeros((groups * 3 * days, WIDE), F32)
-    for k in range(classes // PART):
-        at = pl.ds(k * PART, PART)
-        w = weighted_ref[:, at]
-        fac = facility_ref[:, at]
-        top = w.astype(jnp.bfloat16).astype(F32)
-        rest = w - top
-        mid = rest.astype(jnp.bfloat16).astype(F32)
-        low = rest - mid
-        group = jnp.broadcast_to(fac // WIDE, (days, PART))
-        rows = []
-        for g in range(groups):
-            mine = group == g
-            rows += [jnp.where(mine, top, 0.0), jnp.where(mine, mid, 0.0), jnp.where(mine, low, 0.0)]
-        left = jnp.concatenate(rows, axis=0).astype(jnp.bfloat16)
-        within = jnp.broadcast_to(jnp.bitwise_and(fac, WIDE - 1), (WIDE, PART))
-        member = jnp.where(within == rows_iota((WIDE, PART)), 1.0, 0.0).astype(jnp.bfloat16)
-        total = total + lax.dot_general(
-            left, member, (((1,), (1,)), ((), ())), preferred_element_type=F32
-        )
-    out = []
+def facility_part(weighted, facility, groups):
+    days, classes = weighted.shape
+    top = weighted.astype(jnp.bfloat16).astype(F32)
+    rest = weighted - top
+    mid = rest.astype(jnp.bfloat16).astype(F32)
+    low = rest - mid
+    group = jnp.broadcast_to(facility // WIDE, (days, classes))
+    rows = []
     for g in range(groups):
-        base = g * 3 * days
-        out.append(
-            total[base : base + days]
-            + total[base + days : base + 2 * days]
-            + total[base + 2 * days : base + 3 * days]
-        )
-    return out
+        mine = group == g
+        rows += [jnp.where(mine, top, 0.0), jnp.where(mine, mid, 0.0), jnp.where(mine, low, 0.0)]
+    left = jnp.concatenate(rows, axis=0).astype(jnp.bfloat16)
+    within = jnp.broadcast_to(jnp.bitwise_and(facility, WIDE - 1), (WIDE, classes))
+    member = jnp.where(within == rows_iota((WIDE, classes)), 1.0, 0.0).astype(jnp.bfloat16)
+    return lax.dot_general(left, member, (((1,), (1,)), ((), ())), preferred_element_type=F32)
+
+
+def facility_groups(total, days):
+    parts = [total[k : k + days] for k in range(0, total.shape[0], days)]
+    return [parts[k] + parts[k + 1] + parts[k + 2] for k in range(0, len(parts), 3)]
 
 
 def combined(a, b, mask, distance):
@@ -217,8 +205,8 @@
 
 def first_primal(
     cost_hbm, x_hbm, weights_ref, ends_ref, after_ref, kt_ref, w_ref, inflow_ref, bound_ref, fac_ref, gamma_ref,
-    x1_hbm, sum_ref, weighted_ref, last_ref, lead_ref, moved_ref, caps_ref, room_ref,
-    cost_ref, x_ref, sems,
+    x1_hbm, sum_ref, edge_ref, moved_ref, dual_ref, use_ref, caps_ref, room_ref,
+    cost_ref, x_ref, weighted_ref, sems,
 ):
     days, classes = w_ref.shape
     arrive = block_copies([(cost_hbm, cost_ref), (x_hbm, x_ref)], sems)
@@ -232,8 +220,8 @@
     weights = weights_ref[...]
     rows = rows_iota((days, LANES))
 
-    def step(j, moved):
-        moved = list(moved)
+    def step(j, carry):
+        moved, dual = [list(part) for part in carry]
         for u in range(STEP // LANES):
             at = lanes_of(j, u)
             bound = bound_ref[:, at]
@@ -254,48 +242,48 @@
             sums = row_sums(sums)
             sum_ref[:, at] = sums
             weighted_ref[:, at] = row_sums(weighted)
-            last_ref[:, at] = sums[days - 1 :]
-            lead_ref[:, at] = w_ref[:1, at] - ETA * (sums[:1] - inflow_ref[:1, at])
-        return tuple(moved)
+            inflow = inflow_ref[:, at]
+            edge_ref[:1, at] = sums[days - 1 :]
+            edge_ref[1:, at] = w_ref[:1, at] - ETA * (sums[:1] - inflow[:1])
+            gap = sums - gamma_ref[:, at] * pltpu.roll(sums, 1, 0) - inflow
+            dual[u] = dual[u] + gap * gap
+        return tuple(moved), tuple(dual)
 
     zero = jnp.zeros((8, LANES), F32)
-    moved = (zero,) * (STEP // LANES)
+    carry = ((zero,) * (STEP // LANES),) * 2
     each = BLOCK // STEP
+    groups = caps_ref.shape[1] // WIDE
+    total = jnp.zeros((groups * 3 * days, WIDE), F32)
     for k, block in enumerate(arrive):
         wait_all(block)
-        moved = lax.fori_loop(k * each, (k + 1) * each, step, moved)
+        carry = lax.fori_loop(k * each, (k + 1) * each, step, carry)
         start_all(leave[k : k + 1])
-    total = moved[0]
-    for part in moved[1:]:
-        total = total + part
-    moved_ref[...] = total
-    lead_ref[:, classes:] = jnp.ones((1, LANES), F32)
+        at = pl.ds(k * BLOCK, BLOCK)
+        total = total + facility_part(weighted_ref[:, at], fac_ref[:, at], groups)
+    moved, dual = [sum(part[1:], part[0]) for part in carry]
+    moved_ref[...] = moved
+    dual_ref[...] = jnp.where(rows > 0, (ETA * ETA) * dual, 0.0)
+    for g, part in enumerate(facility_groups(total, days)):
+        use_ref[:, g * WIDE : (g + 1) * WIDE] = part
     for block in leave:
         wait_all(block)
 
 
-def first_use(weighted_ref, sum_ref, inflow_ref, gamma_ref, fac_ref, use_ref, moved_ref):
+def second_core():
+    return lax.rem(lax.axis_index("day"), 2) == 1
+
+
+def first_send(
+    use_ref, moved_ref, dual_ref, chip_ref, far_ref, sum_ref, inflow_ref, gamma_ref, out_ref, prior_ref
+):
     days, classes = sum_ref.shape
-    parts = facility_sums(weighted_ref, fac_ref, use_ref.shape[1])
-    for g, part in enumerate(parts):
-        use_ref[:, g * WIDE : (g + 1) * WIDE] = part
-    total = jnp.zeros((days, PART), F32)
-    for k in range(classes // PART):
-        at = pl.ds(k * PART, PART)
-        sums = sum_ref[:, at]
-        gap = sums - gamma_ref[:, at] * pltpu.roll(sums, 1, 0) - inflow_ref[:, at]
-        total = total + gap * gap
-    moved_ref[...] = jnp.where(
-        rows_iota((days, LANES)) > 0, (ETA * ETA) * folded(total), 0.0
-    )
-
-
-def first_send(use_ref, moved_ref, dual_ref, prior_ref, sum_ref, inflow_ref, gamma_ref, out_ref):
-    days, classes = sum_ref.shape
+    second = second_core()
     total = jnp.zeros((1, PART), F32)
     for k in range(classes // PART):
         at = pl.ds(k * PART, PART)
-        gap = sum_ref[:1, at] - gamma_ref[:, at] * prior_ref[:, at] - inflow_ref[:1, at]
+        prior = jnp.where(second, chip_ref[:1, at], far_ref[:1, at])
+        prior_ref[:, at] = prior
+        gap = sum_ref[:1, at] - gamma_ref[:, at] * prior - inflow_ref[:1, at]
         total = total + gap * gap
     edge = (ETA * ETA) * folded(total)
     dual = dual_ref[...] + jnp.where(rows_iota((days, LANES)) == 0, edge, 0.0)
@@ -318,19 +306,16 @@
     gone = new - caps
     primal = jnp.sum(total[days:, :LANES], axis=0, keepdims=True)
     dual = jnp.sum(total[days:, LANES:] + folded(gone * gone), axis=0, keepdims=True)
-    rows = rows_iota((days, LANES))
-    both = jnp.where(rows == 0, primal, jnp.where(rows == 1, dual, 0.0))
     for k in range(out_ref.shape[0]):
-        out_ref[k] = both
-
-
-def next_duals(
-    w_ref, sum_ref, inflow_ref, gamma_ref, prior_ref, lead_ref, caps_ref, w1_ref, kt_ref, caps_out_ref
-):
+        out_ref[k, :, :LANES] = primal
+        out_ref[k, :, LANES:] = dual
+
+
+def next_duals(w_ref, sum_ref, inflow_ref, gamma_ref, prior_ref, chip_ref, far_ref, w1_ref, kt_ref):
     days, classes = w_ref.shape
     rows = rows_iota((days, LANES))
-    more = ETA * lead_ref[:, classes:]
-    caps_out_ref[...] = caps_ref[...]
+    second = second_core()
+    more = jnp.where(lax.axis_index("day") == lax.axis_size("day") - 1, F32(0.0), F32(ETA))
     for k in range(classes // LANES):
         at = pl.ds(k * LANES, LANES)
         gamma = gamma_ref[:, at]
@@ -338,7 +323,8 @@
         prior = jnp.where(rows == 0, prior_ref[:, at], pltpu.roll(sums, 1, 0))
         w = w_ref[:, at] - ETA * (sums - gamma * prior - inflow_ref[:, at])
         w1_ref[:, at] = w
-        edge = lead_ref[:, at] + more * (gamma * sums[days - 1 :])
+        lead = jnp.where(second, far_ref[1:, at], chip_ref[1:, at])
+        edge = lead + more * (gamma * sums[days - 1 :])
         kt_ref[:, at] = w - gamma * jnp.where(rows == days - 1, edge, pltpu.roll(w, days - 1, 0))
 
 
@@ -365,9 +351,9 @@
 
 
 def second_primal(
-    x_hbm, moved_ref, weights_ref, grad_ref, bound_ref,
-    x2_hbm, sum_ref, weighted_ref, last_ref, omega_ref,
-    x_ref, sems,
+    x_hbm, moved_ref, weights_ref, grad_ref, bound_ref, fac_ref, caps_ref,
+    x2_hbm, sum_ref, last_ref, omega_ref, out_ref,
+    x_ref, weighted_ref, sems,
 ):
     days, classes = sum_ref.shape
     arrive = block_copies([(x_hbm, x_ref)], sems)
@@ -376,8 +362,8 @@
     total = moved_ref[0]
     for k in range(1, moved_ref.shape[0]):
         total = total + moved_ref[k]
-    primal = jnp.sum(total[0:1], axis=1, keepdims=True)
-    dual = jnp.sum(total[1:2], axis=1, keepdims=True)
+    primal = jnp.sum(total[:, :LANES], axis=1, keepdims=True)
+    dual = jnp.sum(total[:, LANES:], axis=1, keepdims=True)
     omega = jnp.sqrt(jnp.sqrt((dual + EPS) / (primal + EPS)))
     omega_ref[...] = jnp.broadcast_to(omega, omega_ref.shape)
     tau = jnp.broadcast_to(ETA / omega, (8, LANES))
@@ -402,23 +388,23 @@
         return 0
 
     each = BLOCK // STEP
+    groups = caps_ref.shape[1] // WIDE
+    total = jnp.zeros((groups * 3 * days, WIDE), F32)
     for k, block in enumerate(arrive):
         wait_all(block)
         lax.fori_loop(k * each, (k + 1) * each, step, 0)
         start_all(leave[k : k + 1])
-    for block in leave:
-        wait_all(block)
-
-
-def second_use(weighted_ref, fac_ref, caps_ref, out_ref):
-    days = weighted_ref.shape[0]
-    parts = facility_sums(weighted_ref, fac_ref, caps_ref.shape[1])
+        at = pl.ds(k * BLOCK, BLOCK)
+        total = total + facility_part(weighted_ref[:, at], fac_ref[:, at], groups)
+    parts = facility_groups(total, days)
     own = caps_ref.shape[1] // out_ref.shape[0]
     out_ref[...] = jnp.zeros(out_ref.shape, F32)
     for k in range(out_ref.shape[0]):
         g, place = divmod(k * own, WIDE)
         out_ref[k, :, :own] = parts[g][:, place : place + own]
         out_ref[k, :, own : 2 * own] = caps_ref[:, k * own : (k + 1) * own]
+    for block in leave:
+        wait_all(block)
 
 
 def last_duals(in_ref, room_ref, omega_ref, w_ref, sum_ref, prior_ref, inflow_ref, gamma_ref, w2_ref, caps2_ref):
@@ -447,6 +433,12 @@
 def to_previous(row):
     n = lax.axis_size("day")
     return lax.ppermute(row, "day", [(i + 1, i) for i in range(n - 1)])
+
+
+def swapped(rows, first):
+    n = lax.axis_size("day")
+    pairs = [(i, i + 1) for i in range(first, n - 1, 2)]
+    return lax.ppermute(rows, "day", pairs + [(j, i) for i, j in pairs])
 
 
 def local(
@@ -481,43 +473,38 @@
         cost=PASS,
     )(*in_hbm(usage, decay_table, ybal_start, inflow, upper, fac, count, index))
     streams = classes // BLOCK
-    x1, sums, weighted, last, lead, moved, caps, room = call(
+    x1, sums, edge, moved, dual, use, caps, room = call(
         first_primal, "first_primal",
-        [pltpu.HBM(field.shape, F32), rows, rows, row, struct(1, classes + LANES), tile, table, table],
+        [pltpu.HBM(field.shape, F32), rows, struct(2, classes), tile, tile, table, table, table],
         [ANY] * 2 + [VM] * 9,
-        [pltpu.VMEM(field.shape, F32), pltpu.VMEM(field.shape, F32), pltpu.SemaphoreType.DMA((3, streams))],
+        [pltpu.VMEM(field.shape, F32), pltpu.VMEM(field.shape, F32), pltpu.VMEM(rows.shape, F32),
+         pltpu.SemaphoreType.DMA((3, streams))],
         limit=8, out_specs=[ANY] + [VM] * 7,
     )(*in_hbm(cost, x_start), weights, ends, after, kt, w, inflow, bound, fac, gamma)
-    prior = to_next(last)
-    lead = to_previous(lead)
-    use, dual = call(
-        first_use, "first_use", [struct(days, facilities), struct(days, LANES)], [VM] * 5,
-        cost=PASS,
-    )(weighted, sums, inflow, gamma, fac)
-    (sent,) = call(first_send, "first_send", [struct(blocks, 2 * days, facilities)], [VM] * 7)(
-        use, moved, dual, prior, sums, inflow, gamma
+    chip = swapped(edge, 0)
+    far = swapped(edge, 1)
+    sent, prior = call(
+        first_send, "first_send", [struct(blocks, 2 * days, facilities), row], [VM] * 8
+    )(use, moved, dual, chip, far, sums, inflow, gamma)
+    got = lax.all_to_all(sent, "cls", 0, 0)
+    caps1, sent = call(
+        caps_step, "caps_step", [table, struct(lax.axis_size("day"), 1, 2 * LANES)], [VM] * 3
+    )(got, caps, room)
+    w1, kt = call(next_duals, "next_duals", [rows, rows], [VM] * 7, cost=PASS)(
+        w, sums, inflow, gamma, prior, chip, far
     )
-    got = lax.all_to_all(sent, "cls", 0, 0)
-    w1, kt, caps = call(next_duals, "next_duals", [rows, rows, table], [VM] * 7, cost=PASS)(
-        w, sums, inflow, gamma, prior, lead, caps
-    )
-    caps1, sent = call(
-        caps_step, "caps_step", [table, struct(lax.axis_size("day"), days, LANES)], [VM] * 3
-    )(got, caps, room)
     got = lax.all_to_all(sent, "day", 0, 0)
     (grad,) = call(
         next_grad, "next_grad", [field], [ANY] + [VM] * 4, [pltpu.SemaphoreType.DMA((1, streams))], cost=PASS
     )(*in_hbm(cost), weights, caps1, kt, fac)
-    x2, sums2, weighted2, last2, omega = call(
-        second_primal, "second_primal", [pltpu.HBM(field.shape, F32), rows, rows, row, tile],
-        [ANY] + [VM] * 4, [pltpu.VMEM(field.shape, F32), pltpu.SemaphoreType.DMA((2, streams))],
+    x2, sums2, last2, omega, sent = call(
+        second_primal, "second_primal",
+        [pltpu.HBM(field.shape, F32), rows, row, tile, struct(blocks, days, LANES)],
+        [ANY] + [VM] * 6,
+        [pltpu.VMEM(field.shape, F32), pltpu.VMEM(rows.shape, F32), pltpu.SemaphoreType.DMA((2, streams))],
         limit=8, out_specs=[ANY] + [VM] * 4,
-    )(*in_hbm(x1), got, weights, grad, bound)
+    )(*in_hbm(x1), got, weights, grad, bound, fac, caps1)
     prior2 = to_next(last2)
-    (sent,) = call(
-        second_use, "second_use", [struct(blocks, days, LANES)], [VM] * 3,
-        cost=PASS,
-    )(weighted2, fac, caps1)
     got = lax.all_to_all(sent, "cls", 0, 0)
     w2, caps2 = call(last_duals, "last_duals", [struct(days, classes), struct(days, own)], [VM] * 8)(
         got, capacity, omega, w1, sums2, prior2, inflow, gamma

time: 77.7 us -> 78.4 us (level)
  blocking collectives: 0 us -> 12.8 us
  starting transfers between devices: 39.2 us -> 32.5 us
  waiting for transfers between devices: 18.4 us -> 11.9 us
  Pallas kernels: 18.7 us -> 19.9 us
    all_to_all x0 -> x1, blocking collectives: none -> 12.8 us  [local(): got = lax.all_to_all(sent, 'cls', 0, 0)]
    ppermute x2 -> x1, starting transfers between devices: 7.91 us -> 2.49 us  [to_next(): return lax.ppermute(row, 'day', [(i, i + 1) for i in range(n - 1)])]
    ppermute x0 -> x2, starting transfers between devices: none -> 5.21 us  [swapped(): return lax.ppermute(rows, 'day', pairs + [(j, i) for i, j in pairs])]
    all_to_all x2 -> x1, starting transfers between devices: 8.22 us -> 3.35 us  [local(): got = lax.all_to_all(sent, 'cls', 0, 0)]
    ppermute x2 -> x1, waiting for transfers between devices: 4.87 us -> 0.43 us  [to_previous(): return lax.ppermute(row, 'day', [(i + 1, i) for i in range(n - 1)])]
    all_to_all x2 -> x1, waiting for transfers between devices: 6.26 us -> 3.29 us  [local(): got = lax.all_to_all(sent, 'cls', 0, 0)]
    pallas_call x1, Pallas kernels: 3.03 us -> 5.16 us  [local(): call(second_primal, 'second_primal', [pltpu.HBM(field.shape, F32), rows,...]
    ppermute x2 -> x1, starting transfers between devices: 4.76 us -> 2.85 us  [to_previous(): return lax.ppermute(row, 'day', [(i + 1, i) for i in range(n - 1)])]
  transfers between devices with their start and end apart: 8 -> 7, of which waited for: 8 -> 6; matrix products, arithmetic and copies ran while one was open for 0% -> 0% of each run, Pallas kernels for 8% -> 7%
where the time goes in v4:
time: 78.4 us; the launch traced here: 77.9 us
  starting transfers between devices  32.5 us (41%)
  Pallas kernels  19.9 us (25%)
  blocking collectives  12.8 us (16%)
  waiting for transfers between devices  11.9 us (15%)
    all_to_all x1, blocking collectives, local(): got = lax.all_to_all(sent, 'cls', 0, 0)  12.8 us
    all_to_all x1, starting transfers between devices, local(): got = lax.all_to_all(sent, 'day', 0, 0)  9.56 us
    all_to_all x1, starting transfers between devices, local(): ends = lax.all_to_all(ends, 'cls', 0, 0)  9.03 us
    pallas_call x1, Pallas kernels, local(): call(first_primal, 'first_primal', [pltpu.HBM(field.shape, F32), rows, st...  6.33 us
    ppermute x2, starting transfers between devices, swapped(): return lax.ppermute(rows, 'day', pairs + [(j, i) for i, j in pairs])  5.21 us
    pallas_call x1, Pallas kernels, local(): call(second_primal, 'second_primal', [pltpu.HBM(field.shape, F32), rows,...  5.16 us
    all_to_all x1, waiting for transfers between devices, local(): got = lax.all_to_all(sent, 'day', 0, 0)  4.33 us
    all_to_all x1, starting transfers between devices, local(): got = lax.all_to_all(sent, 'cls', 0, 0)  3.35 us
  transfers between devices with their start and end apart: 7, of which 6 were waited for; matrix products, arithmetic and copies ran while one was open for 0% of the time, Pallas kernels for 7%

profile of v4, /device:TPU:1, one launch (start us, length us, event | category | flops | bytes accessed | tf_op | source)
XLA Modules:
  0.0 77.9 jit_solution(10331767357513736956)
XLA Ops:
  0.6 1.4 %start.1 = (f32[8,8,128]{2,1,0:T(8,128)}, f32[1,8192]{1,0:T(1,128)S(1)}) custom-call(f32[8,32]{1,0:T(8,128)} %caps_ref.1, f32[8,32]{1,0:T(8,128)} %room_ref.3, f32[8,8192]{1,0:T(8,128)} %w_ref.1), custom_call_target="tpu_custom_call" | custom-call | tf_op jit(solution)/shard_map/start/pallas_call | solution.py:456
  2.1 9.0 %all-to-all-start = ((f32[8,8,128]{2,1,0:T(8,128)}), f32[8,8,128]{2,1,0:T(8,128)S(1)}, u32[]{:S(2)}, u32[]{:S(2)}) async-start(f32[8,8,128]{2,1,0:T(8,128)} %get-tuple-element.34), calls=%async_computation | async-start | bytes 65536 | tf_op jit(solution)/shard_map/all_to_all | solution.py:461
  11.1 2.9 %collective-permute-start = (f32[1,8192]{1,0:T(1,128)S(1)}, f32[1,8192]{1,0:T(1,128)S(1)}, u32[]{:S(2)}, u32[]{:S(2)}) collective-permute-start(f32[1,8192]{1,0:T(1,128)S(1)} %get-tuple-element.35), channel_id=1, source_target_pairs={{8,0},{16,8},{24,16},{32,24},{40,32},{48,40},{56,48},{64,56},{72,6... | collective-permute-start | bytes 98312 | tf_op jit(solution)/shard_map/ppermute | solution.py:435
  14.0 2.5 %load.1 = (f32[8,8192]{1,0:T(8,128)S(1)}, f32[8,8192]{1,0:T(8,128)S(1)}, f32[8,8192]{1,0:T(8,128)S(1)}, f32[8,8192]{1,0:T(8,128)S(1)}, s32[1,8192]{1,0:T(1,128)S...) custom-call(f32[8]{0:T(128)} %usage_hbm.1, f32[16]{0:T(128)} %table_hbm.1, f32[8,8192]{1,0:T(8,128)} %w_ref.1, ...), custom_call_target="tpu_custom_call" | custom-call | flops 10000000 | bytes 8000000 | tf_op jit(solution)/shard_map/load/pallas_call | solution.py:466
  16.5 0.4 collective-permute-done.after_ref
  16.9 1.0 %all-to-all-done.ends_ref = f32[8,8,128]{2,1,0:T(8,128)S(1)} async-done(((f32[8,8,128]{2,1,0:T(8,128)}), f32[8,8,128]{2,1,0:T(8,128)S(1)}, u32[]{:S(2)}, u32[]{:S(2)}) %all-to-all-start) | async-done | bytes 32800 | tf_op jit(solution)/shard_map/all_to_all | solution.py:461
  18.0 6.3 %first_primal.1 = (f32[8,8,8192]{2,1,0:T(8,128)}, f32[8,8192]{1,0:T(8,128)S(1)}, f32[2,8192]{1,0:T(2,128)S(1)}, f32[8,128]{1,0:T(8,128)S(1)}, f32[8,128]{1,0:T(8...) custom-call(f32[8,8,8192]{2,1,0:T(8,128)} %cost_hbm.3, f32[8,8,8192]{2,1,0:T(8,128)} %x_hbm.1, ...), custom_call_target="tpu_custom_call" | custom-call | tf_op jit(solution)/shard_map/first_primal/pallas_call | solution.py:476
  24.3 5.1 %collective-permute-start.2 = (f32[2,8192]{1,0:T(2,128)S(1)}, f32[2,8192]{1,0:T(2,128)S(1)}, u32[]{:S(2)}, u32[]{:S(2)}) collective-permute-start(f32[2,8192]{1,0:T(2,128)S(1)} %get-tuple-element.46), channel_id=1, source_target_pairs={{8,16},{24,32},{40,48},{56,64},{72,80},{88,96},{104,112},{120,128}... | collective-permute-start | bytes 196616 | tf_op jit(solution)/shard_map/ppermute | solution.py:441
  29.4 0.1 collective-permute-start.1
  29.5 1.8 %collective-permute-done.2.far_ref = f32[2,8192]{1,0:T(2,128)S(1)} collective-permute-done((f32[2,8192]{1,0:T(2,128)S(1)}, f32[2,8192]{1,0:T(2,128)S(1)}, u32[]{:S(2)}, u32[]{:S(2)}) %collective-permute-start.2) | collective-permute-done | bytes 65568 | tf_op jit(solution)/shard_map/ppermute | solution.py:441
  31.4 0.0 collective-permute-done.1.chip_ref
  31.4 12.8 %all_to_all.20.in_ref = f32[8,16,256]{2,1,0:T(8,128)S(1)} all-to-all(f32[8,16,256]{2,1,0:T(8,128)S(1)} %get-tuple-element.48), channel_id=1, replica_groups=mesh['day'=32,'cls'=8] {'cls'}, dimensions={0} | all-to-all | bytes 262144 | tf_op jit(solution)/shard_map/all_to_all | solution.py:489
  44.3 0.6 caps_step.1
  44.9 9.6 %all-to-all-start.2 = ((f32[32,1,256]{2,1,0:T(1,128)}), f32[32,1,256]{2,1,0:T(1,128)S(1)}, u32[]{:S(2)}, u32[]{:S(2)}) async-start(f32[32,1,256]{2,1,0:T(1,128)} %get-tuple-element.51), calls=%async_computation.2 | async-start | bytes 65536 | tf_op jit(solution)/shard_map/all_to_all | solution.py:496
  54.5 0.2 next_duals.1
  54.7 2.7 %next_grad.1.grad_ref = f32[8,8,8192]{2,1,0:T(8,128)S(1)} custom-call(f32[8,8,8192]{2,1,0:T(8,128)} %cost_hbm.3, f32[8,128]{1,0:T(8,128)S(1)} %get-tuple-element.33.weights_ref, f32[8,256]{1,0:T(8,128)S(1)} %get-tuple-element.52.caps_ref, f32[8,8192]{1,0:T(8,128)S(1)} %get-tuple-element.54.kt_ref, s32[1,8192]{1,0:T(1,128)S(1)} %get-tuple-element.40.fac_ref), custom_call_target="tpu_custom_call" | custom-call | flops 10000000 | bytes 8000000 | tf_op jit(solution)/shard_map/next_grad/pallas_call | solution.py:497
  57.4 4.3 %all-to-all-done.2.moved_ref = f32[32,1,256]{2,1,0:T(1,128)S(1)} async-done(((f32[32,1,256]{2,1,0:T(1,128)}), f32[32,1,256]{2,1,0:T(1,128)S(1)}, u32[]{:S(2)}, u32[]{:S(2)}) %all-to-all-start.2) | async-done | bytes 32800 | tf_op jit(solution)/shard_map/all_to_all | solution.py:496
  61.7 0.0 copy-start
  61.7 5.2 %second_primal.1 = (f32[8,8,8192]{2,1,0:T(8,128)}, f32[8,8192]{1,0:T(8,128)S(1)}, f32[1,8192]{1,0:T(1,128)S(1)}, f32[8,128]{1,0:T(8,128)S(1)}, f32[8,8,128]{2,1,0:T(8,128)}) custom-call(f32[8,8,8192]{2,1,0:T(8,128)} %get-tuple-element.42.x_hbm, f32[32,1,256]{2,1,0:T(1,128)S(1)} %all-to-all-done.2.moved_ref, f32[8,128]{1,0:T(8,128)S(1)} %get-tuple-element.33.weights_ref, ...), custom_call_target="tpu_custom_call" | custom-call | tf_op jit(solution)/shard_map/second_primal/pallas_call | solution.py:500
  66.9 3.4 %all-to-all-start.3 = ((f32[8,8,128]{2,1,0:T(8,128)}), f32[8,8,128]{2,1,0:T(8,128)S(1)}, u32[]{:S(2)}, u32[]{:S(2)}) async-start(f32[8,8,128]{2,1,0:T(8,128)} %get-tuple-element.56), calls=%async_computation.3 | async-start | bytes 65536 | tf_op jit(solution)/shard_map/all_to_all | solution.py:508
  70.3 2.5 %collective-permute-start.3 = (f32[1,8192]{1,0:T(1,128)S(1)}, f32[1,8192]{1,0:T(1,128)S(1)}, u32[]{:S(2)}, u32[]{:S(2)}) collective-permute-start(f32[1,8192]{1,0:T(1,128)S(1)} %get-tuple-element.60), channel_id=1, source_target_pairs={{0,8},{8,16},{16,24},{24,32},{32,40},{40,48},{48,56},{56,64},{64,7... | collective-permute-start | bytes 98312 | tf_op jit(solution)/shard_map/ppermute | solution.py:430
  72.8 1.0 %collective-permute-done.3.prior_ref = f32[1,8192]{1,0:T(1,128)S(1)} collective-permute-done((f32[1,8192]{1,0:T(1,128)S(1)}, f32[1,8192]{1,0:T(1,128)S(1)}, u32[]{:S(2)}, u32[]{:S(2)}) %collective-permute-start.3) | collective-permute-done | bytes 32800 | tf_op jit(solution)/shard_map/ppermute | solution.py:430
  73.8 3.3 %all-to-all-done.3.in_ref = f32[8,8,128]{2,1,0:T(8,128)S(1)} async-done(((f32[8,8,128]{2,1,0:T(8,128)}), f32[8,8,128]{2,1,0:T(8,128)S(1)}, u32[]{:S(2)}, u32[]{:S(2)}) %all-to-all-start.3) | async-done | bytes 32800 | tf_op jit(solution)/shard_map/all_to_all | solution.py:508
  77.1 0.0 copy-done
  77.1 0.9 %last_duals.1 = (f32[8,8192]{1,0:T(8,128)}, f32[8,32]{1,0:T(8,128)}) custom-call(f32[8,8,128]{2,1,0:T(8,128)S(1)} %all-to-all-done.3.in_ref, f32[8,32]{1,0:T(8,128)S(1)} %copy-done, f32[8,128]{1,0:T(8,128)S(1)} %get-tuple-element.57.omega_ref, f32[8,8192]{1,0:T(8,128)S(1)} %get-tuple-element.58.w_ref, f32[8,8192]{1,0:T(8,128)S(1)} %get-tuple-element.59.sum_ref, ...), custom_call_target="tpu_custom_call" | custom-call | tf_op jit(solution)/shard_map/last_duals/pallas_call | solution.py:509
  (1 shorter events, 0.0 us)
Async XLA Ops:
  2.1 15.9 %all-to-all-start = ((f32[8,8,128]{2,1,0:T(8,128)}), f32[8,8,128]{2,1,0:T(8,128)S(1)}, u32[]{:S(2)}, u32[]{:S(2)}) async-start(f32[8,8,128]{2,1,0:T(8,128)} %get-tuple-element.34), calls=%async_computation | async-start | bytes 65536 | tf_op jit(solution)/shard_map/all_to_all | solution.py:461
  11.1 5.8 %collective-permute-start = (f32[1,8192]{1,0:T(1,128)S(1)}, f32[1,8192]{1,0:T(1,128)S(1)}, u32[]{:S(2)}, u32[]{:S(2)}) collective-permute-start(f32[1,8192]{1,0:T(1,128)S(1)} %get-tuple-element.35), channel_id=1, source_target_pairs={{8,0},{16,8},{24,16},{32,24},{40,32},{48,40},{56,48},{64,56},{72,6... | collective-permute-start | bytes 98312 | tf_op jit(solution)/shard_map/ppermute | solution.py:435
  24.3 7.1 %collective-permute-start.2 = (f32[2,8192]{1,0:T(2,128)S(1)}, f32[2,8192]{1,0:T(2,128)S(1)}, u32[]{:S(2)}, u32[]{:S(2)}) collective-permute-start(f32[2,8192]{1,0:T(2,128)S(1)} %get-tuple-element.46), channel_id=1, source_target_pairs={{8,16},{24,32},{40,48},{56,64},{72,80},{88,96},{104,112},{120,128}... | collective-permute-start | bytes 196616 | tf_op jit(solution)/shard_map/ppermute | solution.py:441
  29.4 1.9 %collective-permute-start.1 = (f32[2,8192]{1,0:T(2,128)S(1)}, f32[2,8192]{1,0:T(2,128)S(1)}, u32[]{:S(2)}, u32[]{:S(2)}) collective-permute-start(f32[2,8192]{1,0:T(2,128)S(1)} %get-tuple-element.46), channel_id=1, source_target_pairs={{0,8},{16,24},{32,40},{48,56},{64,72},{80,88},{96,104},{112,120},{... | collective-permute-start | bytes 196616 | tf_op jit(solution)/shard_map/ppermute | solution.py:441
  44.9 16.8 %all-to-all-start.2 = ((f32[32,1,256]{2,1,0:T(1,128)}), f32[32,1,256]{2,1,0:T(1,128)S(1)}, u32[]{:S(2)}, u32[]{:S(2)}) async-start(f32[32,1,256]{2,1,0:T(1,128)} %get-tuple-element.51), calls=%async_computation.2 | async-start | bytes 65536 | tf_op jit(solution)/shard_map/all_to_all | solution.py:496
  61.7 15.3 %copy-start = (f32[8,32]{1,0:T(8,128)S(1)}, f32[8,32]{1,0:T(8,128)}, u32[]{:S(2)}) copy-start(f32[8,32]{1,0:T(8,128)} %room_ref.3) | copy-start | bytes 3076
  66.9 10.2 %all-to-all-start.3 = ((f32[8,8,128]{2,1,0:T(8,128)}), f32[8,8,128]{2,1,0:T(8,128)S(1)}, u32[]{:S(2)}, u32[]{:S(2)}) async-start(f32[8,8,128]{2,1,0:T(8,128)} %get-tuple-element.56), calls=%async_computation.3 | async-start | bytes 65536 | tf_op jit(solution)/shard_map/all_to_all | solution.py:508
  70.3 3.5 %collective-permute-start.3 = (f32[1,8192]{1,0:T(1,128)S(1)}, f32[1,8192]{1,0:T(1,128)S(1)}, u32[]{:S(2)}, u32[]{:S(2)}) collective-permute-start(f32[1,8192]{1,0:T(1,128)S(1)} %get-tuple-element.60), channel_id=1, source_target_pairs={{0,8},{8,16},{16,24},{24,32},{32,40},{40,48},{48,56},{56,64},{64,7... | collective-permute-start | bytes 98312 | tf_op jit(solution)/shard_map/ppermute | solution.py:430

commit v5 on v4

--- a/solution.py
+++ b/solution.py
@@ -1,3 +1,5 @@
+import functools
+
 import jax
 import jax.numpy as jnp
 from jax import lax
@@ -8,9 +10,10 @@
 ETA = 0.3
 EPS = 1e-6
 LANES = 128
-STEP = 512
+STEP = 1024
 PART = 1024
 BLOCK = 1024
+HEAD = 2048
 WIDE = 64
 
 VM = pl.BlockSpec(memory_space=pltpu.VMEM)
@@ -119,10 +122,6 @@
         mask = jnp.bitwise_and(rows, distance) == 0
         tiles = [combined(tiles[k], tiles[k + 1], mask, distance) for k in range(0, len(tiles), 2)]
     return tiles[0]
-
-
-def spread(tile, row):
-    return jnp.broadcast_to(tile[row : row + 1], tile.shape)
 
 
 def start(caps_ref, room_ref, w_ref, out_ref, row_ref, caps, room, sems):
@@ -147,7 +146,7 @@
     return pl.ds(pl.multiple_of(j * STEP, STEP) + u * LANES, LANES)
 
 
-def block_copies(pairs, sems):
+def block_copies(pairs, sems, first=0):
     classes = pairs[0][0].shape[2]
     return [
         [
@@ -156,7 +155,7 @@
             )
             for n, (a, b) in enumerate(pairs)
         ]
-        for k in range(classes // BLOCK)
+        for k in range(first, classes // BLOCK)
     ]
 
 
@@ -172,8 +171,8 @@
 
 
 def load(
-    usage_hbm, table_hbm, w_hbm, inflow_hbm, upper_hbm, fac_hbm, count_hbm, index_hbm,
-    kt_ref, w_ref, inflow_ref, bound_ref, fac_ref, gamma_ref, weights_ref,
+    usage_hbm, table_hbm, w_hbm, inflow_hbm, upper_hbm, fac_hbm, count_hbm, index_hbm, cost_hbm, x_hbm,
+    cost_ref, x_ref, kt_ref, w_ref, inflow_ref, bound_ref, fac_ref, gamma_ref, weights_ref,
     usage_ref, table_ref, count_ref, index_ref, sems,
 ):
     days, classes = w_ref.shape
@@ -182,7 +181,12 @@
         (index_hbm, index_ref), (w_hbm, w_ref), (inflow_hbm, inflow_ref), (upper_hbm, bound_ref),
     ]
     small = [pltpu.make_async_copy(a, b, sems.at[k]) for k, (a, b) in enumerate(small)]
-    for copy in small:
+    head = pl.ds(0, HEAD)
+    large = [
+        pltpu.make_async_copy(a.at[:, :, head], b, sems.at[len(small) + k])
+        for k, (a, b) in enumerate(((cost_hbm, cost_ref), (x_hbm, x_ref)))
+    ]
+    for copy in small + large:
         copy.start()
     for copy in small:
         copy.wait()
@@ -201,15 +205,17 @@
         return 0
 
     lax.fori_loop(0, classes // STEP, step, 0)
+    wait_all(large)
 
 
 def first_primal(
-    cost_hbm, x_hbm, weights_ref, ends_ref, after_ref, kt_ref, w_ref, inflow_ref, bound_ref, fac_ref, gamma_ref,
-    x1_hbm, sum_ref, edge_ref, moved_ref, dual_ref, use_ref, caps_ref, room_ref,
-    cost_ref, x_ref, weighted_ref, sems,
+    cost_hbm, x_hbm, cost_head, x_head, weights_ref, ends_ref, after_ref, kt_ref, w_ref, inflow_ref, bound_ref, fac_ref, gamma_ref,
+    x1_hbm, sum_ref, weighted_ref, chip_ref, far_ref, moved_ref, caps_ref, room_ref,
+    cost_ref, x_ref, sems,
 ):
     days, classes = w_ref.shape
-    arrive = block_copies([(cost_hbm, cost_ref), (x_hbm, x_ref)], sems)
+    ready = HEAD // BLOCK
+    arrive = block_copies([(cost_hbm, cost_ref), (x_hbm, x_ref)], sems, ready)
     leave = block_copies([(x_ref, x1_hbm)], sems.at[2:])
     start_all(arrive)
     own = caps_ref.shape[1] // ends_ref.shape[0]
@@ -217,56 +223,73 @@
         caps_ref[:, k * own : (k + 1) * own] = ends_ref[k, :, :own]
         room_ref[:, k * own : (k + 1) * own] = ends_ref[k, :, own : 2 * own]
     caps = caps_ref[...]
+    for k in range(classes // LANES):
+        at = pl.ds(k * LANES, LANES)
+        sum_ref[:, at] = pulled_of(caps, fac_ref[:, at])
     weights = weights_ref[...]
-    rows = rows_iota((days, LANES))
-
-    def step(j, carry):
-        moved, dual = [list(part) for part in carry]
+    second = second_core()
+
+    def step(cost_at, x_at, j, moved):
+        moved = list(moved)
         for u in range(STEP // LANES):
             at = lanes_of(j, u)
             bound = bound_ref[:, at]
-            pulled = pulled_of(caps, fac_ref[:, at])
-            kt = kt_ref[:, at]
-            kt = jnp.where(rows == days - 1, kt - gamma_ref[:, at] * after_ref[:, at], kt)
+            late = kt_ref[days - 1 :, at] - gamma_ref[:, at] * after_ref[:, at]
             sums, weighted = [], []
             for t in range(days):
-                old = x_ref[t, :, at]
-                grad = cost_ref[t, :, at] - spread(kt, t) - weights * spread(pulled, t)
+                old = x_at[t, :, at]
+                kt = late if t == days - 1 else kt_ref[t : t + 1, at]
+                grad = cost_at[t, :, at] - kt - weights * sum_ref[t : t + 1, at]
                 new = jnp.minimum(jnp.maximum(old - ETA * grad, 0.0), bound)
                 x_ref[t, :, at] = new
                 gone = new - old
-                moved[u] = moved[u] + gone * gone
+                moved[u % 2] = moved[u % 2] + gone * gone
                 extra = new + gone
                 sums.append(extra)
                 weighted.append(weights * extra)
             sums = row_sums(sums)
             sum_ref[:, at] = sums
             weighted_ref[:, at] = row_sums(weighted)
-            inflow = inflow_ref[:, at]
-            edge_ref[:1, at] = sums[days - 1 :]
-            edge_ref[1:, at] = w_ref[:1, at] - ETA * (sums[:1] - inflow[:1])
-            gap = sums - gamma_ref[:, at] * pltpu.roll(sums, 1, 0) - inflow
-            dual[u] = dual[u] + gap * gap
-        return tuple(moved), tuple(dual)
-
-    zero = jnp.zeros((8, LANES), F32)
-    carry = ((zero,) * (STEP // LANES),) * 2
+            last = sums[days - 1 :]
+            lead = w_ref[:1, at] - ETA * (sums[:1] - inflow_ref[:1, at])
+            chip_ref[:, at] = jnp.where(second, lead, last)
+            far_ref[:, at] = jnp.where(second, last, lead)
+        return tuple(moved)
+
+    moved = (jnp.zeros((8, LANES), F32),) * 2
     each = BLOCK // STEP
-    groups = caps_ref.shape[1] // WIDE
-    total = jnp.zeros((groups * 3 * days, WIDE), F32)
-    for k, block in enumerate(arrive):
-        wait_all(block)
-        carry = lax.fori_loop(k * each, (k + 1) * each, step, carry)
+    for k in range(len(leave)):
+        if k >= ready:
+            wait_all(arrive[k - ready])
+        source = (cost_ref, x_ref) if k >= ready else (cost_head, x_head)
+        moved = lax.fori_loop(k * each, (k + 1) * each, functools.partial(step, *source), moved)
         start_all(leave[k : k + 1])
-        at = pl.ds(k * BLOCK, BLOCK)
-        total = total + facility_part(weighted_ref[:, at], fac_ref[:, at], groups)
-    moved, dual = [sum(part[1:], part[0]) for part in carry]
-    moved_ref[...] = moved
-    dual_ref[...] = jnp.where(rows > 0, (ETA * ETA) * dual, 0.0)
-    for g, part in enumerate(facility_groups(total, days)):
-        use_ref[:, g * WIDE : (g + 1) * WIDE] = part
+    moved_ref[...] = moved[0] + moved[1]
     for block in leave:
         wait_all(block)
+
+
+def facility_sums(weighted_ref, fac_ref, facilities):
+    days, classes = weighted_ref.shape
+    groups = facilities // WIDE
+    total = jnp.zeros((groups * 3 * days, WIDE), F32)
+    for k in range(classes // PART):
+        at = pl.ds(k * PART, PART)
+        total = total + facility_part(weighted_ref[:, at], fac_ref[:, at], groups)
+    return facility_groups(total, days)
+
+
+def first_use(weighted_ref, sum_ref, inflow_ref, gamma_ref, fac_ref, use_ref, dual_ref):
+    days, classes = sum_ref.shape
+    for g, part in enumerate(facility_sums(weighted_ref, fac_ref, use_ref.shape[1])):
+        use_ref[:, g * WIDE : (g + 1) * WIDE] = part
+    total = jnp.zeros((days, PART), F32)
+    for k in range(classes // PART):
+        at = pl.ds(k * PART, PART)
+        sums = sum_ref[:, at]
+        gap = sums - gamma_ref[:, at] * pltpu.roll(sums, 1, 0) - inflow_ref[:, at]
+        total = total + gap * gap
+    dual_ref[...] = jnp.where(rows_iota((days, LANES)) > 0, (ETA * ETA) * folded(total), 0.0)
 
 
 def second_core():
@@ -281,7 +304,7 @@
     total = jnp.zeros((1, PART), F32)
     for k in range(classes // PART):
         at = pl.ds(k * PART, PART)
-        prior = jnp.where(second, chip_ref[:1, at], far_ref[:1, at])
+        prior = jnp.where(second, chip_ref[:, at], far_ref[:, at])
         prior_ref[:, at] = prior
         gap = sum_ref[:1, at] - gamma_ref[:, at] * prior - inflow_ref[:1, at]
         total = total + gap * gap
@@ -323,7 +346,7 @@
         prior = jnp.where(rows == 0, prior_ref[:, at], pltpu.roll(sums, 1, 0))
         w = w_ref[:, at] - ETA * (sums - gamma * prior - inflow_ref[:, at])
         w1_ref[:, at] = w
-        lead = jnp.where(second, far_ref[1:, at], chip_ref[1:, at])
+        lead = jnp.where(second, far_ref[:, at], chip_ref[:, at])
         edge = lead + more * (gamma * sums[days - 1 :])
         kt_ref[:, at] = w - gamma * jnp.where(rows == days - 1, edge, pltpu.roll(w, days - 1, 0))
 
@@ -339,9 +362,8 @@
         for u in range(STEP // LANES):
             at = lanes_of(j, u)
             pulled = pulled_of(caps, fac_ref[:, at])
-            kt = kt_ref[:, at]
             for t in range(days):
-                grad_ref[t, :, at] = grad_ref[t, :, at] - spread(kt, t) - weights * spread(pulled, t)
+                grad_ref[t, :, at] = grad_ref[t, :, at] - kt_ref[t : t + 1, at] - weights * pulled[t : t + 1]
         return 0
 
     each = BLOCK // STEP
@@ -388,15 +410,11 @@
         return 0
 
     each = BLOCK // STEP
-    groups = caps_ref.shape[1] // WIDE
-    total = jnp.zeros((groups * 3 * days, WIDE), F32)
     for k, block in enumerate(arrive):
         wait_all(block)
         lax.fori_loop(k * each, (k + 1) * each, step, 0)
         start_all(leave[k : k + 1])
-        at = pl.ds(k * BLOCK, BLOCK)
-        total = total + facility_part(weighted_ref[:, at], fac_ref[:, at], groups)
-    parts = facility_groups(total, days)
+    parts = facility_sums(weighted_ref, fac_ref, caps_ref.shape[1])
     own = caps_ref.shape[1] // out_ref.shape[0]
     out_ref[...] = jnp.zeros(out_ref.shape, F32)
     for k in range(out_ref.shape[0]):
@@ -463,26 +481,29 @@
         struct(days, opts, classes), struct(days, classes), struct(1, classes), struct(8, LANES)
     )
     table = struct(days, facilities)
-    kt, w, inflow, bound, fac, gamma, weights = call(
+    head = struct(days, opts, HEAD)
+    cost_head, x_head, kt, w, inflow, bound, fac, gamma, weights = call(
         load, "load",
-        [rows, rows, rows, struct(opts, classes),
+        [head, head, rows, rows, rows, struct(opts, classes),
          jax.ShapeDtypeStruct((1, classes), jnp.int32), row, tile],
-        [ANY] * 8,
+        [ANY] * 10,
         [pltpu.SMEM((opts,), F32), pltpu.SMEM(decay_table.shape, F32), pltpu.VMEM((1, classes), jnp.int32),
-         pltpu.VMEM((1, classes), jnp.int32), pltpu.SemaphoreType.DMA((8,))],
+         pltpu.VMEM((1, classes), jnp.int32), pltpu.SemaphoreType.DMA((10,))],
         cost=PASS,
-    )(*in_hbm(usage, decay_table, ybal_start, inflow, upper, fac, count, index))
+    )(*in_hbm(usage, decay_table, ybal_start, inflow, upper, fac, count, index, cost, x_start))
     streams = classes // BLOCK
-    x1, sums, edge, moved, dual, use, caps, room = call(
+    x1, sums, weighted, chip, far, moved, caps, room = call(
         first_primal, "first_primal",
-        [pltpu.HBM(field.shape, F32), rows, struct(2, classes), tile, tile, table, table, table],
-        [ANY] * 2 + [VM] * 9,
-        [pltpu.VMEM(field.shape, F32), pltpu.VMEM(field.shape, F32), pltpu.VMEM(rows.shape, F32),
-         pltpu.SemaphoreType.DMA((3, streams))],
+        [pltpu.HBM(field.shape, F32), rows, rows, row, row, tile, table, table],
+        [ANY] * 2 + [VM] * 11,
+        [pltpu.VMEM(field.shape, F32), pltpu.VMEM(field.shape, F32), pltpu.SemaphoreType.DMA((3, streams))],
         limit=8, out_specs=[ANY] + [VM] * 7,
-    )(*in_hbm(cost, x_start), weights, ends, after, kt, w, inflow, bound, fac, gamma)
-    chip = swapped(edge, 0)
-    far = swapped(edge, 1)
+    )(*in_hbm(cost, x_start), cost_head, x_head, weights, ends, after, kt, w, inflow, bound, fac, gamma)
+    chip = swapped(chip, 0)
+    far = swapped(far, 1)
+    use, dual = call(first_use, "first_use", [table, tile], [VM] * 5, cost=PASS)(
+        weighted, sums, inflow, gamma, fac
+    )
     sent, prior = call(
         first_send, "first_send", [struct(blocks, 2 * days, facilities), row], [VM] * 8
     )(use, moved, dual, chip, far, sums, inflow, gamma)

time: 78.4 us -> 74.4 us (0.949)
  Pallas kernels: 19.9 us -> 15 us
  blocking collectives: 12.8 us -> 11.2 us
  starting transfers between devices: 32.5 us -> 34 us
  waiting for transfers between devices: 11.9 us -> 12.9 us
    pallas_call x2 -> x3, Pallas kernels: 8.87 us -> 5.91 us  [the longest x1 3.25 us: local(): call(first_primal, 'first_primal', [pltpu.HBM(field.shape, F32), rows, ro...]
    all_to_all x1, blocking collectives: 12.8 us -> 11.2 us  [local(): got = lax.all_to_all(sent, 'cls', 0, 0)]
    all_to_all x1, starting transfers between devices: 9.56 us -> 11.1 us  [local(): got = lax.all_to_all(sent, 'day', 0, 0)]
    pallas_call x1, Pallas kernels: 5.16 us -> 3.93 us  [local(): call(second_primal, 'second_primal', [pltpu.HBM(field.shape, F32), rows,...]
where the time goes in v5:
time: 74.4 us; the launch traced here: 73.9 us
  starting transfers between devices  34 us (46%)
  Pallas kernels  15 us (20%)
  waiting for transfers between devices  12.9 us (17%)
  blocking collectives  11.2 us (15%)
    all_to_all x1, blocking collectives, local(): got = lax.all_to_all(sent, 'cls', 0, 0)  11.2 us
    all_to_all x1, starting transfers between devices, local(): got = lax.all_to_all(sent, 'day', 0, 0)  11.1 us
    all_to_all x1, starting transfers between devices, local(): ends = lax.all_to_all(ends, 'cls', 0, 0)  9.03 us
    ppermute x2, starting transfers between devices, swapped(): return lax.ppermute(rows, 'day', pairs + [(j, i) for i, j in pairs])  5.21 us
    all_to_all x1, waiting for transfers between devices, local(): got = lax.all_to_all(sent, 'day', 0, 0)  5.06 us
    pallas_call x1, Pallas kernels, local(): call(second_primal, 'second_primal', [pltpu.HBM(field.shape, F32), rows,...  3.93 us
    all_to_all x1, starting transfers between devices, local(): got = lax.all_to_all(sent, 'cls', 0, 0)  3.35 us
    all_to_all x1, waiting for transfers between devices, local(): got = lax.all_to_all(sent, 'cls', 0, 0)  3.29 us
  transfers between devices with their start and end apart: 7, of which 6 were waited for; matrix products, arithmetic and copies ran while one was open for 0% of the time, Pallas kernels for 7%

profile of v5, /device:TPU:1, one launch (start us, length us, event | category | flops | bytes accessed | tf_op | source)
XLA Modules:
  0.0 73.9 jit_solution(8486406362680991066)
XLA Ops:
  0.6 1.4 %start.1 = (f32[8,8,128]{2,1,0:T(8,128)}, f32[1,8192]{1,0:T(1,128)S(1)}) custom-call(f32[8,32]{1,0:T(8,128)} %caps_ref.1, f32[8,32]{1,0:T(8,128)} %room_ref.3, f32[8,8192]{1,0:T(8,128)} %w_ref.1), custom_call_target="tpu_custom_call" | custom-call | tf_op jit(solution)/shard_map/start/pallas_call | solution.py:474
  2.1 9.0 %all-to-all-start = ((f32[8,8,128]{2,1,0:T(8,128)}), f32[8,8,128]{2,1,0:T(8,128)S(1)}, u32[]{:S(2)}, u32[]{:S(2)}) async-start(f32[8,8,128]{2,1,0:T(8,128)} %get-tuple-element.40), calls=%async_computation | async-start | bytes 65536 | tf_op jit(solution)/shard_map/all_to_all | solution.py:479
  11.1 2.9 %collective-permute-start = (f32[1,8192]{1,0:T(1,128)S(1)}, f32[1,8192]{1,0:T(1,128)S(1)}, u32[]{:S(2)}, u32[]{:S(2)}) collective-permute-start(f32[1,8192]{1,0:T(1,128)S(1)} %get-tuple-element.41), channel_id=1, source_target_pairs={{8,0},{16,8},{24,16},{32,24},{40,32},{48,40},{56,48},{64,56},{72,6... | collective-permute-start | bytes 98312 | tf_op jit(solution)/shard_map/ppermute | solution.py:453
  14.0 2.0 %load.1 = (f32[8,8,2048]{2,1,0:T(8,128)S(1)}, f32[8,8,2048]{2,1,0:T(8,128)S(1)}, f32[8,8192]{1,0:T(8,128)S(1)}, f32[8,8192]{1,0:T(8,128)S(1)}, f32[8,8192]{1,0:T...) custom-call(f32[8]{0:T(128)} %usage_hbm.1, ...), custom_call_target="tpu_custom_call" | custom-call | flops 10000000 | bytes 8000000 | tf_op jit(solution)/shard_map/load/pallas_call | solution.py:485
  16.0 0.9 %collective-permute-done.after_ref = f32[1,8192]{1,0:T(1,128)S(1)} collective-permute-done((f32[1,8192]{1,0:T(1,128)S(1)}, f32[1,8192]{1,0:T(1,128)S(1)}, u32[]{:S(2)}, u32[]{:S(2)}) %collective-permute-start) | collective-permute-done | bytes 32800 | tf_op jit(solution)/shard_map/ppermute | solution.py:453
  16.9 1.0 %all-to-all-done.ends_ref = f32[8,8,128]{2,1,0:T(8,128)S(1)} async-done(((f32[8,8,128]{2,1,0:T(8,128)}), f32[8,8,128]{2,1,0:T(8,128)S(1)}, u32[]{:S(2)}, u32[]{:S(2)}) %all-to-all-start) | async-done | bytes 32800 | tf_op jit(solution)/shard_map/all_to_all | solution.py:479
  18.0 3.2 %first_primal.1 = (f32[8,8,8192]{2,1,0:T(8,128)}, f32[8,8192]{1,0:T(8,128)S(1)}, f32[8,8192]{1,0:T(8,128)S(1)}, f32[1,8192]{1,0:T(1,128)S(1)}, f32[1,8192]{1,0:T...) custom-call(f32[8,8,8192]{2,1,0:T(8,128)} %cost_hbm.5, f32[8,8,8192]{2,1,0:T(8,128)} %x_hbm.3, ...), custom_call_target="tpu_custom_call" | custom-call | tf_op jit(solution)/shard_map/first_primal/pallas_call | solution.py:495
  21.2 2.2 %collective-permute-start.1 = (f32[1,8192]{1,0:T(1,128)S(1)}, f32[1,8192]{1,0:T(1,128)S(1)}, u32[]{:S(2)}, u32[]{:S(2)}) collective-permute-start(f32[1,8192]{1,0:T(1,128)S(1)} %get-tuple-element.54), channel_id=1, source_target_pairs={{0,8},{16,24},{32,40},{48,56},{64,72},{80,88},{96,104},{112,120},{... | collective-permute-start | bytes 98312 | tf_op jit(solution)/shard_map/ppermute | solution.py:459
  23.4 3.0 %collective-permute-start.2 = (f32[1,8192]{1,0:T(1,128)S(1)}, f32[1,8192]{1,0:T(1,128)S(1)}, u32[]{:S(2)}, u32[]{:S(2)}) collective-permute-start(f32[1,8192]{1,0:T(1,128)S(1)} %get-tuple-element.55), channel_id=1, source_target_pairs={{8,16},{24,32},{40,48},{56,64},{72,80},{88,96},{104,112},{120,128}... | collective-permute-start | bytes 98312 | tf_op jit(solution)/shard_map/ppermute | solution.py:459
  26.4 0.6 first_use.1
  27.1 0.0 collective-permute-done.1.chip_ref
  27.1 1.6 %collective-permute-done.2.far_ref = f32[1,8192]{1,0:T(1,128)S(1)} collective-permute-done((f32[1,8192]{1,0:T(1,128)S(1)}, f32[1,8192]{1,0:T(1,128)S(1)}, u32[]{:S(2)}, u32[]{:S(2)}) %collective-permute-start.2) | collective-permute-done | bytes 32800 | tf_op jit(solution)/shard_map/ppermute | solution.py:459
  28.7 11.2 %all_to_all.20.in_ref = f32[8,16,256]{2,1,0:T(8,128)S(1)} all-to-all(f32[8,16,256]{2,1,0:T(8,128)S(1)} %get-tuple-element.56), channel_id=1, replica_groups=mesh['day'=32,'cls'=8] {'cls'}, dimensions={0} | all-to-all | bytes 262144 | tf_op jit(solution)/shard_map/all_to_all | solution.py:510
  39.9 0.6 caps_step.1
  40.6 11.1 %all-to-all-start.2 = ((f32[32,1,256]{2,1,0:T(1,128)}), f32[32,1,256]{2,1,0:T(1,128)S(1)}, u32[]{:S(2)}, u32[]{:S(2)}) async-start(f32[32,1,256]{2,1,0:T(1,128)} %get-tuple-element.59), calls=%async_computation.2 | async-start | bytes 65536 | tf_op jit(solution)/shard_map/all_to_all | solution.py:517
  51.7 0.2 next_duals.1
  51.9 2.0 %next_grad.1.grad_ref = f32[8,8,8192]{2,1,0:T(8,128)S(1)} custom-call(f32[8,8,8192]{2,1,0:T(8,128)} %cost_hbm.5, f32[8,128]{1,0:T(8,128)S(1)} %get-tuple-element.39.weights_ref, f32[8,256]{1,0:T(8,128)S(1)} %get-tuple-element.60.caps_ref, f32[8,8192]{1,0:T(8,128)S(1)} %get-tuple-element.62.kt_ref, s32[1,8192]{1,0:T(1,128)S(1)} %get-tuple-element.46.fac_ref), custom_call_target="tpu_custom_call" | custom-call | flops 10000000 | bytes 8000000 | tf_op jit(solution)/shard_map/next_grad/pallas_call | solution.py:518
  53.9 5.1 %all-to-all-done.2.moved_ref = f32[32,1,256]{2,1,0:T(1,128)S(1)} async-done(((f32[32,1,256]{2,1,0:T(1,128)}), f32[32,1,256]{2,1,0:T(1,128)S(1)}, u32[]{:S(2)}, u32[]{:S(2)}) %all-to-all-start.2) | async-done | bytes 32800 | tf_op jit(solution)/shard_map/all_to_all | solution.py:517
  58.9 0.0 copy-start
  58.9 3.9 %second_primal.1 = (f32[8,8,8192]{2,1,0:T(8,128)}, f32[8,8192]{1,0:T(8,128)S(1)}, f32[1,8192]{1,0:T(1,128)S(1)}, f32[8,128]{1,0:T(8,128)S(1)}, f32[8,8,128]{2,1,0:T(8,128)}) custom-call(f32[8,8,8192]{2,1,0:T(8,128)} %get-tuple-element.48.x_hbm, f32[32,1,256]{2,1,0:T(1,128)S(1)} %all-to-all-done.2.moved_ref, f32[8,128]{1,0:T(8,128)S(1)} %get-tuple-element.39.weights_ref, ...), custom_call_target="tpu_custom_call" | custom-call | tf_op jit(solution)/shard_map/second_primal/pallas_call | solution.py:521
  62.9 3.4 %all-to-all-start.3 = ((f32[8,8,128]{2,1,0:T(8,128)}), f32[8,8,128]{2,1,0:T(8,128)S(1)}, u32[]{:S(2)}, u32[]{:S(2)}) async-start(f32[8,8,128]{2,1,0:T(8,128)} %get-tuple-element.64), calls=%async_computation.3 | async-start | bytes 65536 | tf_op jit(solution)/shard_map/all_to_all | solution.py:529
  66.2 2.5 %collective-permute-start.3 = (f32[1,8192]{1,0:T(1,128)S(1)}, f32[1,8192]{1,0:T(1,128)S(1)}, u32[]{:S(2)}, u32[]{:S(2)}) collective-permute-start(f32[1,8192]{1,0:T(1,128)S(1)} %get-tuple-element.68), channel_id=1, source_target_pairs={{0,8},{8,16},{16,24},{24,32},{32,40},{40,48},{48,56},{56,64},{64,7... | collective-permute-start | bytes 98312 | tf_op jit(solution)/shard_map/ppermute | solution.py:448
  68.7 1.0 %collective-permute-done.3.prior_ref = f32[1,8192]{1,0:T(1,128)S(1)} collective-permute-done((f32[1,8192]{1,0:T(1,128)S(1)}, f32[1,8192]{1,0:T(1,128)S(1)}, u32[]{:S(2)}, u32[]{:S(2)}) %collective-permute-start.3) | collective-permute-done | bytes 32800 | tf_op jit(solution)/shard_map/ppermute | solution.py:448
  69.7 3.3 %all-to-all-done.3.in_ref = f32[8,8,128]{2,1,0:T(8,128)S(1)} async-done(((f32[8,8,128]{2,1,0:T(8,128)}), f32[8,8,128]{2,1,0:T(8,128)S(1)}, u32[]{:S(2)}, u32[]{:S(2)}) %all-to-all-start.3) | async-done | bytes 32800 | tf_op jit(solution)/shard_map/all_to_all | solution.py:529
  73.0 0.0 copy-done
  73.0 0.9 %last_duals.1 = (f32[8,8192]{1,0:T(8,128)}, f32[8,32]{1,0:T(8,128)}) custom-call(f32[8,8,128]{2,1,0:T(8,128)S(1)} %all-to-all-done.3.in_ref, f32[8,32]{1,0:T(8,128)S(1)} %copy-done, f32[8,128]{1,0:T(8,128)S(1)} %get-tuple-element.65.omega_ref, f32[8,8192]{1,0:T(8,128)S(1)} %get-tuple-element.66.w_ref, f32[8,8192]{1,0:T(8,128)S(1)} %get-tuple-element.67.sum_ref, ...), custom_call_target="tpu_custom_call" | custom-call | tf_op jit(solution)/shard_map/last_duals/pallas_call | solution.py:530
  (1 shorter events, 0.0 us)
Async XLA Ops:
  2.1 15.9 %all-to-all-start = ((f32[8,8,128]{2,1,0:T(8,128)}), f32[8,8,128]{2,1,0:T(8,128)S(1)}, u32[]{:S(2)}, u32[]{:S(2)}) async-start(f32[8,8,128]{2,1,0:T(8,128)} %get-tuple-element.40), calls=%async_computation | async-start | bytes 65536 | tf_op jit(solution)/shard_map/all_to_all | solution.py:479
  11.1 5.8 %collective-permute-start = (f32[1,8192]{1,0:T(1,128)S(1)}, f32[1,8192]{1,0:T(1,128)S(1)}, u32[]{:S(2)}, u32[]{:S(2)}) collective-permute-start(f32[1,8192]{1,0:T(1,128)S(1)} %get-tuple-element.41), channel_id=1, source_target_pairs={{8,0},{16,8},{24,16},{32,24},{40,32},{48,40},{56,48},{64,56},{72,6... | collective-permute-start | bytes 98312 | tf_op jit(solution)/shard_map/ppermute | solution.py:453
  21.2 5.9 %collective-permute-start.1 = (f32[1,8192]{1,0:T(1,128)S(1)}, f32[1,8192]{1,0:T(1,128)S(1)}, u32[]{:S(2)}, u32[]{:S(2)}) collective-permute-start(f32[1,8192]{1,0:T(1,128)S(1)} %get-tuple-element.54), channel_id=1, source_target_pairs={{0,8},{16,24},{32,40},{48,56},{64,72},{80,88},{96,104},{112,120},{... | collective-permute-start | bytes 98312 | tf_op jit(solution)/shard_map/ppermute | solution.py:459
  23.4 5.2 %collective-permute-start.2 = (f32[1,8192]{1,0:T(1,128)S(1)}, f32[1,8192]{1,0:T(1,128)S(1)}, u32[]{:S(2)}, u32[]{:S(2)}) collective-permute-start(f32[1,8192]{1,0:T(1,128)S(1)} %get-tuple-element.55), channel_id=1, source_target_pairs={{8,16},{24,32},{40,48},{56,64},{72,80},{88,96},{104,112},{120,128}... | collective-permute-start | bytes 98312 | tf_op jit(solution)/shard_map/ppermute | solution.py:459
  40.6 18.3 %all-to-all-start.2 = ((f32[32,1,256]{2,1,0:T(1,128)}), f32[32,1,256]{2,1,0:T(1,128)S(1)}, u32[]{:S(2)}, u32[]{:S(2)}) async-start(f32[32,1,256]{2,1,0:T(1,128)} %get-tuple-element.59), calls=%async_computation.2 | async-start | bytes 65536 | tf_op jit(solution)/shard_map/all_to_all | solution.py:517
  58.9 14.1 %copy-start = (f32[8,32]{1,0:T(8,128)S(1)}, f32[8,32]{1,0:T(8,128)}, u32[]{:S(2)}) copy-start(f32[8,32]{1,0:T(8,128)} %room_ref.3) | copy-start | bytes 3076
  62.9 10.2 %all-to-all-start.3 = ((f32[8,8,128]{2,1,0:T(8,128)}), f32[8,8,128]{2,1,0:T(8,128)S(1)}, u32[]{:S(2)}, u32[]{:S(2)}) async-start(f32[8,8,128]{2,1,0:T(8,128)} %get-tuple-element.64), calls=%async_computation.3 | async-start | bytes 65536 | tf_op jit(solution)/shard_map/all_to_all | solution.py:529
  66.2 3.5 %collective-permute-start.3 = (f32[1,8192]{1,0:T(1,128)S(1)}, f32[1,8192]{1,0:T(1,128)S(1)}, u32[]{:S(2)}, u32[]{:S(2)}) collective-permute-start(f32[1,8192]{1,0:T(1,128)S(1)} %get-tuple-element.68), channel_id=1, source_target_pairs={{0,8},{8,16},{16,24},{24,32},{32,40},{40,48},{48,56},{56,64},{64,7... | collective-permute-start | bytes 98312 | tf_op jit(solution)/shard_map/ppermute | solution.py:448

commit v6 on v5

--- a/solution.py
+++ b/solution.py
@@ -124,6 +124,15 @@
     return tiles[0]
 
 
+def flat(tile):
+    return jnp.concatenate([tile[t : t + 1] for t in range(tile.shape[0])], axis=1)
+
+
+def unflat(line, rows):
+    width = line.shape[1] // rows
+    return jnp.concatenate([line[:, t * width : (t + 1) * width] for t in range(rows)], axis=0)
+
+
 def start(caps_ref, room_ref, w_ref, out_ref, row_ref, caps, room, sems):
     copies = [
         pltpu.make_async_copy(caps_ref, caps, sems.at[0]),
@@ -132,13 +141,11 @@
     ]
     for copy in copies:
         copy.start()
-    out_ref[...] = jnp.zeros(out_ref.shape, F32)
     copies[0].wait()
     copies[1].wait()
-    own = caps.shape[1]
+    line = flat(jnp.concatenate([caps[...], room[...]], axis=1))
     for k in range(out_ref.shape[0]):
-        out_ref[k, :, :own] = caps[...]
-        out_ref[k, :, own : 2 * own] = room[...]
+        out_ref[k] = line
     copies[2].wait()
 
 
@@ -220,8 +227,9 @@
     start_all(arrive)
     own = caps_ref.shape[1] // ends_ref.shape[0]
     for k in range(ends_ref.shape[0]):
-        caps_ref[:, k * own : (k + 1) * own] = ends_ref[k, :, :own]
-        room_ref[:, k * own : (k + 1) * own] = ends_ref[k, :, own : 2 * own]
+        ends = unflat(ends_ref[k], days)
+        caps_ref[:, k * own : (k + 1) * own] = ends[:, :own]
+        room_ref[:, k * own : (k + 1) * own] = ends[:, own:]
     caps = caps_ref[...]
     for k in range(classes // LANES):
         at = pl.ds(k * LANES, LANES)
@@ -310,25 +318,30 @@
         total = total + gap * gap
     edge = (ETA * ETA) * folded(total)
     dual = dual_ref[...] + jnp.where(rows_iota((days, LANES)) == 0, edge, 0.0)
-    use = use_ref[...]
-    moved = moved_ref[...]
+    line = jnp.concatenate(
+        [
+            flat(use_ref[...]),
+            jnp.sum(moved_ref[...], axis=0, keepdims=True),
+            jnp.sum(dual, axis=0, keepdims=True),
+        ],
+        axis=1,
+    )
     for k in range(out_ref.shape[0]):
-        out_ref[k, :days, :] = use
-        out_ref[k, days:, :LANES] = moved
-        out_ref[k, days:, LANES:] = dual
+        out_ref[k] = line
 
 
 def caps_step(in_ref, caps_ref, room_ref, caps1_ref, out_ref):
-    days = caps_ref.shape[0]
+    days, facilities = caps_ref.shape
     total = in_ref[0]
     for k in range(1, in_ref.shape[0]):
         total = total + in_ref[k]
+    uses = days * facilities
     caps = caps_ref[...]
-    new = jnp.minimum(caps - ETA * (total[:days] - room_ref[...]), 0.0)
+    new = jnp.minimum(caps - ETA * (unflat(total[:, :uses], days) - room_ref[...]), 0.0)
     caps1_ref[...] = new
     gone = new - caps
-    primal = jnp.sum(total[days:, :LANES], axis=0, keepdims=True)
-    dual = jnp.sum(total[days:, LANES:] + folded(gone * gone), axis=0, keepdims=True)
+    primal = total[:, uses : uses + LANES]
+    dual = total[:, uses + LANES :] + jnp.sum(folded(gone * gone), axis=0, keepdims=True)
     for k in range(out_ref.shape[0]):
         out_ref[k, :, :LANES] = primal
         out_ref[k, :, LANES:] = dual
@@ -351,10 +364,14 @@
         kt_ref[:, at] = w - gamma * jnp.where(rows == days - 1, edge, pltpu.roll(w, days - 1, 0))
 
 
-def next_grad(cost_hbm, weights_ref, caps_ref, kt_ref, fac_ref, grad_ref, sems):
+def next_grad(
+    cost_hbm, x_hbm, weights_ref, caps_ref, kt_ref, fac_ref, grad_ref, head_ref, sems, head_sem
+):
     days, classes = kt_ref.shape
     arrive = block_copies([(cost_hbm, grad_ref)], sems)
     start_all(arrive)
+    head = pltpu.make_async_copy(x_hbm.at[:, :, pl.ds(0, BLOCK)], head_ref, head_sem)
+    head.start()
     caps = caps_ref[...]
     weights = weights_ref[...]
 
@@ -370,15 +387,17 @@
     for k, block in enumerate(arrive):
         wait_all(block)
         lax.fori_loop(k * each, (k + 1) * each, step, 0)
+    head.wait()
 
 
 def second_primal(
-    x_hbm, moved_ref, weights_ref, grad_ref, bound_ref, fac_ref, caps_ref,
-    x2_hbm, sum_ref, last_ref, omega_ref, out_ref,
-    x_ref, weighted_ref, sems,
+    x_hbm, x_head, moved_ref, weights_ref, grad_ref, bound_ref, fac_ref,
+    x2_hbm, sum_ref, last_hbm, omega_ref, out_hbm,
+    x_ref, weighted_ref, last_ref, out_ref, sems, small_sems,
 ):
     days, classes = sum_ref.shape
-    arrive = block_copies([(x_hbm, x_ref)], sems)
+    ready = x_head.shape[2] // BLOCK
+    arrive = block_copies([(x_hbm, x_ref)], sems, ready)
     leave = block_copies([(x_ref, x2_hbm)], sems.at[1:])
     start_all(arrive)
     total = moved_ref[0]
@@ -391,13 +410,13 @@
     tau = jnp.broadcast_to(ETA / omega, (8, LANES))
     weights = weights_ref[...]
 
-    def step(j, _):
+    def step(x_at, j, _):
         for u in range(STEP // LANES):
             at = lanes_of(j, u)
             bound = bound_ref[:, at]
             sums, weighted = [], []
             for t in range(days):
-                old = x_ref[t, :, at]
+                old = x_at[t, :, at]
                 new = jnp.minimum(jnp.maximum(old - tau * grad_ref[t, :, at], 0.0), bound)
                 x_ref[t, :, at] = new
                 extra = new + (new - old)
@@ -410,31 +429,41 @@
         return 0
 
     each = BLOCK // STEP
-    for k, block in enumerate(arrive):
-        wait_all(block)
-        lax.fori_loop(k * each, (k + 1) * each, step, 0)
+    for k in range(len(leave)):
+        if k >= ready:
+            wait_all(arrive[k - ready])
+        source = x_ref if k >= ready else x_head
+        lax.fori_loop(k * each, (k + 1) * each, functools.partial(step, source), 0)
         start_all(leave[k : k + 1])
-    parts = facility_sums(weighted_ref, fac_ref, caps_ref.shape[1])
-    own = caps_ref.shape[1] // out_ref.shape[0]
-    out_ref[...] = jnp.zeros(out_ref.shape, F32)
-    for k in range(out_ref.shape[0]):
+    row = pltpu.make_async_copy(last_ref, last_hbm, small_sems.at[0])
+    row.start()
+    blocks = out_ref.shape[0]
+    own = out_ref.shape[2] // days
+    parts = facility_sums(weighted_ref, fac_ref, own * blocks)
+    for k in range(blocks):
         g, place = divmod(k * own, WIDE)
-        out_ref[k, :, :own] = parts[g][:, place : place + own]
-        out_ref[k, :, own : 2 * own] = caps_ref[:, k * own : (k + 1) * own]
+        out_ref[k] = flat(parts[g][:, place : place + own])
+    out = pltpu.make_async_copy(out_ref, out_hbm, small_sems.at[1])
+    out.start()
+    row.wait()
+    out.wait()
     for block in leave:
         wait_all(block)
 
 
-def last_duals(in_ref, room_ref, omega_ref, w_ref, sum_ref, prior_ref, inflow_ref, gamma_ref, w2_ref, caps2_ref):
+def last_duals(
+    in_ref, caps_ref, room_ref, omega_ref, w_ref, sum_ref, prior_ref, inflow_ref, gamma_ref, w2_ref, caps2_ref
+):
     days, classes = w_ref.shape
     sigma = ETA * omega_ref[...]
     own = room_ref.shape[1]
-    use = in_ref[0, :, :own]
-    for k in range(1, in_ref.shape[0]):
-        use = use + in_ref[k, :, :own]
-    caps2_ref[...] = jnp.minimum(
-        in_ref[0, :, own : 2 * own] - sigma[:1, :1] * (use - room_ref[...]), 0.0
-    )
+    blocks = in_ref.shape[0]
+    mine = lax.axis_index("cls")
+    use, caps = in_ref[0], caps_ref[:, :own]
+    for k in range(1, blocks):
+        use = use + in_ref[k]
+        caps = jnp.where(mine == k, caps_ref[:, k * own : (k + 1) * own], caps)
+    caps2_ref[...] = jnp.minimum(caps - sigma[:1, :1] * (unflat(use, days) - room_ref[...]), 0.0)
     rows = rows_iota((days, LANES))
     for k in range(classes // LANES):
         at = pl.ds(k * LANES, LANES)
@@ -472,7 +501,7 @@
     index = decay_index.reshape(1, classes)
 
     ends, row = call(
-        start, "start", [struct(blocks, days, LANES), struct(1, classes)], [ANY] * 3,
+        start, "start", [struct(blocks, 1, 2 * days * own), struct(1, classes)], [ANY] * 3,
         [pltpu.VMEM((days, own), F32), pltpu.VMEM((days, own), F32), pltpu.SemaphoreType.DMA((3,))],
     )(*in_hbm(ycap_start, capacity, ybal_start))
     after = to_previous(row)
@@ -505,7 +534,7 @@
         weighted, sums, inflow, gamma, fac
     )
     sent, prior = call(
-        first_send, "first_send", [struct(blocks, 2 * days, facilities), row], [VM] * 8
+        first_send, "first_send", [struct(blocks, 1, days * facilities + 2 * LANES), row], [VM] * 8
     )(use, moved, dual, chip, far, sums, inflow, gamma)
     got = lax.all_to_all(sent, "cls", 0, 0)
     caps1, sent = call(
@@ -515,20 +544,24 @@
         w, sums, inflow, gamma, prior, chip, far
     )
     got = lax.all_to_all(sent, "day", 0, 0)
-    (grad,) = call(
-        next_grad, "next_grad", [field], [ANY] + [VM] * 4, [pltpu.SemaphoreType.DMA((1, streams))], cost=PASS
-    )(*in_hbm(cost), weights, caps1, kt, fac)
+    grad, x1_head = call(
+        next_grad, "next_grad", [field, struct(days, opts, BLOCK)], [ANY] * 2 + [VM] * 4,
+        [pltpu.SemaphoreType.DMA((1, streams)), pltpu.SemaphoreType.DMA], cost=PASS,
+    )(*in_hbm(cost, x1), weights, caps1, kt, fac)
     x2, sums2, last2, omega, sent = call(
         second_primal, "second_primal",
-        [pltpu.HBM(field.shape, F32), rows, row, tile, struct(blocks, days, LANES)],
+        [pltpu.HBM(field.shape, F32), rows, pltpu.HBM(row.shape, F32), tile,
+         pltpu.HBM((blocks, 1, days * own), F32)],
         [ANY] + [VM] * 6,
-        [pltpu.VMEM(field.shape, F32), pltpu.VMEM(rows.shape, F32), pltpu.SemaphoreType.DMA((2, streams))],
-        limit=8, out_specs=[ANY] + [VM] * 4,
-    )(*in_hbm(x1), got, weights, grad, bound, fac, caps1)
+        [pltpu.VMEM(field.shape, F32), pltpu.VMEM(rows.shape, F32), pltpu.VMEM(row.shape, F32),
+         pltpu.VMEM((blocks, 1, days * own), F32), pltpu.SemaphoreType.DMA((2, streams)),
+         pltpu.SemaphoreType.DMA((2,))],
+        limit=8, out_specs=[ANY, VM, ANY, VM, ANY],
+    )(*in_hbm(x1), x1_head, got, weights, grad, bound, fac)
     prior2 = to_next(last2)
     got = lax.all_to_all(sent, "cls", 0, 0)
-    w2, caps2 = call(last_duals, "last_duals", [struct(days, classes), struct(days, own)], [VM] * 8)(
-        got, capacity, omega, w1, sums2, prior2, inflow, gamma
+    w2, caps2 = call(last_duals, "last_duals", [struct(days, classes), struct(days, own)], [VM] * 9)(
+        got, caps1, capacity, omega, w1, sums2, prior2, inflow, gamma
     )
     return x2, w2, caps2
 

time: 74.4 us -> 75.7 us (1.017)
  blocking collectives: 11.2 us -> 19.5 us
  starting transfers between devices: 34 us -> 29.2 us
  waiting for transfers between devices: 12.9 us -> 10.7 us
    all_to_all x1 -> x2, blocking collectives: 11.2 us -> 19.5 us  [local(): got = lax.all_to_all(sent, 'cls', 0, 0)]
    all_to_all x1, waiting for transfers between devices: 1.04 us -> 4.61 us  [local(): ends = lax.all_to_all(ends, 'cls', 0, 0)]
    all_to_all x1 -> x0, starting transfers between devices: 3.35 us -> none  [local(): got = lax.all_to_all(sent, 'cls', 0, 0)]
    all_to_all x1 -> x0, waiting for transfers between devices: 3.29 us -> none  [local(): got = lax.all_to_all(sent, 'cls', 0, 0)]
    all_to_all x1, starting transfers between devices: 9.03 us -> 6.46 us  [local(): ends = lax.all_to_all(ends, 'cls', 0, 0)]
    ppermute x1, starting transfers between devices: 2.85 us -> 5.15 us  [to_previous(): return lax.ppermute(row, 'day', [(i + 1, i) for i in range(n - 1)])]
    ppermute x1, waiting for transfers between devices: 1 us -> 0.01 us  [to_next(): return lax.ppermute(row, 'day', [(i, i + 1) for i in range(n - 1)])]
    ppermute x1, waiting for transfers between devices: 0.95 us -> 0.01 us  [to_previous(): return lax.ppermute(row, 'day', [(i + 1, i) for i in range(n - 1)])]
  transfers between devices with their start and end apart: 7 -> 6, of which waited for: 6 -> 3; matrix products, arithmetic and copies ran while one was open for 0% -> 0% of each run, Pallas kernels for 7% -> 6%
where the time goes in v6:
time: 75.7 us; the launch traced here: 75.2 us
  starting transfers between devices  29.2 us (39%)
  blocking collectives  19.5 us (26%)
  Pallas kernels  15 us (20%)
  waiting for transfers between devices  10.7 us (14%)
    all_to_all x2, blocking collectives, local(): got = lax.all_to_all(sent, 'cls', 0, 0)  19.5 us
    all_to_all x1, starting transfers between devices, local(): got = lax.all_to_all(sent, 'day', 0, 0)  10.6 us
    all_to_all x1, starting transfers between devices, local(): ends = lax.all_to_all(ends, 'cls', 0, 0)  6.46 us
    ppermute x1, starting transfers between devices, to_previous(): return lax.ppermute(row, 'day', [(i + 1, i) for i in range(n - 1)])  5.15 us
    all_to_all x1, waiting for transfers between devices, local(): got = lax.all_to_all(sent, 'day', 0, 0)  5.04 us
    all_to_all x1, waiting for transfers between devices, local(): ends = lax.all_to_all(ends, 'cls', 0, 0)  4.61 us
    ppermute x2, starting transfers between devices, swapped(): return lax.ppermute(rows, 'day', pairs + [(j, i) for i, j in pairs])  4.55 us
    pallas_call x1, Pallas kernels, local(): call(first_primal, 'first_primal', [pltpu.HBM(field.shape, F32), rows, ro...  3.38 us
  transfers between devices with their start and end apart: 6, of which 3 were waited for; matrix products, arithmetic and copies ran while one was open for 0% of the time, Pallas kernels for 6%

profile of v6, /device:TPU:1, one launch (start us, length us, event | category | flops | bytes accessed | tf_op | source)
XLA Modules:
  0.0 75.2 jit_solution(3215689750724216523)
XLA Ops:
  0.6 1.5 %start.1 = (f32[8,1,512]{2,1,0:T(1,128)}, f32[1,8192]{1,0:T(1,128)S(1)}) custom-call(f32[8,32]{1,0:T(8,128)} %caps_ref.1, f32[8,32]{1,0:T(8,128)} %room_ref.3, f32[8,8192]{1,0:T(8,128)} %w_ref.1), custom_call_target="tpu_custom_call" | custom-call | tf_op jit(solution)/shard_map/start/pallas_call | solution.py:503
  2.1 5.1 %collective-permute-start = (f32[1,8192]{1,0:T(1,128)S(1)}, f32[1,8192]{1,0:T(1,128)S(1)}, u32[]{:S(2)}, u32[]{:S(2)}) collective-permute-start(f32[1,8192]{1,0:T(1,128)S(1)} %get-tuple-element.43), channel_id=1, source_target_pairs={{8,0},{16,8},{24,16},{32,24},{40,32},{48,40},{56,48},{64,56},{72,6... | collective-permute-start | bytes 98312 | tf_op jit(solution)/shard_map/ppermute | solution.py:482
  7.3 6.5 %all-to-all-start = ((f32[8,1,512]{2,1,0:T(1,128)}), f32[8,1,512]{2,1,0:T(1,128)S(1)}, u32[]{:S(2)}, u32[]{:S(2)}) async-start(f32[8,1,512]{2,1,0:T(1,128)} %get-tuple-element.42), calls=%async_computation | async-start | bytes 32768 | tf_op jit(solution)/shard_map/all_to_all | solution.py:508
  13.7 2.0 %load.1 = (f32[8,8,2048]{2,1,0:T(8,128)S(1)}, f32[8,8,2048]{2,1,0:T(8,128)S(1)}, f32[8,8192]{1,0:T(8,128)S(1)}, f32[8,8192]{1,0:T(8,128)S(1)}, f32[8,8192]{1,0:T...) custom-call(f32[8]{0:T(128)} %usage_hbm.1, ...), custom_call_target="tpu_custom_call" | custom-call | flops 10000000 | bytes 8000000 | tf_op jit(solution)/shard_map/load/pallas_call | solution.py:514
  15.8 4.6 %all-to-all-done.ends_ref = f32[8,1,512]{2,1,0:T(1,128)S(1)} async-done(((f32[8,1,512]{2,1,0:T(1,128)}), f32[8,1,512]{2,1,0:T(1,128)S(1)}, u32[]{:S(2)}, u32[]{:S(2)}) %all-to-all-start) | async-done | bytes 16416 | tf_op jit(solution)/shard_map/all_to_all | solution.py:508
  20.4 0.0 collective-permute-done.after_ref
  20.4 3.4 %first_primal.1 = (f32[8,8,8192]{2,1,0:T(8,128)}, f32[8,8192]{1,0:T(8,128)S(1)}, f32[8,8192]{1,0:T(8,128)S(1)}, f32[1,8192]{1,0:T(1,128)S(1)}, f32[1,8192]{1,0:T...) custom-call(f32[8,8,8192]{2,1,0:T(8,128)} %cost_hbm.5, f32[8,8,8192]{2,1,0:T(8,128)} %x_hbm.3, ...), custom_call_target="tpu_custom_call" | custom-call | tf_op jit(solution)/shard_map/first_primal/pallas_call | solution.py:524
  23.7 1.0 %collective-permute-start.1 = (f32[1,8192]{1,0:T(1,128)S(1)}, f32[1,8192]{1,0:T(1,128)S(1)}, u32[]{:S(2)}, u32[]{:S(2)}) collective-permute-start(f32[1,8192]{1,0:T(1,128)S(1)} %get-tuple-element.56), channel_id=1, source_target_pairs={{0,8},{16,24},{32,40},{48,56},{64,72},{80,88},{96,104},{112,120},{... | collective-permute-start | bytes 98312 | tf_op jit(solution)/shard_map/ppermute | solution.py:488
  24.8 3.5 %collective-permute-start.2 = (f32[1,8192]{1,0:T(1,128)S(1)}, f32[1,8192]{1,0:T(1,128)S(1)}, u32[]{:S(2)}, u32[]{:S(2)}) collective-permute-start(f32[1,8192]{1,0:T(1,128)S(1)} %get-tuple-element.57), channel_id=1, source_target_pairs={{8,16},{24,32},{40,48},{56,64},{72,80},{88,96},{104,112},{120,128}... | collective-permute-start | bytes 98312 | tf_op jit(solution)/shard_map/ppermute | solution.py:488
  28.3 0.6 first_use.1
  28.9 0.0 collective-permute-done.1.chip_ref
  28.9 1.1 %collective-permute-done.2.far_ref = f32[1,8192]{1,0:T(1,128)S(1)} collective-permute-done((f32[1,8192]{1,0:T(1,128)S(1)}, f32[1,8192]{1,0:T(1,128)S(1)}, u32[]{:S(2)}, u32[]{:S(2)}) %collective-permute-start.2) | collective-permute-done | bytes 32800 | tf_op jit(solution)/shard_map/ppermute | solution.py:488
  30.0 0.1 first_send.1
  30.1 9.7 %all_to_all.20.in_ref = f32[8,1,2304]{2,1,0:T(1,128)S(1)} all-to-all(f32[8,1,2304]{2,1,0:T(1,128)S(1)} %get-tuple-element.58), channel_id=1, replica_groups=mesh['day'=32,'cls'=8] {'cls'}, dimensions={0} | all-to-all | bytes 147456 | tf_op jit(solution)/shard_map/all_to_all | solution.py:539
  39.7 0.7 caps_step.1
  40.4 10.6 %all-to-all-start.2 = ((f32[32,1,256]{2,1,0:T(1,128)}), f32[32,1,256]{2,1,0:T(1,128)S(1)}, u32[]{:S(2)}, u32[]{:S(2)}) async-start(f32[32,1,256]{2,1,0:T(1,128)} %get-tuple-element.65), calls=%async_computation.2 | async-start | bytes 65536 | tf_op jit(solution)/shard_map/all_to_all | solution.py:546
  51.0 0.2 next_duals.1
  51.2 2.0 %next_grad.1 = (f32[8,8,8192]{2,1,0:T(8,128)S(1)}, f32[8,8,1024]{2,1,0:T(8,128)S(1)}) custom-call(f32[8,8,8192]{2,1,0:T(8,128)} %cost_hbm.5, f32[8,8,8192]{2,1,0:T(8,128)} %get-tuple-element.50.x_hbm, f32[8,128]{1,0:T(8,128)S(1)} %get-tuple-element.41.weights_ref, f32[8,256]{1,0:T(8,128)S(1)} %get-tuple-element.61.caps_ref, ...), custom_call_target="tpu_custom_call" | custom-call | flops 10000000 | bytes 8000000 | tf_op jit(solution)/shard_map/next_grad/pallas_call | solution.py:547
  53.2 5.0 %all-to-all-done.2.moved_ref = f32[32,1,256]{2,1,0:T(1,128)S(1)} async-done(((f32[32,1,256]{2,1,0:T(1,128)}), f32[32,1,256]{2,1,0:T(1,128)S(1)}, u32[]{:S(2)}, u32[]{:S(2)}) %all-to-all-start.2) | async-done | bytes 32800 | tf_op jit(solution)/shard_map/all_to_all | solution.py:546
  58.3 0.0 copy-start
  58.3 3.4 %second_primal.1 = (f32[8,8,8192]{2,1,0:T(8,128)}, f32[8,8192]{1,0:T(8,128)S(1)}, f32[1,8192]{1,0:T(1,128)}, f32[8,128]{1,0:T(8,128)S(1)}, f32[8,1,256]{2,1,0:T(1,128)}) custom-call(f32[8,8,8192]{2,1,0:T(8,128)} %get-tuple-element.50.x_hbm, f32[8,8,1024]{2,1,0:T(8,128)S(1)} %get-tuple-element.64.x_head, f32[32,1,256]{2,1,0:T(1,128)S(1)} %all-to-all-done.2.moved_ref, ...), custom_call_target="tpu_custom_call" | custom-call | tf_op jit(solution)/shard_map/second_primal/pallas_call | solution.py:551
  61.6 2.5 %collective-permute-start.3 = (f32[1,8192]{1,0:T(1,128)}, f32[1,8192]{1,0:T(1,128)S(1)}, u32[]{:S(2)}, u32[]{:S(2)}) collective-permute-start(f32[1,8192]{1,0:T(1,128)} %get-tuple-element.72), channel_id=1, source_target_pairs={{0,8},{8,16},{16,24},{24,32},{32,40},{40,48},{48,56},{56,64},{64,7... | collective-permute-start | bytes 98312 | tf_op jit(solution)/shard_map/ppermute | solution.py:477
  64.1 9.8 %all_to_all.21.in_ref = f32[8,1,256]{2,1,0:T(1,128)S(1)} all-to-all(f32[8,1,256]{2,1,0:T(1,128)} %get-tuple-element.68), channel_id=1, replica_groups=mesh['day'=32,'cls'=8] {'cls'}, dimensions={0} | all-to-all | bytes 16384 | tf_op jit(solution)/shard_map/all_to_all | solution.py:562
  73.9 0.0 collective-permute-done.3.prior_ref
  73.9 0.0 copy-done
  73.9 1.2 %last_duals.1 = (f32[8,8192]{1,0:T(8,128)}, f32[8,32]{1,0:T(8,128)}) custom-call(f32[8,1,256]{2,1,0:T(1,128)S(1)} %all_to_all.21.in_ref, f32[8,256]{1,0:T(8,128)S(1)} %get-tuple-element.61.caps_ref, f32[8,32]{1,0:T(8,128)S(1)} %copy-done, f32[8,128]{1,0:T(8,128)S(1)} %get-tuple-element.69.omega_ref, f32[8,8192]{1,0:T(8,128)S(1)} %get-tuple-element.70.w_ref, ...), custom_call_target="tpu_custom_call" | custom-call | tf_op jit(solution)/shard_map/last_duals/pallas_call | solution.py:563
Async XLA Ops:
  2.1 18.2 %collective-permute-start = (f32[1,8192]{1,0:T(1,128)S(1)}, f32[1,8192]{1,0:T(1,128)S(1)}, u32[]{:S(2)}, u32[]{:S(2)}) collective-permute-start(f32[1,8192]{1,0:T(1,128)S(1)} %get-tuple-element.43), channel_id=1, source_target_pairs={{8,0},{16,8},{24,16},{32,24},{40,32},{48,40},{56,48},{64,56},{72,6... | collective-permute-start | bytes 98312 | tf_op jit(solution)/shard_map/ppermute | solution.py:482
  7.3 13.1 %all-to-all-start = ((f32[8,1,512]{2,1,0:T(1,128)}), f32[8,1,512]{2,1,0:T(1,128)S(1)}, u32[]{:S(2)}, u32[]{:S(2)}) async-start(f32[8,1,512]{2,1,0:T(1,128)} %get-tuple-element.42), calls=%async_computation | async-start | bytes 32768 | tf_op jit(solution)/shard_map/all_to_all | solution.py:508
  23.7 5.2 %collective-permute-start.1 = (f32[1,8192]{1,0:T(1,128)S(1)}, f32[1,8192]{1,0:T(1,128)S(1)}, u32[]{:S(2)}, u32[]{:S(2)}) collective-permute-start(f32[1,8192]{1,0:T(1,128)S(1)} %get-tuple-element.56), channel_id=1, source_target_pairs={{0,8},{16,24},{32,40},{48,56},{64,72},{80,88},{96,104},{112,120},{... | collective-permute-start | bytes 98312 | tf_op jit(solution)/shard_map/ppermute | solution.py:488
  24.8 5.2 %collective-permute-start.2 = (f32[1,8192]{1,0:T(1,128)S(1)}, f32[1,8192]{1,0:T(1,128)S(1)}, u32[]{:S(2)}, u32[]{:S(2)}) collective-permute-start(f32[1,8192]{1,0:T(1,128)S(1)} %get-tuple-element.57), channel_id=1, source_target_pairs={{8,16},{24,32},{40,48},{56,64},{72,80},{88,96},{104,112},{120,128}... | collective-permute-start | bytes 98312 | tf_op jit(solution)/shard_map/ppermute | solution.py:488
  40.4 17.9 %all-to-all-start.2 = ((f32[32,1,256]{2,1,0:T(1,128)}), f32[32,1,256]{2,1,0:T(1,128)S(1)}, u32[]{:S(2)}, u32[]{:S(2)}) async-start(f32[32,1,256]{2,1,0:T(1,128)} %get-tuple-element.65), calls=%async_computation.2 | async-start | bytes 65536 | tf_op jit(solution)/shard_map/all_to_all | solution.py:546
  58.3 15.7 %copy-start = (f32[8,32]{1,0:T(8,128)S(1)}, f32[8,32]{1,0:T(8,128)}, u32[]{:S(2)}) copy-start(f32[8,32]{1,0:T(8,128)} %room_ref.3) | copy-start | bytes 3076
  61.6 12.3 %collective-permute-start.3 = (f32[1,8192]{1,0:T(1,128)}, f32[1,8192]{1,0:T(1,128)S(1)}, u32[]{:S(2)}, u32[]{:S(2)}) collective-permute-start(f32[1,8192]{1,0:T(1,128)} %get-tuple-element.72), channel_id=1, source_target_pairs={{0,8},{8,16},{16,24},{24,32},{32,40},{40,48},{48,56},{56,64},{64,7... | collective-permute-start | bytes 98312 | tf_op jit(solution)/shard_map/ppermute | solution.py:477

commit v7 on v6

--- a/solution.py
+++ b/solution.py
@@ -18,6 +18,7 @@
 
 VM = pl.BlockSpec(memory_space=pltpu.VMEM)
 PASS = pl.CostEstimate(flops=10_000_000, bytes_accessed=8_000_000, transcendentals=0)
+LONG = pl.CostEstimate(flops=10_000_000, bytes_accessed=100_000_000, transcendentals=0)
 ANY = pl.BlockSpec(memory_space=pl.ANY)
 F32 = jnp.float32
 
@@ -143,9 +144,11 @@
         copy.start()
     copies[0].wait()
     copies[1].wait()
-    line = flat(jnp.concatenate([caps[...], room[...]], axis=1))
+    own = caps.shape[1]
+    out_ref[...] = jnp.zeros(out_ref.shape, F32)
     for k in range(out_ref.shape[0]):
-        out_ref[k] = line
+        out_ref[k, :, :own] = caps[...]
+        out_ref[k, :, own : 2 * own] = room[...]
     copies[2].wait()
 
 
@@ -179,7 +182,7 @@
 
 def load(
     usage_hbm, table_hbm, w_hbm, inflow_hbm, upper_hbm, fac_hbm, count_hbm, index_hbm, cost_hbm, x_hbm,
-    cost_ref, x_ref, kt_ref, w_ref, inflow_ref, bound_ref, fac_ref, gamma_ref, weights_ref,
+    cost_ref, x_ref, cost_edge, x_edge, kt_ref, w_ref, inflow_ref, bound_ref, fac_ref, gamma_ref, weights_ref,
     usage_ref, table_ref, count_ref, index_ref, sems,
 ):
     days, classes = w_ref.shape
@@ -193,6 +196,11 @@
         pltpu.make_async_copy(a.at[:, :, head], b, sems.at[len(small) + k])
         for k, (a, b) in enumerate(((cost_hbm, cost_ref), (x_hbm, x_ref)))
     ]
+    large += [
+        pltpu.make_async_copy(a.at[t], b.at[n], sems.at[len(small) + 2 + 2 * n + k])
+        for n, t in enumerate((0, days - 1))
+        for k, (a, b) in enumerate(((cost_hbm, cost_edge), (x_hbm, x_edge)))
+    ]
     for copy in small + large:
         copy.start()
     for copy in small:
@@ -215,39 +223,63 @@
     wait_all(large)
 
 
+def edge_primal(
+    cost_ref, x_ref, weights_ref, ends_ref, after_ref, kt_in_ref, gamma_ref, w_ref, inflow_ref, bound_ref, fac_ref,
+    kt_ref, pulled_ref, chip_ref, far_ref, caps_ref, room_ref,
+):
+    days, classes = w_ref.shape
+    own = caps_ref.shape[1] // ends_ref.shape[0]
+    for k in range(ends_ref.shape[0]):
+        caps_ref[:, k * own : (k + 1) * own] = ends_ref[k, :, :own]
+        room_ref[:, k * own : (k + 1) * own] = ends_ref[k, :, own : 2 * own]
+    caps = caps_ref[...]
+    weights = weights_ref[...]
+    second = second_core()
+    rows = rows_iota((days, LANES))
+
+    def step(j, _):
+        for u in range(STEP // LANES):
+            at = lanes_of(j, u)
+            pulled = pulled_of(caps, fac_ref[:, at])
+            pulled_ref[:, at] = pulled
+            kt = kt_in_ref[:, at]
+            kt = jnp.where(rows == days - 1, kt - gamma_ref[:, at] * after_ref[:, at], kt)
+            kt_ref[:, at] = kt
+            sums = []
+            for n, t in enumerate((0, days - 1)):
+                old = x_ref[n, :, at]
+                grad = cost_ref[n, :, at] - kt[t : t + 1] - weights * pulled[t : t + 1]
+                new = jnp.minimum(jnp.maximum(old - ETA * grad, 0.0), bound_ref[:, at])
+                sums.append(jnp.sum(new + (new - old), axis=0, keepdims=True))
+            lead = w_ref[:1, at] - ETA * (sums[0] - inflow_ref[:1, at])
+            chip_ref[:, at] = jnp.where(second, lead, sums[1])
+            far_ref[:, at] = jnp.where(second, sums[1], lead)
+        return 0
+
+    lax.fori_loop(0, classes // STEP, step, 0)
+
+
 def first_primal(
-    cost_hbm, x_hbm, cost_head, x_head, weights_ref, ends_ref, after_ref, kt_ref, w_ref, inflow_ref, bound_ref, fac_ref, gamma_ref,
-    x1_hbm, sum_ref, weighted_ref, chip_ref, far_ref, moved_ref, caps_ref, room_ref,
+    cost_hbm, x_hbm, cost_head, x_head, weights_ref, pulled_ref, kt_ref, bound_ref,
+    x1_hbm, sum_ref, weighted_ref, moved_ref,
     cost_ref, x_ref, sems,
 ):
-    days, classes = w_ref.shape
+    days, classes = kt_ref.shape
     ready = HEAD // BLOCK
     arrive = block_copies([(cost_hbm, cost_ref), (x_hbm, x_ref)], sems, ready)
     leave = block_copies([(x_ref, x1_hbm)], sems.at[2:])
     start_all(arrive)
-    own = caps_ref.shape[1] // ends_ref.shape[0]
-    for k in range(ends_ref.shape[0]):
-        ends = unflat(ends_ref[k], days)
-        caps_ref[:, k * own : (k + 1) * own] = ends[:, :own]
-        room_ref[:, k * own : (k + 1) * own] = ends[:, own:]
-    caps = caps_ref[...]
-    for k in range(classes // LANES):
-        at = pl.ds(k * LANES, LANES)
-        sum_ref[:, at] = pulled_of(caps, fac_ref[:, at])
     weights = weights_ref[...]
-    second = second_core()
 
     def step(cost_at, x_at, j, moved):
         moved = list(moved)
         for u in range(STEP // LANES):
             at = lanes_of(j, u)
             bound = bound_ref[:, at]
-            late = kt_ref[days - 1 :, at] - gamma_ref[:, at] * after_ref[:, at]
             sums, weighted = [], []
             for t in range(days):
                 old = x_at[t, :, at]
-                kt = late if t == days - 1 else kt_ref[t : t + 1, at]
-                grad = cost_at[t, :, at] - kt - weights * sum_ref[t : t + 1, at]
+                grad = cost_at[t, :, at] - kt_ref[t : t + 1, at] - weights * pulled_ref[t : t + 1, at]
                 new = jnp.minimum(jnp.maximum(old - ETA * grad, 0.0), bound)
                 x_ref[t, :, at] = new
                 gone = new - old
@@ -255,13 +287,8 @@
                 extra = new + gone
                 sums.append(extra)
                 weighted.append(weights * extra)
-            sums = row_sums(sums)
-            sum_ref[:, at] = sums
+            sum_ref[:, at] = row_sums(sums)
             weighted_ref[:, at] = row_sums(weighted)
-            last = sums[days - 1 :]
-            lead = w_ref[:1, at] - ETA * (sums[:1] - inflow_ref[:1, at])
-            chip_ref[:, at] = jnp.where(second, lead, last)
-            far_ref[:, at] = jnp.where(second, last, lead)
         return tuple(moved)
 
     moved = (jnp.zeros((8, LANES), F32),) * 2
@@ -391,7 +418,7 @@
 
 
 def second_primal(
-    x_hbm, x_head, moved_ref, weights_ref, grad_ref, bound_ref, fac_ref,
+    x_hbm, x_head, moved_ref, weights_ref, grad_ref, bound_ref, fac_ref, caps_ref,
     x2_hbm, sum_ref, last_hbm, omega_ref, out_hbm,
     x_ref, weighted_ref, last_ref, out_ref, sems, small_sems,
 ):
@@ -438,11 +465,13 @@
     row = pltpu.make_async_copy(last_ref, last_hbm, small_sems.at[0])
     row.start()
     blocks = out_ref.shape[0]
-    own = out_ref.shape[2] // days
+    own = caps_ref.shape[1] // blocks
+    out_ref[...] = jnp.zeros(out_ref.shape, F32)
     parts = facility_sums(weighted_ref, fac_ref, own * blocks)
     for k in range(blocks):
         g, place = divmod(k * own, WIDE)
-        out_ref[k] = flat(parts[g][:, place : place + own])
+        out_ref[k, :, :own] = parts[g][:, place : place + own]
+        out_ref[k, :, own : 2 * own] = caps_ref[:, k * own : (k + 1) * own]
     out = pltpu.make_async_copy(out_ref, out_hbm, small_sems.at[1])
     out.start()
     row.wait()
@@ -452,18 +481,17 @@
 
 
 def last_duals(
-    in_ref, caps_ref, room_ref, omega_ref, w_ref, sum_ref, prior_ref, inflow_ref, gamma_ref, w2_ref, caps2_ref
+    in_ref, room_ref, omega_ref, w_ref, sum_ref, prior_ref, inflow_ref, gamma_ref, w2_ref, caps2_ref
 ):
     days, classes = w_ref.shape
     sigma = ETA * omega_ref[...]
     own = room_ref.shape[1]
-    blocks = in_ref.shape[0]
-    mine = lax.axis_index("cls")
-    use, caps = in_ref[0], caps_ref[:, :own]
-    for k in range(1, blocks):
-        use = use + in_ref[k]
-        caps = jnp.where(mine == k, caps_ref[:, k * own : (k + 1) * own], caps)
-    caps2_ref[...] = jnp.minimum(caps - sigma[:1, :1] * (unflat(use, days) - room_ref[...]), 0.0)
+    use = in_ref[0, :, :own]
+    for k in range(1, in_ref.shape[0]):
+        use = use + in_ref[k, :, :own]
+    caps2_ref[...] = jnp.minimum(
+        in_ref[0, :, own : 2 * own] - sigma[:1, :1] * (use - room_ref[...]), 0.0
+    )
     rows = rows_iota((days, LANES))
     for k in range(classes // LANES):
         at = pl.ds(k * LANES, LANES)
@@ -501,7 +529,7 @@
     index = decay_index.reshape(1, classes)
 
     ends, row = call(
-        start, "start", [struct(blocks, 1, 2 * days * own), struct(1, classes)], [ANY] * 3,
+        start, "start", [struct(blocks, days, LANES), struct(1, classes)], [ANY] * 3,
         [pltpu.VMEM((days, own), F32), pltpu.VMEM((days, own), F32), pltpu.SemaphoreType.DMA((3,))],
     )(*in_hbm(ycap_start, capacity, ybal_start))
     after = to_previous(row)
@@ -511,26 +539,28 @@
     )
     table = struct(days, facilities)
     head = struct(days, opts, HEAD)
-    cost_head, x_head, kt, w, inflow, bound, fac, gamma, weights = call(
+    two = struct(2, opts, classes)
+    cost_head, x_head, cost_edge, x_edge, kt, w, inflow, bound, fac, gamma, weights = call(
         load, "load",
-        [head, head, rows, rows, rows, struct(opts, classes),
+        [head, head, two, two, rows, rows, rows, struct(opts, classes),
          jax.ShapeDtypeStruct((1, classes), jnp.int32), row, tile],
         [ANY] * 10,
         [pltpu.SMEM((opts,), F32), pltpu.SMEM(decay_table.shape, F32), pltpu.VMEM((1, classes), jnp.int32),
-         pltpu.VMEM((1, classes), jnp.int32), pltpu.SemaphoreType.DMA((10,))],
+         pltpu.VMEM((1, classes), jnp.int32), pltpu.SemaphoreType.DMA((14,))],
         cost=PASS,
     )(*in_hbm(usage, decay_table, ybal_start, inflow, upper, fac, count, index, cost, x_start))
     streams = classes // BLOCK
-    x1, sums, weighted, chip, far, moved, caps, room = call(
-        first_primal, "first_primal",
-        [pltpu.HBM(field.shape, F32), rows, rows, row, row, tile, table, table],
-        [ANY] * 2 + [VM] * 11,
-        [pltpu.VMEM(field.shape, F32), pltpu.VMEM(field.shape, F32), pltpu.SemaphoreType.DMA((3, streams))],
-        limit=8, out_specs=[ANY] + [VM] * 7,
-    )(*in_hbm(cost, x_start), cost_head, x_head, weights, ends, after, kt, w, inflow, bound, fac, gamma)
+    kt, pulled, chip, far, caps, room = call(
+        edge_primal, "edge_primal", [rows, rows, row, row, table, table], [VM] * 11
+    )(cost_edge, x_edge, weights, ends, after, kt, gamma, w, inflow, bound, fac)
     chip = swapped(chip, 0)
     far = swapped(far, 1)
-    use, dual = call(first_use, "first_use", [table, tile], [VM] * 5, cost=PASS)(
+    x1, sums, weighted, moved = call(
+        first_primal, "first_primal", [pltpu.HBM(field.shape, F32), rows, rows, tile], [ANY] * 2 + [VM] * 6,
+        [pltpu.VMEM(field.shape, F32), pltpu.VMEM(field.shape, F32), pltpu.SemaphoreType.DMA((3, streams))],
+        limit=8, out_specs=[ANY] + [VM] * 3, cost=LONG,
+    )(*in_hbm(cost, x_start), cost_head, x_head, weights, pulled, kt, bound)
+    use, dual = call(first_use, "first_use", [table, tile], [VM] * 5)(
         weighted, sums, inflow, gamma, fac
     )
     sent, prior = call(
@@ -551,17 +581,17 @@
     x2, sums2, last2, omega, sent = call(
         second_primal, "second_primal",
         [pltpu.HBM(field.shape, F32), rows, pltpu.HBM(row.shape, F32), tile,
-         pltpu.HBM((blocks, 1, days * own), F32)],
-        [ANY] + [VM] * 6,
+         pltpu.HBM((blocks, days, LANES), F32)],
+        [ANY] + [VM] * 7,
         [pltpu.VMEM(field.shape, F32), pltpu.VMEM(rows.shape, F32), pltpu.VMEM(row.shape, F32),
-         pltpu.VMEM((blocks, 1, days * own), F32), pltpu.SemaphoreType.DMA((2, streams)),
+         pltpu.VMEM((blocks, days, LANES), F32), pltpu.SemaphoreType.DMA((2, streams)),
          pltpu.SemaphoreType.DMA((2,))],
         limit=8, out_specs=[ANY, VM, ANY, VM, ANY],
-    )(*in_hbm(x1), x1_head, got, weights, grad, bound, fac)
+    )(*in_hbm(x1), x1_head, got, weights, grad, bound, fac, caps1)
     prior2 = to_next(last2)
     got = lax.all_to_all(sent, "cls", 0, 0)
-    w2, caps2 = call(last_duals, "last_duals", [struct(days, classes), struct(days, own)], [VM] * 9)(
-        got, caps1, capacity, omega, w1, sums2, prior2, inflow, gamma
+    w2, caps2 = call(last_duals, "last_duals", [struct(days, classes), struct(days, own)], [VM] * 8)(
+        got, capacity, omega, w1, sums2, prior2, inflow, gamma
     )
     return x2, w2, caps2
 

time: 75.7 us -> 71.3 us (0.942)
  blocking collectives: 19.5 us -> 11.1 us
  starting transfers between devices: 29.2 us -> 32.2 us
    all_to_all x2 -> x1, blocking collectives: 19.5 us -> 11.1 us  [local(): got = lax.all_to_all(sent, 'cls', 0, 0)]
    all_to_all x1, waiting for transfers between devices: 4.61 us -> 1.04 us  [local(): ends = lax.all_to_all(ends, 'cls', 0, 0)]
    all_to_all x0 -> x1, starting transfers between devices: none -> 3.34 us  [local(): got = lax.all_to_all(sent, 'cls', 0, 0)]
    all_to_all x0 -> x1, waiting for transfers between devices: none -> 2.98 us  [local(): got = lax.all_to_all(sent, 'cls', 0, 0)]
    all_to_all x1, starting transfers between devices: 6.46 us -> 9.03 us  [local(): ends = lax.all_to_all(ends, 'cls', 0, 0)]
    ppermute x1, starting transfers between devices: 5.15 us -> 2.85 us  [to_previous(): return lax.ppermute(row, 'day', [(i + 1, i) for i in range(n - 1)])]
    ppermute x1, waiting for transfers between devices: 0.01 us -> 1.32 us  [to_next(): return lax.ppermute(row, 'day', [(i, i + 1) for i in range(n - 1)])]
    all_to_all x1, starting transfers between devices: 10.6 us -> 9.3 us  [local(): got = lax.all_to_all(sent, 'day', 0, 0)]
  transfers between devices with their start and end apart: 6 -> 7, of which waited for: 3 -> 5; matrix products, arithmetic and copies ran while one was open for 0% -> 0% of each run, Pallas kernels for 6% -> 11%
where the time goes in v7:
time: 71.3 us; the launch traced here: 70.7 us
  starting transfers between devices  32.2 us (45%)
  Pallas kernels  15.4 us (22%)
  waiting for transfers between devices  11.3 us (16%)
  blocking collectives  11.1 us (16%)
  between operations  0.73 us (1%)
    all_to_all x1, blocking collectives, local(): got = lax.all_to_all(sent, 'cls', 0, 0)  11.1 us
    all_to_all x1, starting transfers between devices, local(): got = lax.all_to_all(sent, 'day', 0, 0)  9.3 us
    all_to_all x1, starting transfers between devices, local(): ends = lax.all_to_all(ends, 'cls', 0, 0)  9.03 us
    ppermute x2, starting transfers between devices, swapped(): return lax.ppermute(rows, 'day', pairs + [(j, i) for i, j in pairs])  5.21 us
    all_to_all x1, waiting for transfers between devices, local(): got = lax.all_to_all(sent, 'day', 0, 0)  5.04 us
    all_to_all x1, starting transfers between devices, local(): got = lax.all_to_all(sent, 'cls', 0, 0)  3.34 us
    pallas_call x1, Pallas kernels, local(): call(second_primal, 'second_primal', [pltpu.HBM(field.shape, F32), rows,...  3.33 us
    pallas_call x1, Pallas kernels, local(): call(first_primal, 'first_primal', [pltpu.HBM(field.shape, F32), rows, ro...  3.08 us
  transfers between devices with their start and end apart: 7, of which 5 were waited for; matrix products, arithmetic and copies ran while one was open for 0% of the time, Pallas kernels for 11%

profile of v7, /device:TPU:1, one launch (start us, length us, event | category | flops | bytes accessed | tf_op | source)
XLA Modules:
  0.0 70.7 jit_solution(10007440233063605255)
XLA Ops:
  0.6 1.4 %start.1 = (f32[8,8,128]{2,1,0:T(8,128)}, f32[1,8192]{1,0:T(1,128)S(1)}) custom-call(f32[8,32]{1,0:T(8,128)} %caps_ref.1, f32[8,32]{1,0:T(8,128)} %room_ref.3, f32[8,8192]{1,0:T(8,128)} %w_ref.1), custom_call_target="tpu_custom_call" | custom-call | tf_op jit(solution)/shard_map/start/pallas_call | solution.py:531
  2.1 9.0 %all-to-all-start = ((f32[8,8,128]{2,1,0:T(8,128)}), f32[8,8,128]{2,1,0:T(8,128)S(1)}, u32[]{:S(2)}, u32[]{:S(2)}) async-start(f32[8,8,128]{2,1,0:T(8,128)} %get-tuple-element.48), calls=%async_computation | async-start | bytes 65536 | tf_op jit(solution)/shard_map/all_to_all | solution.py:536
  11.1 2.9 %collective-permute-start = (f32[1,8192]{1,0:T(1,128)S(1)}, f32[1,8192]{1,0:T(1,128)S(1)}, u32[]{:S(2)}, u32[]{:S(2)}) collective-permute-start(f32[1,8192]{1,0:T(1,128)S(1)} %get-tuple-element.49), channel_id=1, source_target_pairs={{8,0},{16,8},{24,16},{32,24},{40,32},{48,40},{56,48},{64,56},{72,6... | collective-permute-start | bytes 98312 | tf_op jit(solution)/shard_map/ppermute | solution.py:510
  14.0 2.1 %load.1 = (f32[8,8,2048]{2,1,0:T(8,128)S(1)}, f32[8,8,2048]{2,1,0:T(8,128)S(1)}, f32[2,8,8192]{2,1,0:T(8,128)S(1)}, f32[2,8,8192]{2,1,0:T(8,128)S(1)}, f32[8,819...) custom-call(f32[8]{0:T(128)} %usage_hbm.1, ...), custom_call_target="tpu_custom_call" | custom-call | flops 10000000 | bytes 8000000 | tf_op jit(solution)/shard_map/load/pallas_call | solution.py:543
  16.0 0.9 %collective-permute-done.after_ref = f32[1,8192]{1,0:T(1,128)S(1)} collective-permute-done((f32[1,8192]{1,0:T(1,128)S(1)}, f32[1,8192]{1,0:T(1,128)S(1)}, u32[]{:S(2)}, u32[]{:S(2)}) %collective-permute-start) | collective-permute-done | bytes 32800 | tf_op jit(solution)/shard_map/ppermute | solution.py:510
  16.9 1.0 %all-to-all-done.ends_ref = f32[8,8,128]{2,1,0:T(8,128)S(1)} async-done(((f32[8,8,128]{2,1,0:T(8,128)}), f32[8,8,128]{2,1,0:T(8,128)S(1)}, u32[]{:S(2)}, u32[]{:S(2)}) %all-to-all-start) | async-done | bytes 32800 | tf_op jit(solution)/shard_map/all_to_all | solution.py:536
  18.0 1.1 %edge_primal.1 = (f32[8,8192]{1,0:T(8,128)S(1)}, f32[8,8192]{1,0:T(8,128)S(1)}, f32[1,8192]{1,0:T(1,128)S(1)}, f32[1,8192]{1,0:T(1,128)S(1)}, f32[8,256]{1,0:T(8,128)S(1)}, /*index=5*/f32[8,256]{1,0:T(8,128)S(1)}) custom-call(f32[2,8,8192]{2,1,0:T(8,128)S(1)} %get-tuple-element.46.cost_ref, f32[2,8,8192]{2,1,0:T(8,128)S(1)} %get-tuple-element.47.x_ref, ...), custom_call_target="tpu_custom_call" | custom-call | tf_op jit(solution)/shard_map/edge_primal/pallas_call | solution.py:553
  19.1 2.2 %collective-permute-start.1 = (f32[1,8192]{1,0:T(1,128)S(1)}, f32[1,8192]{1,0:T(1,128)S(1)}, u32[]{:S(2)}, u32[]{:S(2)}) collective-permute-start(f32[1,8192]{1,0:T(1,128)S(1)} %get-tuple-element.64), channel_id=1, source_target_pairs={{0,8},{16,24},{32,40},{48,56},{64,72},{80,88},{96,104},{112,120},{... | collective-permute-start | bytes 98312 | tf_op jit(solution)/shard_map/ppermute | solution.py:516
  21.3 3.0 %collective-permute-start.2 = (f32[1,8192]{1,0:T(1,128)S(1)}, f32[1,8192]{1,0:T(1,128)S(1)}, u32[]{:S(2)}, u32[]{:S(2)}) collective-permute-start(f32[1,8192]{1,0:T(1,128)S(1)} %get-tuple-element.65), channel_id=1, source_target_pairs={{8,16},{24,32},{40,48},{56,64},{72,80},{88,96},{104,112},{120,128}... | collective-permute-start | bytes 98312 | tf_op jit(solution)/shard_map/ppermute | solution.py:516
  24.3 3.1 %first_primal.1 = (f32[8,8,8192]{2,1,0:T(8,128)}, f32[8,8192]{1,0:T(8,128)S(1)}, f32[8,8192]{1,0:T(8,128)S(1)}, f32[8,128]{1,0:T(8,128)S(1)}) custom-call(f32[8,8,8192]{2,1,0:T(8,128)} %cost_hbm.5, f32[8,8,8192]{2,1,0:T(8,128)} %x_hbm.3, f32[8,8,2048]{2,1,0:T(8,128)S(1)} %get-tuple-element.43.cost_head, f32[8,8,2048]{2,1,0:T(8,128)S(1)} %get-tuple-element.44.x_head, ...), custom_call_target="tpu_custom_call" | custom-call | flops 10000000 | bytes 100000000 | tf_op jit(solution)/shard_map/first_primal/pallas_call | solution.py:558
  27.4 0.6 first_use.1
  28.0 0.0 collective-permute-done.1.chip_ref
  28.0 0.0 collective-permute-done.2.far_ref
  28.0 0.1 first_send.1
  28.1 11.1 %all_to_all.20.in_ref = f32[8,1,2304]{2,1,0:T(1,128)S(1)} all-to-all(f32[8,1,2304]{2,1,0:T(1,128)S(1)} %get-tuple-element.66), channel_id=1, replica_groups=mesh['day'=32,'cls'=8] {'cls'}, dimensions={0} | all-to-all | bytes 147456 | tf_op jit(solution)/shard_map/all_to_all | solution.py:569
  39.2 0.7 caps_step.1
  39.8 9.3 %all-to-all-start.2 = ((f32[32,1,256]{2,1,0:T(1,128)}), f32[32,1,256]{2,1,0:T(1,128)S(1)}, u32[]{:S(2)}, u32[]{:S(2)}) async-start(f32[32,1,256]{2,1,0:T(1,128)} %get-tuple-element.73), calls=%async_computation.2 | async-start | bytes 65536 | tf_op jit(solution)/shard_map/all_to_all | solution.py:576
  49.1 0.2 next_duals.1
  49.3 2.0 %next_grad.1 = (f32[8,8,8192]{2,1,0:T(8,128)S(1)}, f32[8,8,1024]{2,1,0:T(8,128)S(1)}) custom-call(f32[8,8,8192]{2,1,0:T(8,128)} %cost_hbm.5, f32[8,8,8192]{2,1,0:T(8,128)} %get-tuple-element.58.x_hbm, f32[8,128]{1,0:T(8,128)S(1)} %get-tuple-element.45.weights_ref, f32[8,256]{1,0:T(8,128)S(1)} %get-tuple-element.69.caps_ref, ...), custom_call_target="tpu_custom_call" | custom-call | flops 10000000 | bytes 8000000 | tf_op jit(solution)/shard_map/next_grad/pallas_call | solution.py:577
  51.3 5.0 %all-to-all-done.2.moved_ref = f32[32,1,256]{2,1,0:T(1,128)S(1)} async-done(((f32[32,1,256]{2,1,0:T(1,128)}), f32[32,1,256]{2,1,0:T(1,128)S(1)}, u32[]{:S(2)}, u32[]{:S(2)}) %all-to-all-start.2) | async-done | bytes 32800 | tf_op jit(solution)/shard_map/all_to_all | solution.py:576
  56.4 0.0 copy-start
  56.4 3.3 %second_primal.1 = (f32[8,8,8192]{2,1,0:T(8,128)}, f32[8,8192]{1,0:T(8,128)S(1)}, f32[1,8192]{1,0:T(1,128)}, f32[8,128]{1,0:T(8,128)S(1)}, f32[8,8,128]{2,1,0:T(8,128)}) custom-call(f32[8,8,8192]{2,1,0:T(8,128)} %get-tuple-element.58.x_hbm, f32[8,8,1024]{2,1,0:T(8,128)S(1)} %get-tuple-element.72.x_head, f32[32,1,256]{2,1,0:T(1,128)S(1)} %all-to-all-done.2.moved_ref, ...), custom_call_target="tpu_custom_call" | custom-call | tf_op jit(solution)/shard_map/second_primal/pallas_call | solution.py:581
  59.7 3.3 %all-to-all-start.3 = ((f32[8,8,128]{2,1,0:T(8,128)}), f32[8,8,128]{2,1,0:T(8,128)S(1)}, u32[]{:S(2)}, u32[]{:S(2)}) async-start(f32[8,8,128]{2,1,0:T(8,128)} %get-tuple-element.76), calls=%async_computation.3 | async-start | bytes 65536 | tf_op jit(solution)/shard_map/all_to_all | solution.py:592
  63.1 2.5 %collective-permute-start.3 = (f32[1,8192]{1,0:T(1,128)}, f32[1,8192]{1,0:T(1,128)S(1)}, u32[]{:S(2)}, u32[]{:S(2)}) collective-permute-start(f32[1,8192]{1,0:T(1,128)} %get-tuple-element.80), channel_id=1, source_target_pairs={{0,8},{8,16},{16,24},{24,32},{32,40},{40,48},{48,56},{56,64},{64,7... | collective-permute-start | bytes 98312 | tf_op jit(solution)/shard_map/ppermute | solution.py:505
  65.6 1.3 %collective-permute-done.3.prior_ref = f32[1,8192]{1,0:T(1,128)S(1)} collective-permute-done((f32[1,8192]{1,0:T(1,128)}, f32[1,8192]{1,0:T(1,128)S(1)}, u32[]{:S(2)}, u32[]{:S(2)}) %collective-permute-start.3) | collective-permute-done | bytes 32800 | tf_op jit(solution)/shard_map/ppermute | solution.py:505
  66.9 3.0 %all-to-all-done.3.in_ref = f32[8,8,128]{2,1,0:T(8,128)S(1)} async-done(((f32[8,8,128]{2,1,0:T(8,128)}), f32[8,8,128]{2,1,0:T(8,128)S(1)}, u32[]{:S(2)}, u32[]{:S(2)}) %all-to-all-start.3) | async-done | bytes 32800 | tf_op jit(solution)/shard_map/all_to_all | solution.py:592
  69.9 0.0 copy-done
  69.9 0.9 %last_duals.1 = (f32[8,8192]{1,0:T(8,128)}, f32[8,32]{1,0:T(8,128)}) custom-call(f32[8,8,128]{2,1,0:T(8,128)S(1)} %all-to-all-done.3.in_ref, f32[8,32]{1,0:T(8,128)S(1)} %copy-done, f32[8,128]{1,0:T(8,128)S(1)} %get-tuple-element.77.omega_ref, f32[8,8192]{1,0:T(8,128)S(1)} %get-tuple-element.78.w_ref, f32[8,8192]{1,0:T(8,128)S(1)} %get-tuple-element.79.sum_ref, ...), custom_call_target="tpu_custom_call" | custom-call | tf_op jit(solution)/shard_map/last_duals/pallas_call | solution.py:593
Async XLA Ops:
  2.1 15.9 %all-to-all-start = ((f32[8,8,128]{2,1,0:T(8,128)}), f32[8,8,128]{2,1,0:T(8,128)S(1)}, u32[]{:S(2)}, u32[]{:S(2)}) async-start(f32[8,8,128]{2,1,0:T(8,128)} %get-tuple-element.48), calls=%async_computation | async-start | bytes 65536 | tf_op jit(solution)/shard_map/all_to_all | solution.py:536
  11.1 5.8 %collective-permute-start = (f32[1,8192]{1,0:T(1,128)S(1)}, f32[1,8192]{1,0:T(1,128)S(1)}, u32[]{:S(2)}, u32[]{:S(2)}) collective-permute-start(f32[1,8192]{1,0:T(1,128)S(1)} %get-tuple-element.49), channel_id=1, source_target_pairs={{8,0},{16,8},{24,16},{32,24},{40,32},{48,40},{56,48},{64,56},{72,6... | collective-permute-start | bytes 98312 | tf_op jit(solution)/shard_map/ppermute | solution.py:510
  19.1 9.0 %collective-permute-start.1 = (f32[1,8192]{1,0:T(1,128)S(1)}, f32[1,8192]{1,0:T(1,128)S(1)}, u32[]{:S(2)}, u32[]{:S(2)}) collective-permute-start(f32[1,8192]{1,0:T(1,128)S(1)} %get-tuple-element.64), channel_id=1, source_target_pairs={{0,8},{16,24},{32,40},{48,56},{64,72},{80,88},{96,104},{112,120},{... | collective-permute-start | bytes 98312 | tf_op jit(solution)/shard_map/ppermute | solution.py:516
  21.3 6.8 %collective-permute-start.2 = (f32[1,8192]{1,0:T(1,128)S(1)}, f32[1,8192]{1,0:T(1,128)S(1)}, u32[]{:S(2)}, u32[]{:S(2)}) collective-permute-start(f32[1,8192]{1,0:T(1,128)S(1)} %get-tuple-element.65), channel_id=1, source_target_pairs={{8,16},{24,32},{40,48},{56,64},{72,80},{88,96},{104,112},{120,128}... | collective-permute-start | bytes 98312 | tf_op jit(solution)/shard_map/ppermute | solution.py:516
  39.8 16.6 %all-to-all-start.2 = ((f32[32,1,256]{2,1,0:T(1,128)}), f32[32,1,256]{2,1,0:T(1,128)S(1)}, u32[]{:S(2)}, u32[]{:S(2)}) async-start(f32[32,1,256]{2,1,0:T(1,128)} %get-tuple-element.73), calls=%async_computation.2 | async-start | bytes 65536 | tf_op jit(solution)/shard_map/all_to_all | solution.py:576
  56.4 13.5 %copy-start = (f32[8,32]{1,0:T(8,128)S(1)}, f32[8,32]{1,0:T(8,128)}, u32[]{:S(2)}) copy-start(f32[8,32]{1,0:T(8,128)} %room_ref.3) | copy-start | bytes 3076
  59.7 10.1 %all-to-all-start.3 = ((f32[8,8,128]{2,1,0:T(8,128)}), f32[8,8,128]{2,1,0:T(8,128)S(1)}, u32[]{:S(2)}, u32[]{:S(2)}) async-start(f32[8,8,128]{2,1,0:T(8,128)} %get-tuple-element.76), calls=%async_computation.3 | async-start | bytes 65536 | tf_op jit(solution)/shard_map/all_to_all | solution.py:592
  63.1 3.8 %collective-permute-start.3 = (f32[1,8192]{1,0:T(1,128)}, f32[1,8192]{1,0:T(1,128)S(1)}, u32[]{:S(2)}, u32[]{:S(2)}) collective-permute-start(f32[1,8192]{1,0:T(1,128)} %get-tuple-element.80), channel_id=1, source_target_pairs={{0,8},{8,16},{16,24},{24,32},{32,40},{40,48},{48,56},{56,64},{64,7... | collective-permute-start | bytes 98312 | tf_op jit(solution)/shard_map/ppermute | solution.py:505

commit v8 on v7

--- a/solution.py
+++ b/solution.py
@@ -260,9 +260,9 @@
 
 
 def first_primal(
-    cost_hbm, x_hbm, cost_head, x_head, weights_ref, pulled_ref, kt_ref, bound_ref,
-    x1_hbm, sum_ref, weighted_ref, moved_ref,
-    cost_ref, x_ref, sems,
+    cost_hbm, x_hbm, cost_head, x_head, weights_ref, pulled_ref, kt_ref, bound_ref, inflow_ref, gamma_ref, fac_ref,
+    x1_hbm, sum_ref, moved_ref, use_ref, dual_ref,
+    cost_ref, x_ref, weighted_ref, sems,
 ):
     days, classes = kt_ref.shape
     ready = HEAD // BLOCK
@@ -300,6 +300,7 @@
         moved = lax.fori_loop(k * each, (k + 1) * each, functools.partial(step, *source), moved)
         start_all(leave[k : k + 1])
     moved_ref[...] = moved[0] + moved[1]
+    interior_use(weighted_ref, sum_ref, inflow_ref, gamma_ref, fac_ref, use_ref, dual_ref)
     for block in leave:
         wait_all(block)
 
@@ -314,7 +315,7 @@
     return facility_groups(total, days)
 
 
-def first_use(weighted_ref, sum_ref, inflow_ref, gamma_ref, fac_ref, use_ref, dual_ref):
+def interior_use(weighted_ref, sum_ref, inflow_ref, gamma_ref, fac_ref, use_ref, dual_ref):
     days, classes = sum_ref.shape
     for g, part in enumerate(facility_sums(weighted_ref, fac_ref, use_ref.shape[1])):
         use_ref[:, g * WIDE : (g + 1) * WIDE] = part
@@ -555,14 +556,13 @@
     )(cost_edge, x_edge, weights, ends, after, kt, gamma, w, inflow, bound, fac)
     chip = swapped(chip, 0)
     far = swapped(far, 1)
-    x1, sums, weighted, moved = call(
-        first_primal, "first_primal", [pltpu.HBM(field.shape, F32), rows, rows, tile], [ANY] * 2 + [VM] * 6,
-        [pltpu.VMEM(field.shape, F32), pltpu.VMEM(field.shape, F32), pltpu.SemaphoreType.DMA((3, streams))],
-        limit=8, out_specs=[ANY] + [VM] * 3, cost=LONG,
-    )(*in_hbm(cost, x_start), cost_head, x_head, weights, pulled, kt, bound)
-    use, dual = call(first_use, "first_use", [table, tile], [VM] * 5)(
-        weighted, sums, inflow, gamma, fac
-    )
+    x1, sums, moved, use, dual = call(
+        first_primal, "first_primal", [pltpu.HBM(field.shape, F32), rows, tile, table, tile],
+        [ANY] * 2 + [VM] * 9,
+        [pltpu.VMEM(field.shape, F32), pltpu.VMEM(field.shape, F32), pltpu.VMEM(rows.shape, F32),
+         pltpu.SemaphoreType.DMA((3, streams))],
+        limit=8, out_specs=[ANY] + [VM] * 4, cost=LONG,
+    )(*in_hbm(cost, x_start), cost_head, x_head, weights, pulled, kt, bound, inflow, gamma, fac)
     sent, prior = call(
         first_send, "first_send", [struct(blocks, 1, days * facilities + 2 * LANES), row], [VM] * 8
     )(use, moved, dual, chip, far, sums, inflow, gamma)

time: 71.3 us -> 70.9 us (level)
    pallas_call x2 -> x1, Pallas kernels: 3.72 us -> 3.64 us  [local(): call(first_primal, 'first_primal', [pltpu.HBM(field.shape, F32), rows, ti...]
where the time goes in v8:
time: 70.9 us; the launch traced here: 70.4 us
  starting transfers between devices  32 us (45%)
  Pallas kernels  15.3 us (22%)
  waiting for transfers between devices  11.3 us (16%)
  blocking collectives  11.1 us (16%)
  between operations  0.74 us (1%)
    all_to_all x1, blocking collectives, local(): got = lax.all_to_all(sent, 'cls', 0, 0)  11.1 us
    all_to_all x1, starting transfers between devices, local(): got = lax.all_to_all(sent, 'day', 0, 0)  9.04 us
    all_to_all x1, starting transfers between devices, local(): ends = lax.all_to_all(ends, 'cls', 0, 0)  9.03 us
    ppermute x2, starting transfers between devices, swapped(): return lax.ppermute(rows, 'day', pairs + [(j, i) for i, j in pairs])  5.21 us
    all_to_all x1, waiting for transfers between devices, local(): got = lax.all_to_all(sent, 'day', 0, 0)  5.04 us
    pallas_call x1, Pallas kernels, local(): call(first_primal, 'first_primal', [pltpu.HBM(field.shape, F32), rows, ti...  3.64 us
    all_to_all x1, starting transfers between devices, local(): got = lax.all_to_all(sent, 'cls', 0, 0)  3.35 us
    pallas_call x1, Pallas kernels, local(): call(second_primal, 'second_primal', [pltpu.HBM(field.shape, F32), rows,...  3.34 us
  transfers between devices with their start and end apart: 7, of which 5 were waited for; matrix products, arithmetic and copies ran while one was open for 0% of the time, Pallas kernels for 11%

profile of v8, /device:TPU:1, one launch (start us, length us, event | category | flops | bytes accessed | tf_op | source)
XLA Modules:
  0.0 70.4 jit_solution(326000479603375379)
XLA Ops:
  0.6 1.4 %start.1 = (f32[8,8,128]{2,1,0:T(8,128)}, f32[1,8192]{1,0:T(1,128)S(1)}) custom-call(f32[8,32]{1,0:T(8,128)} %caps_ref.1, f32[8,32]{1,0:T(8,128)} %room_ref.3, f32[8,8192]{1,0:T(8,128)} %w_ref.1), custom_call_target="tpu_custom_call" | custom-call | tf_op jit(solution)/shard_map/start/pallas_call | solution.py:532
  2.1 9.0 %all-to-all-start = ((f32[8,8,128]{2,1,0:T(8,128)}), f32[8,8,128]{2,1,0:T(8,128)S(1)}, u32[]{:S(2)}, u32[]{:S(2)}) async-start(f32[8,8,128]{2,1,0:T(8,128)} %get-tuple-element.47), calls=%async_computation | async-start | bytes 65536 | tf_op jit(solution)/shard_map/all_to_all | solution.py:537
  11.1 2.9 %collective-permute-start = (f32[1,8192]{1,0:T(1,128)S(1)}, f32[1,8192]{1,0:T(1,128)S(1)}, u32[]{:S(2)}, u32[]{:S(2)}) collective-permute-start(f32[1,8192]{1,0:T(1,128)S(1)} %get-tuple-element.48), channel_id=1, source_target_pairs={{8,0},{16,8},{24,16},{32,24},{40,32},{48,40},{56,48},{64,56},{72,6... | collective-permute-start | bytes 98312 | tf_op jit(solution)/shard_map/ppermute | solution.py:511
  14.0 2.1 %load.1 = (f32[8,8,2048]{2,1,0:T(8,128)S(1)}, f32[8,8,2048]{2,1,0:T(8,128)S(1)}, f32[2,8,8192]{2,1,0:T(8,128)S(1)}, f32[2,8,8192]{2,1,0:T(8,128)S(1)}, f32[8,819...) custom-call(f32[8]{0:T(128)} %usage_hbm.1, ...), custom_call_target="tpu_custom_call" | custom-call | flops 10000000 | bytes 8000000 | tf_op jit(solution)/shard_map/load/pallas_call | solution.py:544
  16.0 0.9 %collective-permute-done.after_ref = f32[1,8192]{1,0:T(1,128)S(1)} collective-permute-done((f32[1,8192]{1,0:T(1,128)S(1)}, f32[1,8192]{1,0:T(1,128)S(1)}, u32[]{:S(2)}, u32[]{:S(2)}) %collective-permute-start) | collective-permute-done | bytes 32800 | tf_op jit(solution)/shard_map/ppermute | solution.py:511
  16.9 1.0 %all-to-all-done.ends_ref = f32[8,8,128]{2,1,0:T(8,128)S(1)} async-done(((f32[8,8,128]{2,1,0:T(8,128)}), f32[8,8,128]{2,1,0:T(8,128)S(1)}, u32[]{:S(2)}, u32[]{:S(2)}) %all-to-all-start) | async-done | bytes 32800 | tf_op jit(solution)/shard_map/all_to_all | solution.py:537
  18.0 1.1 %edge_primal.1 = (f32[8,8192]{1,0:T(8,128)S(1)}, f32[8,8192]{1,0:T(8,128)S(1)}, f32[1,8192]{1,0:T(1,128)S(1)}, f32[1,8192]{1,0:T(1,128)S(1)}, f32[8,256]{1,0:T(8,128)S(1)}, /*index=5*/f32[8,256]{1,0:T(8,128)S(1)}) custom-call(f32[2,8,8192]{2,1,0:T(8,128)S(1)} %get-tuple-element.45.cost_ref, f32[2,8,8192]{2,1,0:T(8,128)S(1)} %get-tuple-element.46.x_ref, ...), custom_call_target="tpu_custom_call" | custom-call | tf_op jit(solution)/shard_map/edge_primal/pallas_call | solution.py:554
  19.1 2.2 %collective-permute-start.1 = (f32[1,8192]{1,0:T(1,128)S(1)}, f32[1,8192]{1,0:T(1,128)S(1)}, u32[]{:S(2)}, u32[]{:S(2)}) collective-permute-start(f32[1,8192]{1,0:T(1,128)S(1)} %get-tuple-element.61), channel_id=1, source_target_pairs={{0,8},{16,24},{32,40},{48,56},{64,72},{80,88},{96,104},{112,120},{... | collective-permute-start | bytes 98312 | tf_op jit(solution)/shard_map/ppermute | solution.py:517
  21.3 3.0 %collective-permute-start.2 = (f32[1,8192]{1,0:T(1,128)S(1)}, f32[1,8192]{1,0:T(1,128)S(1)}, u32[]{:S(2)}, u32[]{:S(2)}) collective-permute-start(f32[1,8192]{1,0:T(1,128)S(1)} %get-tuple-element.62), channel_id=1, source_target_pairs={{8,16},{24,32},{40,48},{56,64},{72,80},{88,96},{104,112},{120,128}... | collective-permute-start | bytes 98312 | tf_op jit(solution)/shard_map/ppermute | solution.py:517
  24.3 3.6 %first_primal.1 = (f32[8,8,8192]{2,1,0:T(8,128)}, f32[8,8192]{1,0:T(8,128)S(1)}, f32[8,128]{1,0:T(8,128)S(1)}, f32[8,256]{1,0:T(8,128)S(1)}, f32[8,128]{1,0:T(8,128)S(1)}) custom-call(f32[8,8,8192]{2,1,0:T(8,128)} %cost_hbm.5, f32[8,8,8192]{2,1,0:T(8,128)} %x_hbm.3, f32[8,8,2048]{2,1,0:T(8,128)S(1)} %get-tuple-element.42.cost_head, ...), custom_call_target="tpu_custom_call" | custom-call | flops 10000000 | bytes 100000000 | tf_op jit(solution)/shard_map/first_primal/pallas_call | solution.py:559
  27.9 0.0 collective-permute-done.1.chip_ref
  27.9 0.0 collective-permute-done.2.far_ref
  28.0 0.1 first_send.1
  28.0 11.1 %all_to_all.20.in_ref = f32[8,1,2304]{2,1,0:T(1,128)S(1)} all-to-all(f32[8,1,2304]{2,1,0:T(1,128)S(1)} %get-tuple-element.64), channel_id=1, replica_groups=mesh['day'=32,'cls'=8] {'cls'}, dimensions={0} | all-to-all | bytes 147456 | tf_op jit(solution)/shard_map/all_to_all | solution.py:569
  39.1 0.7 caps_step.1
  39.8 9.0 %all-to-all-start.2 = ((f32[32,1,256]{2,1,0:T(1,128)}), f32[32,1,256]{2,1,0:T(1,128)S(1)}, u32[]{:S(2)}, u32[]{:S(2)}) async-start(f32[32,1,256]{2,1,0:T(1,128)} %get-tuple-element.71), calls=%async_computation.2 | async-start | bytes 65536 | tf_op jit(solution)/shard_map/all_to_all | solution.py:576
  48.8 0.2 next_duals.1
  49.0 2.0 %next_grad.1 = (f32[8,8,8192]{2,1,0:T(8,128)S(1)}, f32[8,8,1024]{2,1,0:T(8,128)S(1)}) custom-call(f32[8,8,8192]{2,1,0:T(8,128)} %cost_hbm.5, f32[8,8,8192]{2,1,0:T(8,128)} %get-tuple-element.57.x_hbm, f32[8,128]{1,0:T(8,128)S(1)} %get-tuple-element.44.weights_ref, f32[8,256]{1,0:T(8,128)S(1)} %get-tuple-element.67.caps_ref, ...), custom_call_target="tpu_custom_call" | custom-call | flops 10000000 | bytes 8000000 | tf_op jit(solution)/shard_map/next_grad/pallas_call | solution.py:577
  51.0 5.0 %all-to-all-done.2.moved_ref = f32[32,1,256]{2,1,0:T(1,128)S(1)} async-done(((f32[32,1,256]{2,1,0:T(1,128)}), f32[32,1,256]{2,1,0:T(1,128)S(1)}, u32[]{:S(2)}, u32[]{:S(2)}) %all-to-all-start.2) | async-done | bytes 32800 | tf_op jit(solution)/shard_map/all_to_all | solution.py:576
  56.1 0.0 copy-start
  56.1 3.3 %second_primal.1 = (f32[8,8,8192]{2,1,0:T(8,128)}, f32[8,8192]{1,0:T(8,128)S(1)}, f32[1,8192]{1,0:T(1,128)}, f32[8,128]{1,0:T(8,128)S(1)}, f32[8,8,128]{2,1,0:T(8,128)}) custom-call(f32[8,8,8192]{2,1,0:T(8,128)} %get-tuple-element.57.x_hbm, f32[8,8,1024]{2,1,0:T(8,128)S(1)} %get-tuple-element.70.x_head, f32[32,1,256]{2,1,0:T(1,128)S(1)} %all-to-all-done.2.moved_ref, ...), custom_call_target="tpu_custom_call" | custom-call | tf_op jit(solution)/shard_map/second_primal/pallas_call | solution.py:581
  59.4 3.3 %all-to-all-start.3 = ((f32[8,8,128]{2,1,0:T(8,128)}), f32[8,8,128]{2,1,0:T(8,128)S(1)}, u32[]{:S(2)}, u32[]{:S(2)}) async-start(f32[8,8,128]{2,1,0:T(8,128)} %get-tuple-element.74), calls=%async_computation.3 | async-start | bytes 65536 | tf_op jit(solution)/shard_map/all_to_all | solution.py:592
  62.8 2.5 %collective-permute-start.3 = (f32[1,8192]{1,0:T(1,128)}, f32[1,8192]{1,0:T(1,128)S(1)}, u32[]{:S(2)}, u32[]{:S(2)}) collective-permute-start(f32[1,8192]{1,0:T(1,128)} %get-tuple-element.78), channel_id=1, source_target_pairs={{0,8},{8,16},{16,24},{24,32},{32,40},{40,48},{48,56},{56,64},{64,7... | collective-permute-start | bytes 98312 | tf_op jit(solution)/shard_map/ppermute | solution.py:506
  65.3 1.3 %collective-permute-done.3.prior_ref = f32[1,8192]{1,0:T(1,128)S(1)} collective-permute-done((f32[1,8192]{1,0:T(1,128)}, f32[1,8192]{1,0:T(1,128)S(1)}, u32[]{:S(2)}, u32[]{:S(2)}) %collective-permute-start.3) | collective-permute-done | bytes 32800 | tf_op jit(solution)/shard_map/ppermute | solution.py:506
  66.6 3.0 %all-to-all-done.3.in_ref = f32[8,8,128]{2,1,0:T(8,128)S(1)} async-done(((f32[8,8,128]{2,1,0:T(8,128)}), f32[8,8,128]{2,1,0:T(8,128)S(1)}, u32[]{:S(2)}, u32[]{:S(2)}) %all-to-all-start.3) | async-done | bytes 32800 | tf_op jit(solution)/shard_map/all_to_all | solution.py:592
  69.6 0.0 copy-done
  69.6 0.9 %last_duals.1 = (f32[8,8192]{1,0:T(8,128)}, f32[8,32]{1,0:T(8,128)}) custom-call(f32[8,8,128]{2,1,0:T(8,128)S(1)} %all-to-all-done.3.in_ref, f32[8,32]{1,0:T(8,128)S(1)} %copy-done, f32[8,128]{1,0:T(8,128)S(1)} %get-tuple-element.75.omega_ref, f32[8,8192]{1,0:T(8,128)S(1)} %get-tuple-element.76.w_ref, f32[8,8192]{1,0:T(8,128)S(1)} %get-tuple-element.77.sum_ref, ...), custom_call_target="tpu_custom_call" | custom-call | tf_op jit(solution)/shard_map/last_duals/pallas_call | solution.py:593
Async XLA Ops:
  2.1 15.9 %all-to-all-start = ((f32[8,8,128]{2,1,0:T(8,128)}), f32[8,8,128]{2,1,0:T(8,128)S(1)}, u32[]{:S(2)}, u32[]{:S(2)}) async-start(f32[8,8,128]{2,1,0:T(8,128)} %get-tuple-element.47), calls=%async_computation | async-start | bytes 65536 | tf_op jit(solution)/shard_map/all_to_all | solution.py:537
  11.1 5.8 %collective-permute-start = (f32[1,8192]{1,0:T(1,128)S(1)}, f32[1,8192]{1,0:T(1,128)S(1)}, u32[]{:S(2)}, u32[]{:S(2)}) collective-permute-start(f32[1,8192]{1,0:T(1,128)S(1)} %get-tuple-element.48), channel_id=1, source_target_pairs={{8,0},{16,8},{24,16},{32,24},{40,32},{48,40},{56,48},{64,56},{72,6... | collective-permute-start | bytes 98312 | tf_op jit(solution)/shard_map/ppermute | solution.py:511
  19.1 8.9 %collective-permute-start.1 = (f32[1,8192]{1,0:T(1,128)S(1)}, f32[1,8192]{1,0:T(1,128)S(1)}, u32[]{:S(2)}, u32[]{:S(2)}) collective-permute-start(f32[1,8192]{1,0:T(1,128)S(1)} %get-tuple-element.61), channel_id=1, source_target_pairs={{0,8},{16,24},{32,40},{48,56},{64,72},{80,88},{96,104},{112,120},{... | collective-permute-start | bytes 98312 | tf_op jit(solution)/shard_map/ppermute | solution.py:517
  21.3 6.7 %collective-permute-start.2 = (f32[1,8192]{1,0:T(1,128)S(1)}, f32[1,8192]{1,0:T(1,128)S(1)}, u32[]{:S(2)}, u32[]{:S(2)}) collective-permute-start(f32[1,8192]{1,0:T(1,128)S(1)} %get-tuple-element.62), channel_id=1, source_target_pairs={{8,16},{24,32},{40,48},{56,64},{72,80},{88,96},{104,112},{120,128}... | collective-permute-start | bytes 98312 | tf_op jit(solution)/shard_map/ppermute | solution.py:517
  39.8 16.3 %all-to-all-start.2 = ((f32[32,1,256]{2,1,0:T(1,128)}), f32[32,1,256]{2,1,0:T(1,128)S(1)}, u32[]{:S(2)}, u32[]{:S(2)}) async-start(f32[32,1,256]{2,1,0:T(1,128)} %get-tuple-element.71), calls=%async_computation.2 | async-start | bytes 65536 | tf_op jit(solution)/shard_map/all_to_all | solution.py:576
  56.1 13.5 %copy-start = (f32[8,32]{1,0:T(8,128)S(1)}, f32[8,32]{1,0:T(8,128)}, u32[]{:S(2)}) copy-start(f32[8,32]{1,0:T(8,128)} %room_ref.3) | copy-start | bytes 3076
  59.4 10.1 %all-to-all-start.3 = ((f32[8,8,128]{2,1,0:T(8,128)}), f32[8,8,128]{2,1,0:T(8,128)S(1)}, u32[]{:S(2)}, u32[]{:S(2)}) async-start(f32[8,8,128]{2,1,0:T(8,128)} %get-tuple-element.74), calls=%async_computation.3 | async-start | bytes 65536 | tf_op jit(solution)/shard_map/all_to_all | solution.py:592
  62.8 3.8 %collective-permute-start.3 = (f32[1,8192]{1,0:T(1,128)}, f32[1,8192]{1,0:T(1,128)S(1)}, u32[]{:S(2)}, u32[]{:S(2)}) collective-permute-start(f32[1,8192]{1,0:T(1,128)} %get-tuple-element.78), channel_id=1, source_target_pairs={{0,8},{8,16},{16,24},{24,32},{32,40},{40,48},{48,56},{56,64},{64,7... | collective-permute-start | bytes 98312 | tf_op jit(solution)/shard_map/ppermute | solution.py:506
